TPU v7x, 32 devices: a whole 2x2x4 slice. The times are simulated.
32 devices in a mesh: dp: 8 (over z, y), tensor: 4 (over x, core).
Axes of the slice: x: 2, y: 2, z: 4, core: 2. Of those that a mesh axis runs over, the one named last changes fastest.
Arguments:
- kept_rows: bfloat16 [4096, 1152], P('dp', 'tensor'), may hold values from -6 to 6
- owner_index: int32 [4096], P('dp'), may hold values from 0 to 7, as said below
- kept_position: int32 [4096], P('dp'), may hold values from 0 to 1023, as said below
- resolution: int32 [8], P('dp'), may hold values from 0 to 1, as said below
- mask_token: bfloat16 [1152], replicated, may hold values from -6 to 6
- condition: bfloat16 [32, 1152], P('dp'), may hold values from -3 to 3, as said below
- modulate_weight: bfloat16 [1152, 6912], P('tensor'), may hold values from -0.1875 to 0.1875
- entry_weight: bfloat16 [1152, 3, 1152], P(None, None, 'tensor'), may hold values from -3 to 3, as said below
- output_weight: bfloat16 [1152, 1152], P('tensor'), may hold values from -0.75 to 0.75
- expand_weight: bfloat16 [1152, 4608], P(None, 'tensor'), may hold values from -0.1875 to 0.1875
- shrink_weight: bfloat16 [4608, 1152], P('tensor'), may hold values from -0.09375 to 0.09375
- cotangent: bfloat16 [8192, 1152], P('dp'), may hold values from -6 to 6
Outputs:
- layer_out: bfloat16 [8192, 1152], P('dp', 'tensor')
- kept_grad: bfloat16 [4096, 1152], P('dp', 'tensor')
- mask_grad: float32 [1152], P('dp')
- condition_grad: float32 [32, 1152], P('dp', 'tensor')
- modulate_grad: float32 [1152, 6912], P('tensor', 'dp')
- entry_grad: float32 [1152, 3, 1152], P('dp', None, 'tensor')
- output_grad: float32 [1152, 1152], P('tensor', 'dp')
- expand_grad: float32 [1152, 4608], P('dp', 'tensor')
- shrink_grad: float32 [4608, 1152], P('tensor', 'dp')
Inputs may be any that keep to these rules, and one draw needn't show every extreme that they name: `owner_index`: every owner receives exactly 512 kept rows in all. The kept rows of one index of dp going to one owner number at most 128, and in every draw some pair of a sender and an owner has exactly 128. `kept_position`: the kept rows of one owner have distinct positions, exactly half of the positions of each of its images. `resolution`: one entry a region of an owner, regions in order: 1 means the region is one image of 1024 tokens that uses the first of the region's four condition rows; 0 means four images of a quarter of 1024 tokens each, one after another, using the region's four condition rows in order. `condition`: independent entries of mean zero. `entry_weight`: independent entries of mean zero.
All inputs are finite; a program needn't handle non-finite values.
Results may differ from a plain program's by a relative error of at most 0.017.
Values may be sent and summed in bfloat16 or wider, within the bound.
No kernel may reach another device: no remote copies, remote signals or barrier semaphores. Data moves between devices by JAX's collectives and lax.ppermute only.
A program may use at most 256 MiB of HBM per device.

v0:
```python
from functools import partial

import jax
import jax.numpy as jnp
from jax import lax
from jax.sharding import PartitionSpec as P

HEAD = 72


epsilon = 1e-06
gelu_coeff = 0.7978845608028654


def normalize(rows):
    centered = rows - jnp.mean(rows, axis=-1, keepdims=True)
    inverse = lax.rsqrt(jnp.mean(centered * centered, axis=-1, keepdims=True) + epsilon)
    return (centered * inverse, inverse)


def normalize_back(unit, inverse, grad):
    return inverse * (
        grad
        - jnp.mean(grad, axis=-1, keepdims=True)
        - unit * jnp.mean(grad * unit, axis=-1, keepdims=True)
    )


def gelu_tanh(value):
    inner = gelu_coeff * (value + 0.044715 * value * value * value)
    return 0.5 * value * (1.0 + jnp.tanh(inner))


def gelu_slope(value):
    curve = jnp.tanh(gelu_coeff * (value + 0.044715 * value * value * value))
    return 0.5 * (1.0 + curve) + 0.5 * value * (1.0 - curve * curve) * gelu_coeff * (
        1.0 + 3.0 * 0.044715 * value * value
    )


def attend(queries, keys_all, values_all, groups):
    rows, width_part = queries.shape
    heads_part = width_part // HEAD
    shape = (groups, rows // groups, heads_part, HEAD)
    scores = jnp.einsum(
        "gqhe,gkhe->ghqk",
        queries.reshape(shape),
        keys_all.reshape(shape),
        preferred_element_type=jnp.float32,
    ) * HEAD ** (-0.5)
    top = jnp.max(scores, axis=-1, keepdims=True)
    spread = jnp.exp(scores - top)
    total = jnp.sum(spread, axis=-1, keepdims=True)
    probs = (spread / total).astype(jnp.bfloat16)
    attended = jnp.einsum(
        "ghqk,gkhe->gqhe", probs, values_all.reshape(shape), preferred_element_type=jnp.float32
    )
    summary = (top + jnp.log(total))[..., 0]
    return (
        attended.reshape(rows, width_part),
        jnp.transpose(summary, (0, 2, 1)).reshape(rows, heads_part),
    )


def attend_back(queries, keys_all, values_all, summary, attended_grad, groups):
    rows, width_part = queries.shape
    heads_part = width_part // HEAD
    length = rows // groups
    shape = (groups, length, heads_part, HEAD)
    query_view = queries.reshape(shape)
    key_view = keys_all.reshape(shape)
    grad_view = attended_grad.reshape(shape)
    scale = HEAD ** (-0.5)
    scores = (
        jnp.einsum("gqhe,gkhe->ghqk", query_view, key_view, preferred_element_type=jnp.float32)
        * scale
    )
    lse = jnp.transpose(summary.reshape(groups, length, heads_part), (0, 2, 1))[..., None]
    probs = jnp.exp(scores - lse)
    value_grad = jnp.einsum(
        "ghqk,gqhe->gkhe", probs.astype(jnp.bfloat16), grad_view, preferred_element_type=jnp.float32
    )
    prob_grad = jnp.einsum(
        "gqhe,gkhe->ghqk", grad_view, values_all.reshape(shape), preferred_element_type=jnp.float32
    )
    score_grad = (probs * (prob_grad - jnp.sum(probs * prob_grad, axis=-1, keepdims=True))).astype(
        jnp.bfloat16
    )
    query_grad = (
        jnp.einsum("ghqk,gkhe->gqhe", score_grad, key_view, preferred_element_type=jnp.float32)
        * scale
    )
    key_grad = (
        jnp.einsum("ghqk,gqhe->gkhe", score_grad, query_view, preferred_element_type=jnp.float32)
        * scale
    )
    return jnp.concatenate(
        [
            query_grad.reshape(rows, width_part),
            key_grad.reshape(rows, width_part),
            value_grad.reshape(rows, width_part),
        ],
        axis=1,
    )


def body(
    kept_rows,
    owner_index,
    kept_position,
    resolution,
    mask_token,
    condition,
    modulate_weight,
    entry_weight,
    output_weight,
    expand_weight,
    shrink_weight,
    cotangent,
):
    owners = lax.axis_size("dp")
    kept_count, width_part = kept_rows.shape
    width = mask_token.shape[0]
    blocks = resolution.shape[0]
    own_tokens = cotangent.shape[0]
    region = own_tokens // blocks
    quarter = region // 4
    capacity = 2 * kept_count // owners
    slots_all = owners * capacity
    column_start = lax.axis_index("tensor") * width_part

    def columns(field):
        return lax.dynamic_slice_in_dim(field, column_start, width_part, 1)

    owner_hot = (owner_index[:, None] == jnp.arange(owners, dtype=jnp.int32)[None, :]).astype(
        jnp.bfloat16
    )
    earlier = (jnp.arange(kept_count)[:, None] > jnp.arange(kept_count)[None, :]).astype(
        jnp.bfloat16
    )
    before = jnp.dot(earlier, owner_hot, preferred_element_type=jnp.float32)
    ranking = jnp.sum(before * owner_hot, axis=1).astype(jnp.int32)
    slot_index = owner_index * capacity + ranking
    packing = jnp.arange(slots_all, dtype=jnp.int32)[:, None] == slot_index[None, :]
    pack_matrix = packing.astype(jnp.bfloat16)
    slot_place = jnp.sum(jnp.where(packing, kept_position[None, :] + 1, 0), axis=1) - 1
    arrived_place = lax.all_to_all(
        slot_place.reshape(owners, capacity), "dp", split_axis=0, concat_axis=0, tiled=True
    ).reshape(slots_all)
    unpacking = jnp.arange(own_tokens, dtype=jnp.int32)[:, None] == arrived_place[None, :]
    unpack_matrix = unpacking.astype(jnp.bfloat16)
    filled = jnp.any(unpacking, axis=1)
    token_row = mask_token.astype(jnp.float32)[None, :]
    packed = jnp.dot(
        pack_matrix,
        lax.all_gather(kept_rows, "tensor", axis=1, tiled=True),
        preferred_element_type=jnp.float32,
    ).astype(jnp.bfloat16)
    arrived = lax.all_to_all(
        packed.reshape(owners, capacity, width), "dp", split_axis=0, concat_axis=0, tiled=True
    )
    placed = jnp.dot(
        unpack_matrix, arrived.reshape(slots_all, width), preferred_element_type=jnp.float32
    )
    spatial = jnp.where(filled[:, None], placed, token_row)
    context_part = columns(condition.astype(jnp.float32))
    lifted = jax.nn.silu(context_part).astype(jnp.bfloat16)
    table = lax.psum(jnp.dot(lifted, modulate_weight, preferred_element_type=jnp.float32), "tensor")
    big = resolution == 1
    grouped = table.reshape(blocks, 4, 6 * width)
    chosen = jnp.where(big[:, None, None], grouped[:, 0:1], grouped)

    def per_token(index):
        piece = chosen[:, :, index * width : (index + 1) * width]
        return jnp.broadcast_to(piece[:, :, None, :], (blocks, 4, quarter, width)).reshape(
            own_tokens, width
        )

    shift_one, scale_one, gate_one, shift_two, scale_two, gate_two = [
        per_token(index) for index in range(6)
    ]

    def table_rows(field):
        sums = field.reshape(blocks, 4, quarter, field.shape[1]).sum(axis=2)
        first = jnp.where(big[:, None], sums.sum(axis=1), sums[:, 0])
        rest = jnp.where(big[:, None, None], 0.0, sums[:, 1:])
        return jnp.concatenate([first[:, None], rest], axis=1).reshape(4 * blocks, field.shape[1])

    unit_one, inverse_one = normalize(spatial)
    normed_one = (unit_one * (1.0 + scale_one) + shift_one).astype(jnp.bfloat16)
    entry_flat = entry_weight.reshape(width, 3 * width_part)
    projected = jnp.dot(normed_one, entry_flat, preferred_element_type=jnp.float32).astype(
        jnp.bfloat16
    )
    queries = projected[:, :width_part]
    keys_all = projected[:, width_part : 2 * width_part]
    values_all = projected[:, 2 * width_part :]
    number = 0
    attended_block, summary = lax.cond(
        big[number],
        partial(attend, groups=1),
        partial(attend, groups=4),
        queries,
        keys_all,
        values_all,
    )
    summaries = [summary]
    attended = attended_block.astype(jnp.bfloat16)
    branch = lax.psum(
        jnp.dot(attended, output_weight, preferred_element_type=jnp.float32).astype(jnp.bfloat16),
        "tensor",
    ).astype(jnp.float32)
    middle = spatial + gate_one * branch
    unit_two, inverse_two = normalize(middle)
    normed_two = (unit_two * (1.0 + scale_two) + shift_two).astype(jnp.bfloat16)
    hidden = jnp.dot(normed_two, expand_weight, preferred_element_type=jnp.float32)
    activated = gelu_tanh(hidden).astype(jnp.bfloat16)
    feed_part = lax.psum_scatter(
        jnp.dot(activated, shrink_weight, preferred_element_type=jnp.float32).astype(jnp.bfloat16),
        "tensor",
        scatter_dimension=1,
        tiled=True,
    ).astype(jnp.float32)
    layer_out = (columns(middle) + columns(gate_two) * feed_part).astype(jnp.bfloat16)
    upstream = cotangent.astype(jnp.float32)
    feed_grad = (gate_two * upstream).astype(jnp.bfloat16)
    shrink_grad = jnp.dot(activated.T, feed_grad, preferred_element_type=jnp.float32)
    hidden_grad = (
        jnp.dot(feed_grad, shrink_weight.T, preferred_element_type=jnp.float32) * gelu_slope(hidden)
    ).astype(jnp.bfloat16)
    expand_grad = jnp.dot(normed_two.T, hidden_grad, preferred_element_type=jnp.float32)
    gate_two_rows = lax.dynamic_update_slice_in_dim(
        jnp.zeros((4 * blocks, width), jnp.float32),
        table_rows(columns(upstream) * feed_part),
        column_start,
        1,
    )
    normed_two_grad, gate_two_table = (
        lax.psum(
            jnp.dot(hidden_grad, expand_weight.T, preferred_element_type=jnp.float32).astype(
                jnp.bfloat16
            ),
            "tensor",
        ).astype(jnp.float32),
        lax.psum(gate_two_rows.astype(jnp.bfloat16), "tensor").astype(jnp.float32),
    )
    middle_grad = upstream + normalize_back(
        unit_two, inverse_two, normed_two_grad * (1.0 + scale_two)
    )
    branch_grad = (gate_one * middle_grad).astype(jnp.bfloat16)
    output_grad = jnp.dot(attended.T, branch_grad, preferred_element_type=jnp.float32)
    attended_grad = jnp.dot(
        branch_grad, output_weight.T, preferred_element_type=jnp.float32
    ).astype(jnp.bfloat16)
    number = 0
    pieces = lax.cond(
        big[number],
        partial(attend_back, groups=1),
        partial(attend_back, groups=4),
        queries,
        keys_all,
        values_all,
        summaries[number],
        attended_grad,
    )
    projected_grad = pieces.astype(jnp.bfloat16)
    entry_grad = jnp.dot(normed_one.T, projected_grad, preferred_element_type=jnp.float32).reshape(
        width, 3, width_part
    )
    normed_one_grad = lax.psum(
        jnp.dot(projected_grad, entry_flat.T, preferred_element_type=jnp.float32).astype(
            jnp.bfloat16
        ),
        "tensor",
    ).astype(jnp.float32)
    spatial_grad = middle_grad + normalize_back(
        unit_one, inverse_one, normed_one_grad * (1.0 + scale_one)
    )
    table_grad = jnp.concatenate(
        [
            table_rows(normed_one_grad),
            table_rows(normed_one_grad * unit_one),
            table_rows(middle_grad * branch),
            table_rows(normed_two_grad),
            table_rows(normed_two_grad * unit_two),
            gate_two_table,
        ],
        axis=1,
    ).astype(jnp.bfloat16)
    modulate_grad = jnp.dot(lifted.T, table_grad, preferred_element_type=jnp.float32)
    logistic = jax.nn.sigmoid(context_part)
    condition_grad = (
        jnp.dot(table_grad, modulate_weight.T, preferred_element_type=jnp.float32)
        * logistic
        * (1.0 + context_part * (1.0 - logistic))
    )
    token_grad = jnp.sum(jnp.where(filled[:, None], 0.0, spatial_grad), axis=0)
    back_part = columns(spatial_grad).astype(jnp.bfloat16)
    slots_back = jnp.dot(unpack_matrix.T, back_part, preferred_element_type=jnp.float32).astype(
        jnp.bfloat16
    )
    returned = lax.all_to_all(
        slots_back.reshape(owners, capacity, width_part),
        "dp",
        split_axis=0,
        concat_axis=0,
        tiled=True,
    )
    kept_grad = jnp.dot(
        pack_matrix.T, returned.reshape(slots_all, width_part), preferred_element_type=jnp.float32
    ).astype(jnp.bfloat16)
    entry_sum, expand_sum, token_sum = (
        lax.psum_scatter(entry_grad, "dp", scatter_dimension=0, tiled=True),
        lax.psum_scatter(expand_grad, "dp", scatter_dimension=0, tiled=True),
        lax.psum_scatter(token_grad, "dp", scatter_dimension=0, tiled=True),
    )
    output_sum, shrink_sum, modulate_sum = (
        lax.psum_scatter(output_grad, "dp", scatter_dimension=1, tiled=True),
        lax.psum_scatter(shrink_grad, "dp", scatter_dimension=1, tiled=True),
        lax.psum_scatter(modulate_grad, "dp", scatter_dimension=1, tiled=True),
    )
    return (
        layer_out,
        kept_grad,
        token_sum,
        condition_grad,
        modulate_sum,
        entry_sum,
        output_sum,
        expand_sum,
        shrink_sum,
    )


def solution(mesh):
    return jax.shard_map(
        body,
        mesh=mesh,
        in_specs=(
            P("dp", "tensor"),
            P("dp"),
            P("dp"),
            P("dp"),
            P(),
            P("dp", None),
            P("tensor", None),
            P(None, None, "tensor"),
            P("tensor", None),
            P(None, "tensor"),
            P("tensor", None),
            P("dp", None),
        ),
        out_specs=(
            P("dp", "tensor"),
            P("dp", "tensor"),
            P("dp"),
            P("dp", "tensor"),
            P("tensor", "dp"),
            P("dp", None, "tensor"),
            P("tensor", "dp"),
            P("dp", "tensor"),
            P("tensor", "dp"),
        ),
        check_vma=False,
    )
```

profile of v0, /device:TPU:0, one launch (start us, length us, event | category | flops | bytes accessed | tf_op | source)
XLA Modules:
  0.0 1045.5 jit_solution(13782044897362118838)
XLA Ops:
  11.2 7.3 all-to-all-start
  18.5 11.3 %all-gather.2.cloned.1.call-done = bf16[512,1152]{0,1:T(8,128)(2,1)} async-done(((bf16[512,288]{0,1:T(8,128)(2,1)}), bf16[512,1152]{0,1:T(8,128)(2,1)}) %all-gather.2.cloned.1.call-update) | async-done | bytes 1179664 | tf_op jit(solution)/shard_map/all_gather | solution.py:156
  29.8 4.3 convolution_convert_fusion
  34.1 5.5 all-to-all-start.1
  39.6 3.5 fusion.95
  44.5 29.2 %all-reduce.6.cloned.1.call-done = f32[4,6912]{1,0:T(4,128)} async-done(((f32[4,6912]{1,0:T(4,128)}), f32[4,6912]{1,0:T(4,128)}) %all-reduce.6.cloned.1.call-update) | async-done | bytes 110608 | tf_op jit(solution)/shard_map/psum | solution.py:168
  75.7 18.3 %all-to-all-done.1 = bf16[8,128,1152]{2,1,0:T(8,128)(2,1)} async-done(((bf16[8,128,1152]{2,1,0:T(8,128)(2,1)}), bf16[8,128,1152]{2,1,0:T(8,128)(2,1)}, u32[]{:S(2)}, u32[]{:S(2)}) %all-to-all-start.1) | async-done | bytes 2359328 | tf_op jit(solution)/shard_map/all_to_all | solution.py:159
  93.9 4.8 fusion.102
  102.1 2.5 convolution_convert_fusion.5
  105.7 11.1 %conditional.6 = (f32[1024,4]{0,1:T(4,128)S(1)}, bf16[1024,288]{0,1:T(8,128)(2,1)S(1)}) conditional(s32[]{:T(128)} %convert_element_type.142, (bf16[1024,288]{0,1:T(8,128)(2,1)}, bf16[1024,288]{0,1:T(8,128)(2,1)S(1)}, bf16[1024,288]{0,1:T(8,128)(2,1)}) %tuple.42, (bf16[1024,288]{0,1:T(8,128)(2,1)}, bf16[1024,288]{0,1:T(8,128)(2,1)S(1)}, ...), branch_computations={%region_6.9_spmd, %region_9.12_spmd} | conditional | flops 1245999104 | bytes 55181356
  106.2 2.4 reshape.383
  108.6 1.2 reshape.384
  109.8 2.4 reshape.386
  112.3 2.1 multiply_reduce_fusion
  117.6 4.0 convolution_convert_fusion.2
  121.7 3.6 multiply_convert_fusion.2
  125.3 65.2 %all-reduce.8.cloned.1.call-done = bf16[1024,1152]{1,0:T(8,128)(2,1)} async-done(((bf16[1024,1152]{1,0:T(8,128)(2,1)}), bf16[1024,1152]{1,0:T(8,128)(2,1)}) %all-reduce.8.cloned.1.call-update) | async-done | bytes 2359312 | tf_op jit(solution)/shard_map/psum | solution.py:209
  190.5 3.8 fusion.99
  196.4 3.5 fusion.104
  200.0 5.0 fusion.52
  205.1 1.4 copy-done.41
  206.5 4.8 convolution_convert_fusion.3
  211.6 55.6 %all-reduce.10.cloned.1.call-done = bf16[1024,1152]{1,0:T(8,128)(2,1)} async-done(((bf16[1024,1152]{1,0:T(8,128)(2,1)}), bf16[1024,1152]{1,0:T(8,128)(2,1)}) %all-reduce.10.cloned.1.call-update) | async-done | bytes 2359312 | tf_op jit(solution)/shard_map/psum | solution.py:239
  267.2 4.5 fusion.54
  272.4 5.5 fusion.98
  279.4 1.8 convolution_convert_fusion.6
  281.2 22.9 %conditional.7 = (bf16[1024,864]{0,1:T(8,128)(2,1)}) conditional(s32[]{:T(128)} %convert_element_type.142, (bf16[1024,288]{0,1:T(8,128)(2,1)}, bf16[1024,288]{0,1:T(8,128)(2,1)S(1)}, f32[1024,4]{0,1:T(4,128)S(1)}, bf16[1024,288]{0,1:T(8,128)(2,1)}, bf16[1024,288]{0,1:T(8,128)(2,1)}) %tuple.43, (bf16[1024,288]{0,1:T(8,128)(2,1)}, ...), branch_computations={%region_19.21_spmd, %region_21.23_spmd} | conditional | flops 3076714496 | bytes 140066880
  281.2 2.4 reshape.393
  283.6 1.2 reshape.394
  284.8 1.7 reshape.396
  286.6 2.4 reshape.397
  289.0 2.0 fusion.28
  297.2 1.4 pad_maximum_fusion
  304.0 6.4 convolution_convert_fusion.1
  310.5 8.1 fusion.53
  318.9 4.1 convert_element_type.153
  323.0 3.1 bitcast_reduce_fusion
  326.1 2.6 bitcast_reduce_fusion.2
  328.7 62.4 %all-reduce.12.cloned.1.call-done = bf16[1024,1152]{1,0:T(8,128)(2,1)} async-done(((bf16[1024,1152]{1,0:T(8,128)(2,1)}), bf16[1024,1152]{1,0:T(8,128)(2,1)}) %all-reduce.12.cloned.1.call-update) | async-done | bytes 2359312 | tf_op jit(solution)/shard_map/psum | solution.py:270
  391.1 4.5 fusion.55
  395.7 3.0 bitcast_reduce_fusion.3
  398.9 28.0 %reduce-scatter.19.cloned.1.call-done = bf16[288,1024]{1,0:T(8,128)(2,1)} async-done(((bf16[1152,1024]{1,0:T(8,128)(2,1)}), bf16[288,1024]{1,0:T(8,128)(2,1)}) %reduce-scatter.19.cloned.1.call-update) | async-done | bytes 589840
  426.9 1.4 copy.157
  428.3 2.1 bitcast_reduce_fusion.5
  430.7 4.4 fusion.68
  435.3 6.1 psum.39
  441.4 5.6 convolution_bitcast_fusion
  448.1 4.3 fusion.105
  452.5 6.6 fusion.107
  459.1 5.9 copy.146
  465.3 7.9 fusion.106
  473.3 8.9 fusion.97
  482.8 4.9 select_reduce_fusion
  487.8 1.3 fusion.62
  490.1 5.8 all-to-all-start.2
  497.1 34.9 %all-reduce = f32[1152]{0:T(1024)S(1)} all-reduce(f32[1152]{0:T(1024)S(1)} %get-tuple-element.147), channel_id=3, replica_groups=mesh['dp'=8,'tensor'=4] {'dp'}, use_global_device_ids=true, to_apply=%region_27.28.clone | all-reduce | flops 1152 | bytes 9216
  532.7 2.5 fusion.63
  536.3 4.0 fusion.65
  540.2 104.5 %reduce-scatter.21.cloned.1.call-done = f32[864,288]{1,0:T(8,128)} async-done(((f32[6912,288]{1,0:T(8,128)}), f32[864,288]{1,0:T(8,128)}) %reduce-scatter.21.cloned.1.call-update) | async-done | bytes 995344
  644.7 2.7 copy.159
  647.4 67.4 %reduce-scatter.13.cloned.1.call-done = f32[288,144]{0,1:T(8,128)} async-done(((f32[288,1152]{0,1:T(8,128)}), f32[288,144]{0,1:T(8,128)}) %reduce-scatter.13.cloned.1.call-update) | async-done | bytes 165904 | tf_op jit(solution)/shard_map/reduce_scatter | solution.py:318
  714.8 107.3 %reduce-scatter.11.cloned.1.call-done = f32[144,3,288]{2,0,1:T(8,128)} async-done(((f32[1152,3,288]{2,0,1:T(8,128)}), f32[144,3,288]{2,0,1:T(8,128)}) %reduce-scatter.11.cloned.1.call-update) | async-done | bytes 497680 | tf_op jit(solution)/shard_map/reduce_scatter | solution.py:313
  822.1 108.4 %reduce-scatter.15.cloned.1.call-done = f32[144,1152]{1,0:T(8,128)} async-done(((f32[1152,1152]{1,0:T(8,128)}), f32[144,1152]{1,0:T(8,128)}) %reduce-scatter.15.cloned.1.call-update) | async-done | bytes 663568 | tf_op jit(solution)/shard_map/reduce_scatter | solution.py:314
  930.5 108.0 %reduce-scatter.17.cloned.1.call-done = f32[1152,144]{0,1:T(8,128)} async-done(((f32[1152,1152]{0,1:T(8,128)}), f32[1152,144]{0,1:T(8,128)}) %reduce-scatter.17.cloned.1.call-update) | async-done | bytes 663568 | tf_op jit(solution)/shard_map/reduce_scatter | solution.py:319
  (163 shorter events, 31.2 us)
Async XLA Ops:
  7.2 189.3 %copy-start = (bf16[1152,1152]{1,0:T(8,128)(2,1)S(1)}, bf16[1152,1152]{1,0:T(8,128)(2,1)}, u32[]{:S(2)}) copy-start(bf16[1152,1152]{1,0:T(8,128)(2,1)} %param.25) | copy-start | bytes 7962628
  7.2 22.6 %all-gather.2.cloned.1.call-start = ((), (), s32[]{:S(2)}) async-start(), calls=%async_computation.9 | async-start | bytes 1474560 | tf_op jit(solution)/shard_map/all_gather | solution.py:156
  10.3 23.7 %copy-start.29 = (s32[512]{0:T(512)}, s32[512]{0:T(512)S(1)}, u32[]{:S(2)}) copy-start(s32[512]{0:T(512)S(1)} %convert_add_fusion) | copy-start | bytes 6148
  11.2 22.8 %all-to-all-start = ((s32[8,1,128]{2,1,0:T(1,128)}), s32[8,1,128]{2,1,0:T(1,128)S(1)}, u32[]{:S(2)}, u32[]{:S(2)}) async-start(s32[8,1,128]{2,1,0:T(1,128)} %bitcast.37), calls=%async_computation | async-start | bytes 8192 | tf_op jit(solution)/shard_map/all_to_all | solution.py:147
  34.0 9.9 copy-start.31
  34.1 59.9 %copy-start.32 = (s32[8,1,128]{2,1,0:T(1,128)}, s32[8,1,128]{2,1,0:T(1,128)S(1)}, u32[]{:S(2)}) copy-start(s32[8,1,128]{2,1,0:T(1,128)S(1)} %all-to-all-done) | copy-start | bytes 12292
  34.1 59.9 %all-to-all-start.1 = ((bf16[8,128,1152]{2,1,0:T(8,128)(2,1)}), bf16[8,128,1152]{2,1,0:T(8,128)(2,1)}, u32[]{:S(2)}, u32[]{:S(2)}) async-start(bf16[8,128,1152]{2,1,0:T(8,128)(2,1)} %bitcast.278), calls=%async_computation.1 | async-start | bytes 4718592 | tf_op jit(solution)/shard_map/all_to_all | solution.py:159
  39.6 34.1 %all-reduce.6.cloned.1.call-start = ((), (), s32[]{:S(2)}) async-start(), calls=%async_computation.10 | async-start | bytes 221184 | tf_op jit(solution)/shard_map/psum | solution.py:168
  43.2 147.3 %all-reduce.8.cloned.1.call-start = ((), (), s32[]{:S(2)}) async-start(), calls=%async_computation.11 | async-start | bytes 4718592 | tf_op jit(solution)/shard_map/psum | solution.py:209
  44.5 54.3 %copy-start.34 = (pred[1024]{0:T(1024)(128)(4,1)}, pred[1024]{0:T(1024)(128)(4,1)S(1)}, u32[]{:S(2)}) copy-start(pred[1024]{0:T(1024)(128)(4,1)S(1)} %fusion.49) | copy-start | bytes 3076
  75.7 23.8 %copy-start.22 = (f32[4,1152]{1,0:T(4,128)}, f32[4,1152]{1,0:T(4,128)S(1)}, u32[]{:S(2)}) copy-start(f32[4,1152]{1,0:T(4,128)S(1)} %get-tuple-element.168) | copy-start | bytes 55300
  98.8 2.2 copy-start.4
  98.8 2.2 copy-start.24
  99.4 2.6 copy-start.37
  99.5 5.1 copy-start.26
  101.0 3.5 copy-start.16
  112.3 2.8 copy-start.19
  116.8 0.8 copy-start.20
  121.7 145.5 %all-reduce.10.cloned.1.call-start = ((), (), s32[]{:S(2)}) async-start(), calls=%async_computation.12 | async-start | bytes 4718592 | tf_op jit(solution)/shard_map/psum | solution.py:239
  194.3 2.1 copy-start.2
  196.4 3.5 copy-start.17
  196.4 3.5 copy-start.14
  196.4 3.5 copy-start.36
  200.0 5.1 copy-start.40
  205.1 1.4 copy-start.41
  211.3 179.8 %all-reduce.12.cloned.1.call-start = ((), (), s32[]{:S(2)}) async-start(), calls=%async_computation.13 | async-start | bytes 4718592 | tf_op jit(solution)/shard_map/psum | solution.py:270
  267.2 4.5 copy-start.3
  267.2 5.2 copy-start.6
  277.8 3.3 copy-start.5
  277.8 1.5 copy-start.38
  279.4 1.8 copy-start.18
  291.0 1.5 copy-start.13
  293.7 1.2 copy-start.15
  293.7 1.9 copy-start.10
  310.4 116.4 %reduce-scatter.19.cloned.1.call-start = ((), (), s32[]{:S(2)}) async-start(), calls=%async_computation.18 | async-start | bytes 2949120
  318.6 326.1 %reduce-scatter.21.cloned.1.call-start = ((), (), s32[]{:S(2)}) async-start(), calls=%async_computation.19 | async-start | bytes 11943936
  323.0 68.1 %copy-start.23 = (f32[4,1152]{1,0:T(4,128)S(1)}, f32[4,1152]{1,0:T(4,128)}, u32[]{:S(2)}) copy-start(f32[4,1152]{1,0:T(4,128)} %copy-done.22) | copy-start | bytes 55300
  323.0 68.1 %copy-start.25 = (f32[1024]{0:T(1024)S(1)}, f32[1024]{0:T(1024)}, u32[]{:S(2)}) copy-start(f32[1024]{0:T(1024)} %copy-done.24) | copy-start | bytes 12292
  323.0 68.1 %copy-start.27 = (f32[1024]{0:T(1024)S(1)}, f32[1024]{0:T(1024)}, u32[]{:S(2)}) copy-start(f32[1024]{0:T(1024)} %copy-done.26) | copy-start | bytes 12292
  391.1 4.5 copy-start.7
  430.4 11.1 %copy-start.28 = (bf16[4,1152]{1,0:T(4,128)(2,1)S(1)}, bf16[4,1152]{1,0:T(4,128)(2,1)}, u32[]{:S(2)}) copy-start(bf16[4,1152]{1,0:T(4,128)(2,1)} %param.21) | copy-start | bytes 27652
  447.1 1.1 copy-start.21
  447.1 267.7 %reduce-scatter.13.cloned.1.call-start = ((), (), s32[]{:S(2)}) async-start(), calls=%async_computation.15 | async-start | bytes 1990656 | tf_op jit(solution)/shard_map/reduce_scatter | solution.py:318
  452.5 369.6 %reduce-scatter.11.cloned.1.call-start = ((), (), s32[]{:S(2)}) async-start(), calls=%async_computation.14 | async-start | bytes 5971968 | tf_op jit(solution)/shard_map/reduce_scatter | solution.py:313
  465.0 465.5 %reduce-scatter.15.cloned.1.call-start = ((), (), s32[]{:S(2)}) async-start(), calls=%async_computation.16 | async-start | bytes 5971968 | tf_op jit(solution)/shard_map/reduce_scatter | solution.py:314
  473.2 565.3 %reduce-scatter.17.cloned.1.call-start = ((), (), s32[]{:S(2)}) async-start(), calls=%async_computation.17 | async-start | bytes 5971968 | tf_op jit(solution)/shard_map/reduce_scatter | solution.py:319
  482.1 0.7 copy-start.35
  482.8 5.0 copy-start.33
  487.8 8.1 copy-start.39
  487.8 44.9 %copy-start.30 = (s32[512]{0:T(512)S(1)}, s32[512]{0:T(512)}, u32[]{:S(2)}) copy-start(s32[512]{0:T(512)} %copy-done.29) | copy-start | bytes 6148
  487.8 47.4 %copy-start.11 = (bf16[1024,288]{1,0:T(8,128)(2,1)S(1)}, bf16[1024,288]{1,0:T(8,128)(2,1)}, u32[]{:S(2)}) copy-start(bf16[1024,288]{1,0:T(8,128)(2,1)} %get-tuple-element.163) | copy-start | bytes 1769476
  490.1 42.6 %all-to-all-start.2 = ((bf16[8,128,288]{1,2,0:T(8,128)(2,1)}), bf16[8,128,288]{1,2,0:T(8,128)(2,1)}, u32[]{:S(2)}, u32[]{:S(2)}) async-start(bf16[8,128,288]{1,2,0:T(8,128)(2,1)} %bitcast.258), calls=%async_computation.2 | async-start | bytes 1179648 | tf_op jit(solution)/shard_map/all_to_all | solution.py:302
  532.0 506.5 %copy-start.1 = (bf16[1152,1152]{1,0:T(8,128)(2,1)S(1)}, bf16[1152,1152]{1,0:T(8,128)(2,1)}, u32[]{:S(2)}) copy-start(bf16[1152,1152]{1,0:T(8,128)(2,1)} %param.25) | copy-start | bytes 7962628
Sparse Core Ops, SparseCore 0:
  9.6 20.1 all-gather.1
  43.3 30.3 all-reduce.5
  121.8 68.6 all-reduce.7
  211.4 55.7 all-reduce.9
  310.5 80.5 all-reduce.11
  393.7 33.1 reduce-scatter.18
  447.2 197.4 reduce-scatter.20
  649.2 65.5 reduce-scatter.12
  719.0 103.0 reduce-scatter.10
  826.5 103.8 reduce-scatter.14
  934.6 103.7 reduce-scatter.16
where the time goes:
time: 1050 us
  waiting for transfers between devices  766 us (73%)
  matrix products  99.2 us (9%)
  other arithmetic  57.2 us (5%)
  blocking collectives  41 us (4%)
  local copies, waits for them, and re-layouts  39.6 us (4%)
  starting transfers between devices  19.8 us (2%)
  between operations  16.2 us (2%)
    unnamed x13, waiting for transfers between devices  133 us
    reduce_scatter x1, waiting for transfers between devices, body(): lax.psum_scatter(expand_grad, 'dp', scatter_dimension=0, tiled=True)  108 us
    reduce_scatter x1, waiting for transfers between devices, body(): lax.psum_scatter(shrink_grad, 'dp', scatter_dimension=1, tiled=True)  108 us
    reduce_scatter x1, waiting for transfers between devices, body(): lax.psum_scatter(entry_grad, 'dp', scatter_dimension=0, tiled=True)  107 us
    reduce_scatter x1, waiting for transfers between devices, body(): lax.psum_scatter(output_grad, 'dp', scatter_dimension=1, tiled=True)  67.4 us
    psum x1, waiting for transfers between devices, body(): lax.psum(jnp.dot(attended, output_weight, preferred_element_type=jnp.floa...  65.2 us
    psum x1, waiting for transfers between devices, body(): lax.psum(jnp.dot(projected_grad, entry_flat.T, preferred_element_type=jnp...  62.4 us
    psum x1, waiting for transfers between devices, body(): lax.psum(jnp.dot(hidden_grad, expand_weight.T, preferred_element_type=jnp...  55.6 us
  transfers between devices with their start and end apart: 14, of which 12 were waited for; matrix products, arithmetic and copies ran while one was open for 9% of the time, Pallas kernels for 0%

commit v1 on v0

v1 whole, which is shorter than its diff:
```python
from functools import partial

import jax
import jax.numpy as jnp
from jax import lax
from jax.experimental import pallas as pl
from jax.experimental.pallas import tpu as pltpu
from jax.sharding import PartitionSpec as P

HEAD = 72
QUARTERS = 4
SPARE = 8
scale = HEAD ** (-0.5)
epsilon = 1e-06
gelu_coeff = 0.7978845608028654
low = jnp.bfloat16
full = jnp.float32
VMEM_ASK = 48 * 1024 * 1024


def dot(a, b, dims=((1,), (0,))):
    return lax.dot_general(a, b, (dims, ((), ())), preferred_element_type=full)


def normalize(rows):
    centered = rows - jnp.mean(rows, axis=-1, keepdims=True)
    inverse = lax.rsqrt(jnp.mean(centered * centered, axis=-1, keepdims=True) + epsilon)
    return (centered * inverse, inverse)


def normalize_back(unit, inverse, grad):
    return inverse * (
        grad
        - jnp.mean(grad, axis=-1, keepdims=True)
        - unit * jnp.mean(grad * unit, axis=-1, keepdims=True)
    )


def gelu_both(value):
    square = value * value
    curve = jnp.tanh(gelu_coeff * (value + 0.044715 * square * value))
    slope = 0.5 * (1.0 + curve) + 0.5 * value * (1.0 - curve * curve) * gelu_coeff * (
        1.0 + 3.0 * 0.044715 * square
    )
    return (0.5 * value * (1.0 + curve), slope)


def swap(value, axis, bit):
    size = lax.axis_size(axis)
    return lax.ppermute(value, axis, [(index, index ^ bit) for index in range(size)])


def gather_blocks(own):
    near = swap(own, "tensor", 1)
    across = swap(own, "tensor", 2)
    return [own, near, across, swap(across, "tensor", 1)]


def sum_blocks(parts):
    got = swap(parts[3], "tensor", 1)
    far = (parts[2].astype(full) + got.astype(full)).astype(low)
    across = swap(far, "tensor", 2)
    got = swap(parts[1], "tensor", 1)
    return parts[0].astype(full) + got.astype(full) + across.astype(full)


def sum_owners(partial_sum):
    owners = lax.axis_size("dp")
    me = lax.axis_index("dp")
    rows, columns = partial_sum.shape
    step = 1
    held = partial_sum.reshape(owners, rows // owners, columns)
    while step < owners:
        pairs = held.reshape(held.shape[0] // 2, 2, held.shape[1], columns)
        mine = (me // step) % 2
        given = lax.dynamic_index_in_dim(pairs, 1 - mine, 1, keepdims=False)
        kept = lax.dynamic_index_in_dim(pairs, mine, 1, keepdims=False)
        got = swap(given, "dp", step)
        total = kept.astype(full) + got.astype(full)
        step *= 2
        held = total if step >= owners else total.astype(low)
    return held.reshape(rows // owners, columns)


def exchange_owners(slabs):
    owners = slabs.shape[0]
    if owners <= 8:
        return jnp.stack(
            [slabs[0]] + [swap(slabs[index], "dp", index) for index in range(1, owners)]
        )
    order = jnp.arange(owners, dtype=jnp.int32) ^ lax.axis_index("dp")
    sent = jnp.take(slabs, order, axis=0)
    got = lax.all_to_all(sent, "dp", split_axis=0, concat_axis=0, tiled=True)
    return jnp.take(got, order, axis=0)


def attend_kernel(projected_ref, bias_ref, output_ref, attended_ref, part_ref):
    rows, width_part = attended_ref.shape
    half = rows // 2
    for chunk in (1, 0):
        span = slice(chunk * half, (chunk + 1) * half)
        pieces = []
        for head in range(width_part // HEAD):
            at = head * HEAD
            queries = projected_ref[span, at : at + HEAD]
            keys = projected_ref[:, width_part + at : width_part + at + HEAD]
            values = projected_ref[:, 2 * width_part + at : 2 * width_part + at + HEAD]
            scores = dot(queries, keys, ((1,), (1,))) * scale + bias_ref[span, :]
            spread = jnp.exp(scores - jnp.max(scores, axis=1, keepdims=True))
            probs = spread * (1.0 / jnp.sum(spread, axis=1, keepdims=True))
            pieces.append(dot(probs.astype(low), values))
        attended = jnp.concatenate(pieces, axis=1).astype(low)
        attended_ref[span, :] = attended
        part_ref[span, :] = dot(attended, output_ref[...]).astype(low)


def attend_back_kernel(projected_ref, bias_ref, output_ref, branch_grad_ref, grad_ref):
    rows, width_all = projected_ref.shape
    width_part = width_all // 3
    attended_grad = dot(branch_grad_ref[...], output_ref[...], ((1,), (1,))).astype(low)
    pieces = [[], [], []]
    for head in range(width_part // HEAD):
        at = head * HEAD
        queries = projected_ref[:, at : at + HEAD]
        keys = projected_ref[:, width_part + at : width_part + at + HEAD]
        values = projected_ref[:, 2 * width_part + at : 2 * width_part + at + HEAD]
        grad = attended_grad[:, at : at + HEAD]
        scores = dot(keys, queries, ((1,), (1,))) * scale + bias_ref[...]
        spread = jnp.exp(scores - jnp.max(scores, axis=0, keepdims=True))
        probs = spread * (1.0 / jnp.sum(spread, axis=0, keepdims=True))
        pieces[2].append(dot(probs.astype(low), grad))
        prob_grad = dot(values, grad, ((1,), (1,)))
        delta = jnp.sum(probs * prob_grad, axis=0, keepdims=True)
        score_grad = (probs * (prob_grad - delta)).astype(low)
        pieces[1].append(dot(score_grad, queries) * scale)
        pieces[0].append(dot(score_grad, keys, ((0,), (0,))) * scale)
    grad_ref[...] = jnp.concatenate(pieces[0] + pieces[1] + pieces[2], axis=1).astype(low)


def body(
    kept_rows,
    owner_index,
    kept_position,
    resolution,
    mask_token,
    condition,
    modulate_weight,
    entry_weight,
    output_weight,
    expand_weight,
    shrink_weight,
    cotangent,
):
    owners = lax.axis_size("dp")
    me = lax.axis_index("dp")
    lane = lax.axis_index("tensor")
    kept_count, width_part = kept_rows.shape
    width = mask_token.shape[0]
    own_tokens = cotangent.shape[0]
    quarter = own_tokens // QUARTERS
    group = quarter // 2
    arrived_count = own_tokens // 2
    block = group + SPARE
    rows = QUARTERS * block
    capacity = 2 * kept_count // owners
    slots_all = owners * capacity
    big = resolution[0] == 1

    owner_local = owner_index ^ me
    owner_hot = (owner_local[:, None] == jnp.arange(owners, dtype=jnp.int32)[None, :]).astype(low)
    earlier = (jnp.arange(kept_count)[:, None] > jnp.arange(kept_count)[None, :]).astype(low)
    before = dot(earlier, owner_hot)
    ranking = jnp.sum(before * owner_hot.astype(full), axis=1).astype(jnp.int32)
    slot_index = owner_local * capacity + ranking
    pack_matrix = (
        slot_index[:, None] == jnp.arange(slots_all, dtype=jnp.int32)[None, :]
    ).astype(low)
    context_part = lax.dynamic_slice_in_dim(
        condition.astype(full), lane * width_part, width_part, 1
    )
    lifted = jax.nn.silu(context_part).astype(low)
    coded = kept_position + 1
    tags = jnp.stack([coded // 32, coded % 32]).astype(low)
    tags = jnp.concatenate([tags, jnp.zeros((6, kept_count), low)])
    packed = dot(jnp.concatenate([kept_rows.T, tags]), pack_matrix).astype(low)
    packed = jnp.transpose(packed.reshape(width_part + 8, owners, capacity), (1, 0, 2))
    riders = lifted.reshape(-1, capacity)
    packed = jnp.concatenate(
        [packed, jnp.broadcast_to(riders[None], (owners,) + riders.shape)], axis=1
    )
    arrived = exchange_owners(packed)
    lifted_all = arrived[:, width_part + 8 :].reshape(owners * QUARTERS, width_part)
    arrived_rows = jnp.transpose(arrived[:, : width_part + 2], (1, 0, 2)).reshape(
        width_part + 2, slots_all
    )
    place = (
        arrived_rows[width_part].astype(full) * 32.0 + arrived_rows[width_part + 1].astype(full)
    ).astype(jnp.int32) - 1
    arrived_rows = arrived_rows[:width_part]

    place_column = place[:, None]
    there = place_column >= 0
    slot_rank = jnp.sum((there & (place_column < place[None, :])).astype(jnp.int32), axis=0)
    slot_rank = jnp.where(place >= 0, slot_rank, -1)
    positions = jnp.arange(own_tokens, dtype=jnp.int32)[None, :]
    token_rank = jnp.sum((there & (place_column < positions)).astype(jnp.int32), axis=0)
    filled = jnp.sum((place_column == positions).astype(jnp.int32), axis=0) > 0

    def row_of(rank):
        return ((rank // group) ^ lane) * block + rank % group

    spare_row = ((jnp.arange(own_tokens, dtype=jnp.int32) // quarter) ^ lane) * block + group
    token_row = jnp.where(filled, row_of(token_rank), spare_row)
    row_ids = jnp.arange(rows, dtype=jnp.int32)
    row_inner = row_ids % block
    row_rank = jnp.where(
        row_inner < group, ((row_ids // block) ^ lane) * group + row_inner, own_tokens
    )
    is_spare = row_inner == group
    spread_matrix = (row_ids[:, None] == token_row[None, :]).astype(low)
    slot_matrix = (row_rank[:, None] == slot_rank[None, :]).astype(low)
    rank_matrix = (
        slot_rank[:, None] == jnp.arange(arrived_count, dtype=jnp.int32)[None, :]
    ).astype(low)
    compact = dot(arrived_rows, rank_matrix).astype(low)
    gathered = jnp.zeros((width, arrived_count), low)
    for index, piece in enumerate(gather_blocks(compact)):
        gathered = lax.dynamic_update_slice(gathered, piece, ((lane ^ index) * width_part, 0))
    select_matrix = (
        row_rank[:, None] == jnp.arange(arrived_count, dtype=jnp.int32)[None, :]
    ).astype(low)
    spatial = dot(select_matrix, gathered, ((1,), (1,)))
    spatial = jnp.where(is_spare[:, None], mask_token.astype(full)[None, :], spatial)

    table = dot(lifted, modulate_weight)
    table = table + swap(table, "tensor", 1)
    table = table + swap(table, "tensor", 2)
    local_rows = jnp.arange(QUARTERS, dtype=jnp.int32) ^ lane
    chosen = jnp.where(big, table[0:1], jnp.take(table, local_rows, axis=0))

    def per_row(index):
        piece = chosen[:, index * width : (index + 1) * width]
        return jnp.broadcast_to(piece[:, None, :], (QUARTERS, block, width)).reshape(rows, width)

    def own_row(index):
        return chosen[0:1, index * width : (index + 1) * width]

    upstream = dot(spread_matrix, cotangent)
    feed_grad = (per_row(5) * upstream).astype(low)
    upstream_own = upstream[:block]

    key_block = row_ids // block
    same = key_block[:, None] == key_block[None, :]
    kept_key = (row_inner < group)[None, :]
    spare_key = is_spare[None, :]
    allowed_small = same & (kept_key | spare_key)
    allowed_big = kept_key | (spare_key & (key_block == 0)[None, :])
    allowed = jnp.where(big, allowed_big, allowed_small)
    weight_log = jnp.where(
        spare_key, jnp.log(jnp.where(big, float(arrived_count), float(group))), 0.0
    )
    bias = jnp.where(allowed, weight_log, -1e30)

    unit_one, inverse_one = normalize(spatial)
    normed_one = (unit_one * (1.0 + per_row(1)) + per_row(0)).astype(low)
    entry_flat = jnp.transpose(entry_weight, (1, 2, 0)).reshape(3 * width_part, width)
    projected = dot(normed_one, entry_flat, ((1,), (1,))).astype(low)
    attended, branch_part = pl.pallas_call(
        attend_kernel,
        out_shape=(
            jax.ShapeDtypeStruct((rows, width_part), low),
            jax.ShapeDtypeStruct((rows, width), low),
        ),
        compiler_params=pltpu.CompilerParams(vmem_limit_bytes=VMEM_ASK),
    )(projected, bias, output_weight)
    branch = sum_blocks(branch_part.reshape(QUARTERS, block, width))
    middle = spatial[:block] + own_row(2) * branch
    unit_two, inverse_two = normalize(middle)
    normed_two = (unit_two * (1.0 + own_row(4)) + own_row(3)).astype(low)
    normed_two = jnp.concatenate(gather_blocks(normed_two))
    hidden = dot(normed_two, expand_weight)
    activated, slope = gelu_both(hidden)
    activated = activated.astype(low)
    hidden_grad = (dot(feed_grad, shrink_weight, ((1,), (1,))) * slope).astype(low)
    normed_two_grad = sum_blocks(
        dot(hidden_grad, expand_weight, ((1,), (1,))).astype(low).reshape(QUARTERS, block, width)
    )
    middle_grad = upstream_own + normalize_back(
        unit_two, inverse_two, normed_two_grad * (1.0 + own_row(4))
    )
    branch_grad = (own_row(2) * middle_grad).astype(low)
    branch_grad = jnp.concatenate(gather_blocks(branch_grad))

    feed = sum_blocks(dot(activated, shrink_weight).astype(low).reshape(QUARTERS, block, width))
    out_own = (middle + own_row(5) * feed).astype(low)
    shrink_grad = sum_owners(dot(feed_grad, activated, ((0,), (0,))).astype(low))
    expand_grad = sum_owners(dot(normed_two, hidden_grad, ((0,), (0,))).astype(low))
    column_ids = jnp.arange(width, dtype=jnp.int32)
    column_from = ((column_ids // width_part) ^ lane) * width_part + column_ids % width_part
    column_matrix = (column_ids[:, None] == column_from[None, :]).astype(low)

    def to_columns(own):
        moved = dot(own, column_matrix).astype(low)
        pieces = [
            moved[:, index * width_part : (index + 1) * width_part] for index in range(QUARTERS)
        ]
        return jnp.concatenate(
            [pieces[0]] + [swap(pieces[index], "tensor", index) for index in range(1, QUARTERS)]
        )

    layer_out = dot(to_columns(out_own), spread_matrix, ((0,), (0,))).astype(low).T

    output_grad = sum_owners(dot(branch_grad, attended, ((0,), (0,))).astype(low))
    projected_grad = pl.pallas_call(
        attend_back_kernel,
        out_shape=jax.ShapeDtypeStruct((rows, 3 * width_part), low),
        compiler_params=pltpu.CompilerParams(vmem_limit_bytes=VMEM_ASK),
    )(projected, bias.T, output_weight, branch_grad)
    normed_one_grad = sum_blocks(
        dot(projected_grad, entry_flat).astype(low).reshape(QUARTERS, block, width)
    )
    entry_grad = sum_owners(dot(normed_one, projected_grad, ((0,), (0,))).astype(low))
    unit_own = unit_one[:block]
    spatial_grad = middle_grad + normalize_back(
        unit_own, inverse_one[:block], normed_one_grad * (1.0 + own_row(1))
    )
    back = to_columns(spatial_grad.astype(low))
    slots_back = dot(back, slot_matrix, ((0,), (0,))).astype(low)

    sums = jnp.concatenate(
        [
            jnp.sum(field, axis=0)
            for field in (
                normed_one_grad,
                normed_one_grad * unit_own,
                middle_grad * branch,
                normed_two_grad,
                normed_two_grad * unit_two,
                upstream_own * feed,
            )
        ]
    )
    mask_sum = spatial_grad[group]
    mask_high = mask_sum.astype(low)
    mask_rest = (mask_sum - mask_high.astype(full)).astype(low)
    sums = jnp.concatenate([sums.astype(low), mask_high, mask_rest])
    sums = jnp.stack(gather_blocks(sums.reshape(-1, 128))).reshape(QUARTERS, 8 * width)
    table_local = sums[:, : 6 * width]
    mask_total = jnp.sum(
        sums[:, 6 * width : 7 * width].astype(full) + sums[:, 7 * width :].astype(full), axis=0
    )
    first = jnp.arange(QUARTERS, dtype=jnp.int32)[:, None] == 0
    table_small = jnp.take(table_local, local_rows, axis=0)
    table_big = jnp.where(first, jnp.sum(table_local.astype(full), axis=0, keepdims=True), 0.0)
    table_grad = jnp.where(big, table_big, table_small.astype(full)).astype(low)
    logistic = jax.nn.sigmoid(context_part)
    condition_grad = (
        dot(table_grad, modulate_weight, ((1,), (1,)))
        * logistic
        * (1.0 + context_part * (1.0 - logistic))
    )
    table_part = 6 * width // owners
    mask_part = width // owners
    mask_high = mask_total.astype(low)
    mask_rest = (mask_total - mask_high.astype(full)).astype(low)
    riders = jnp.concatenate(
        [
            jnp.transpose(table_grad.reshape(QUARTERS, owners, table_part), (1, 0, 2)).reshape(
                owners, QUARTERS * table_part
            ),
            mask_high.reshape(owners, mask_part),
            mask_rest.reshape(owners, mask_part),
        ],
        axis=1,
    )
    rider_rows = -(-riders.shape[1] // capacity)
    riders = jnp.pad(riders, ((0, 0), (0, rider_rows * capacity - riders.shape[1])))
    owner_order = jnp.arange(owners, dtype=jnp.int32) ^ me
    riders = jnp.take(riders, owner_order, axis=0).reshape(owners, rider_rows, capacity)
    slabs = jnp.transpose(slots_back.reshape(width_part, owners, capacity), (1, 0, 2))
    returned = exchange_owners(jnp.concatenate([slabs, riders], axis=1))
    riders = returned[:, width_part:].reshape(owners, rider_rows * capacity)
    table_all = riders[:, : QUARTERS * table_part].reshape(owners * QUARTERS, table_part)
    modulate_grad = dot(lifted_all, table_all, ((0,), (0,)))
    mask_pieces = riders[:, QUARTERS * table_part :].astype(full)
    mask_grad = jnp.sum(
        mask_pieces[:, :mask_part] + mask_pieces[:, mask_part : 2 * mask_part], axis=0
    )
    returned = jnp.transpose(returned[:, :width_part], (1, 0, 2)).reshape(width_part, slots_all)
    kept_grad = dot(returned, pack_matrix, ((1,), (1,))).astype(low).T

    return (
        layer_out,
        kept_grad,
        mask_grad,
        condition_grad,
        modulate_grad,
        entry_grad.reshape(entry_grad.shape[0], 3, width_part),
        output_grad.T,
        expand_grad,
        shrink_grad.T,
    )


def solution(mesh):
    return jax.shard_map(
        body,
        mesh=mesh,
        in_specs=(
            P("dp", "tensor"),
            P("dp"),
            P("dp"),
            P("dp"),
            P(),
            P("dp", None),
            P("tensor", None),
            P(None, None, "tensor"),
            P("tensor", None),
            P(None, "tensor"),
            P("tensor", None),
            P("dp", None),
        ),
        out_specs=(
            P("dp", "tensor"),
            P("dp", "tensor"),
            P("dp"),
            P("dp", "tensor"),
            P("tensor", "dp"),
            P("dp", None, "tensor"),
            P("tensor", "dp"),
            P("dp", "tensor"),
            P("tensor", "dp"),
        ),
        check_vma=False,
    )
```

time: 1050 us -> 363 us (0.35)
  waiting for transfers between devices: 766 us -> 136 us
  matrix products: 99.2 us -> 51.5 us
  starting transfers between devices: 19.8 us -> 64.8 us
  blocking collectives: 41 us -> 0 us
  other arithmetic: 57.2 us -> 39.4 us
  Pallas kernels: 0 us -> 13.5 us
  between operations: 16.2 us -> 2.95 us
    reduce_scatter x4 -> x0, waiting for transfers between devices: 391 us -> none  [the longest x1 108 us: body(): lax.psum_scatter(expand_grad, 'dp', scatter_dimension=0, tiled=True)]
    psum x4 -> x0, waiting for transfers between devices: 212 us -> none  [the longest x1 65.2 us: body(): lax.psum(jnp.dot(attended, output_weight, preferred_element_type=jnp.floa...]
    ppermute x0 -> x58, waiting for transfers between devices: none -> 136 us  [swap(): lax.ppermute(value, axis, [(index, index ^ bit) for index in range(size)])]
    unnamed x13 -> x0, waiting for transfers between devices: 133 us -> none
    ppermute x0 -> x58, starting transfers between devices: none -> 64.8 us  [swap(): lax.ppermute(value, axis, [(index, index ^ bit) for index in range(size)])]
    dot_general x26 -> x23, matrix products: 93.5 us -> 51.5 us  [dot(): return lax.dot_general(a, b, (dims, ((), ())), preferred_element_type=full)]
    unnamed x1 -> x0, blocking collectives: 34.9 us -> none
    reduce_sum x11 -> x7, other arithmetic: 35.6 us -> 6.67 us  [the longest x1 3.21 us: body(): jnp.sum((there & (place_column < place[None, :])).astype(jnp.int32), axis=0)]
  transfers between devices with their start and end apart: 14 -> 58, of which waited for: 12 -> 18; matrix products, arithmetic and copies ran while one was open for 9% -> 27% of each run, Pallas kernels for 0% -> 2%
where the time goes in v1:
time: 363 us; the launch traced here: 356 us
  waiting for transfers between devices  136 us (37%)
  starting transfers between devices  64.8 us (18%)
  matrix products  51.5 us (14%)
  local copies, waits for them, and re-layouts  48.3 us (13%)
  other arithmetic  39.4 us (11%)
  Pallas kernels  13.5 us (4%)
    ppermute x58, waiting for transfers between devices, swap(): lax.ppermute(value, axis, [(index, index ^ bit) for index in range(size)])  136 us
    ppermute x58, starting transfers between devices, swap(): lax.ppermute(value, axis, [(index, index ^ bit) for index in range(size)])  64.8 us
    dot_general x23, matrix products, dot(): return lax.dot_general(a, b, (dims, ((), ())), preferred_element_type=full)  51.5 us
    unnamed x139, local copies, waits for them, and re-layouts  12.2 us
    another operation x9, local copies, waits for them, and re-layouts, exchange_owners(): jnp.stack([slabs[0]] + [swap(slabs[index], 'dp', index) for index in rang...  11.8 us
    squeeze x12, local copies, waits for them, and re-layouts, sum_owners(): given = lax.dynamic_index_in_dim(pairs, 1 - mine, 1, keepdims=False)  7.97 us
    convert_element_type x8, other arithmetic, sum_owners(): held = total if step >= owners else total.astype(low)  7.76 us
  transfers between devices with their start and end apart: 58, of which 18 were waited for; matrix products, arithmetic and copies ran while one was open for 27% of the time, Pallas kernels for 2%

profile of v1, /device:TPU:0, one launch (start us, length us, event | category | flops | bytes accessed | tf_op | source)
XLA Modules:
  0.0 356.2 jit_solution(11025843489866205501)
XLA Ops:
  4.1 1.7 fusion.29
  6.0 2.2 pad_maximum_fusion.4
  8.8 3.0 collective-permute-start
  15.3 3.0 collective-permute-start.3
  22.1 2.8 fusion.172
  25.7 2.0 select_select_fusion
  28.3 3.6 %collective-permute-start.5 = (bf16[305,128]{1,0:T(8,128)(2,1)S(1)}, bf16[305,128]{1,0:T(8,128)(2,1)S(1)}, u32[]{:S(2)}, u32[]{:S(2)}) collective-permute-start(bf16[305,128]{1,0:T(8,128)(2,1)S(1)} %bitcast.251), channel_id=1, source_target_pairs={{0,24},{4,28},{8,16},{12,20},{16,8},{20,12},{24,0},{28,4},{1,25},{... | collective-permute-start | bytes 234248 | tf_op jit(solution)/shard_map/ppermute | solution.py:50
  33.3 1.7 copy.182
  34.9 1.7 copy.183
  36.6 1.7 copy.184
  40.6 3.6 %stack.81 = bf16[8,305,128]{2,0,1:T(8,128)(2,1)S(1)} concatenate(bf16[1,305,128]{2,0,1:T(2,128)(2,1)S(1)} %get-tuple-element.147, bf16[1,305,128]{2,0,1:T(2,128)(2,1)} %copy.181, bf16[1,305,128]{2,0,1:T(2,128)(2,1)} %copy.182, bf16[1,305,128]{2,0,1:T(2,128)(2,1)} %copy.183, bf16[1,305,128]{2,0,1:T(2,128)(2,1)} %copy.184, bf16[1,305,128]{2,0,1:T(2,128)(2,1)} %copy.185, ...), dimensions={0} | concatenate | bytes 1249280 | tf_op jit(solution)/shard_map/stack | solution.py:88
  44.4 3.2 convert_reduce_fusion
  48.6 1.7 collective-permute-start.11
  55.0 6.6 %collective-permute-done.8 = bf16[288,512]{1,0:T(8,128)(2,1)} collective-permute-done((bf16[288,512]{1,0:T(8,128)(2,1)}, bf16[288,512]{1,0:T(8,128)(2,1)}, u32[]{:S(2)}, u32[]{:S(2)}) %collective-permute-start.8) | collective-permute-done | bytes 294944 | tf_op jit(solution)/shard_map/ppermute | solution.py:50
  62.4 1.7 constant_dynamic-update-slice_fusion.1
  64.8 2.3 fusion.171
  67.6 2.0 fusion.11
  70.5 1.6 convolution_convert_fusion.7.projected_ref
  72.1 6.4 %shard_map.187 = (bf16[544,288]{1,0:T(8,128)(2,1)S(1)}, bf16[544,1152]{1,0:T(8,128)(2,1)S(1)}) custom-call(bf16[544,864]{1,0:T(8,128)(2,1)S(1)} %convolution_convert_fusion.7.projected_ref, f32[544,544]{1,0:T(8,128)S(1)} %copy-done.3, bf16[288,1152]{1,0:T(8,128)(2,1)S(1)} %copy-done.6), custom_call_target="tpu_custom_call" | custom-call | tf_op jit(solution)/shard_map/pallas_call | solution.py:268
  83.2 8.8 %collective-permute-done.14 = bf16[136,1152]{1,0:T(8,128)(2,1)} collective-permute-done((bf16[136,1152]{1,0:T(8,128)(2,1)}, bf16[136,1152]{1,0:T(8,128)(2,1)}, u32[]{:S(2)}, u32[]{:S(2)}) %collective-permute-start.14) | collective-permute-done | bytes 313376 | tf_op jit(solution)/shard_map/ppermute | solution.py:50
  91.9 1.6 fusion.163
  96.0 8.4 %collective-permute-done.16 = bf16[136,1152]{1,0:T(8,128)(2,1)} collective-permute-done((bf16[136,1152]{1,0:T(8,128)(2,1)}, bf16[136,1152]{1,0:T(8,128)(2,1)}, u32[]{:S(2)}, u32[]{:S(2)}) %collective-permute-start.16) | collective-permute-done | bytes 313376 | tf_op jit(solution)/shard_map/ppermute | solution.py:50
  104.6 3.7 %fusion.10 = (bf16[544,1152]{1,0:T(8,128)(2,1)S(1)}, f32[544,1152]{1,0:T(8,128)S(1)}) fusion(f32[4,1152]{1,0:T(4,128)S(1)} %get-tuple-element.162, bf16[1024,1152]{1,0:T(8,128)(2,1)} %param.23, s32[1024]{0:T(1024)S(1)} %fusion.130), kind=kOutput, calls=%fused_computation.32 | convolution fusion | flops 1285267456 | bytes 6141952 | tf_op jit(solution)/shard_map/dot_general | solution.py:22
  108.4 3.2 fusion.75
  111.6 2.5 convolution_convert_fusion
  114.2 2.5 fusion.3
  116.7 2.3 convolution_convert_fusion.4
  119.0 2.0 convolution_convert_fusion.3
  122.3 3.9 %convolution_convert_fusion.1 = bf16[1152,1152]{1,0:T(8,128)(2,1)S(1)} fusion(bf16[544,1152]{1,0:T(8,128)(2,1)S(1)} %fusion.3, bf16[136,1152]{1,0:T(8,128)(2,1)} %collective-permute-done.17, bf16[136,1152]{1,0:T(8,128)(2,1)} %collective-permute-done.16, bf16[136,1152]{1,0:T(8,128)(2,1)} %collective-permute-done.15, bf16[136,1152]{1,0:T(8,128)(2,1)} %add_convert_fusion.4), kind=kOutput, calls=%fused_computation.4 | convolution fusion | flops 1450229760 | bytes 5160960 | tf_op jit(solution)/shard_map/dot_general | solution.py:22
  129.8 8.0 %collective-permute-done.26 = bf16[136,1152]{1,0:T(8,128)(2,1)S(1)} collective-permute-done((bf16[136,1152]{1,0:T(8,128)(2,1)S(1)}, bf16[136,1152]{1,0:T(8,128)(2,1)S(1)}, u32[]{:S(2)}, u32[]{:S(2)}) %collective-permute-start.26) | collective-permute-done | bytes 313376 | tf_op jit(solution)/shard_map/ppermute | solution.py:50
  138.4 5.8 %collective-permute-done.20 = bf16[136,1152]{1,0:T(8,128)(2,1)S(1)} collective-permute-done((bf16[136,1152]{1,0:T(8,128)(2,1)S(1)}, bf16[136,1152]{1,0:T(8,128)(2,1)S(1)}, u32[]{:S(2)}, u32[]{:S(2)}) %collective-permute-start.20) | collective-permute-done | bytes 313376 | tf_op jit(solution)/shard_map/ppermute | solution.py:50
  144.1 1.8 multiply_reduce_fusion.3
  150.2 6.2 %collective-permute-done.28 = bf16[136,1152]{1,0:T(8,128)(2,1)S(1)} collective-permute-done((bf16[136,1152]{1,0:T(8,128)(2,1)S(1)}, bf16[136,1152]{1,0:T(8,128)(2,1)S(1)}, u32[]{:S(2)}, u32[]{:S(2)}) %collective-permute-start.28) | collective-permute-done | bytes 313376 | tf_op jit(solution)/shard_map/ppermute | solution.py:50
  162.4 1.6 convolution_convert_fusion.6
  164.0 2.5 copy.194
  166.5 1.8 dynamic-slice_bitcast_fusion.6
  170.9 7.1 %shard_map.188 = bf16[544,864]{1,0:T(8,128)(2,1)S(1)} custom-call(bf16[544,864]{1,0:T(8,128)(2,1)S(1)} %copy-done.5, f32[544,544]{1,0:T(8,128)S(1)} %copy-done.2, bf16[288,1152]{1,0:T(8,128)(2,1)S(1)} %copy-done.6, bf16[544,1152]{1,0:T(8,128)(2,1)S(1)} %pad_maximum_fusion.1.branch_grad_ref), custom_call_target="tpu_custom_call" | custom-call | tf_op jit(solution)/shard_map/pallas_call | solution.py:314
  179.0 3.2 convolution_convert_fusion.2
  182.2 4.2 %copy.193 = bf16[1152,864]{1,0:T(8,128)(2,1)} copy(bf16[1152,864]{0,1:T(8,128)(2,1)} %convolution_convert_fusion.2) | data formatting | bytes 3981312 | tf_op jit(solution)/shard_map/convert_element_type | solution.py:322
  186.4 3.3 convolution_convert_fusion.5
  192.2 1.9 fusion.4
  194.1 24.2 %collective-permute-done.52 = bf16[4,144,1152]{2,1,0:T(8,128)(2,1)} collective-permute-done((bf16[4,144,1152]{2,1,0:T(8,128)(2,1)}, bf16[4,144,1152]{2,1,0:T(8,128)(2,1)}, u32[]{:S(2)}, u32[]{:S(2)}) %collective-permute-start.52) | collective-permute-done | bytes 1327136 | tf_op jit(solution)/shard_map/ppermute | solution.py:50
  218.3 1.6 fusion.5
  220.0 7.8 %collective-permute-done.49 = bf16[4,144,288]{2,1,0:T(8,128)(2,1)} collective-permute-done((bf16[4,144,288]{2,1,0:T(8,128)(2,1)}, bf16[4,144,288]{2,1,0:T(8,128)(2,1)}, u32[]{:S(2)}, u32[]{:S(2)}) %collective-permute-start.49) | collective-permute-done | bytes 331808 | tf_op jit(solution)/shard_map/ppermute | solution.py:50
  229.9 9.3 %collective-permute-done.50 = bf16[2,144,288]{2,1,0:T(8,128)(2,1)S(1)} collective-permute-done((bf16[2,144,288]{2,1,0:T(8,128)(2,1)S(1)}, bf16[2,144,288]{2,1,0:T(8,128)(2,1)S(1)}, u32[]{:S(2)}, u32[]{:S(2)}) %collective-permute-start.50) | collective-permute-done | bytes 165920 | tf_op jit(solution)/shard_map/ppermute | solution.py:50
  239.3 2.5 collective-permute-start.51
  242.7 3.5 collective-permute-done.51
  251.8 1.9 collective-permute-done.37
  257.5 3.9 %fusion.40 = f32[4,288]{1,0:T(4,128)} fusion(bf16[288,6912]{1,0:T(8,128)(2,1)} %param.18, bf16[4,6912]{1,0:T(4,128)(2,1)S(1)} %gather_fusion.1, bf16[6912]{0:T(1024)(128)(2,1)S(1)} %convert_reduce_fusion.3, pred[4]{0:T(512)(128)(4,1)S(1)} %copy-done.48, pred[4]{0:T(512)(128)(4,1)S(1)} %copy-done.41, pred[]{:T(512)} %bitcast.11, bf16[4,1152]{1,0:T(4,128)(2,1)} %param.17, ...), kind=kOutput, calls=%fused_computation.93 | convolution fusion | flops 16046208 | bytes 4057357 | tf_op jit(solution)/shard_map/dot_general | solution.py:22
  263.8 1.7 fusion.30
  265.7 1.6 collective-permute-start.39
  271.4 9.0 %collective-permute-done.53 = bf16[2,144,1152]{2,1,0:T(8,128)(2,1)S(1)} collective-permute-done((bf16[2,144,1152]{2,1,0:T(8,128)(2,1)}, bf16[2,144,1152]{2,1,0:T(8,128)(2,1)S(1)}, u32[]{:S(2)}, u32[]{:S(2)}) %collective-permute-start.53) | collective-permute-done | bytes 663584 | tf_op jit(solution)/shard_map/ppermute | solution.py:50
  280.4 1.9 collective-permute-start.42
  283.3 1.9 collective-permute-start.43
  285.3 3.6 %collective-permute-start.44 = (bf16[318,128]{1,0:T(8,128)(2,1)S(1)}, bf16[318,128]{1,0:T(8,128)(2,1)S(1)}, u32[]{:S(2)}, u32[]{:S(2)}) collective-permute-start(bf16[318,128]{1,0:T(8,128)(2,1)S(1)} %get-tuple-element.145), channel_id=1, source_target_pairs={{0,24},{4,28},{8,16},{12,20},{16,8},{20,12},{24,0},{28,4},{1,25},{... | collective-permute-start | bytes 244232 | tf_op jit(solution)/shard_map/ppermute | solution.py:50
  289.5 5.4 %collective-permute-done.43 = bf16[318,128]{1,0:T(8,128)(2,1)S(1)} collective-permute-done((bf16[318,128]{1,0:T(8,128)(2,1)S(1)}, bf16[318,128]{1,0:T(8,128)(2,1)S(1)}, u32[]{:S(2)}, u32[]{:S(2)}) %collective-permute-start.43) | collective-permute-done | bytes 81440 | tf_op jit(solution)/shard_map/ppermute | solution.py:50
  294.8 7.6 %collective-permute-start.54 = (bf16[1,144,1152]{2,1,0:T(8,128)(2,1)}, bf16[1,144,1152]{2,1,0:T(8,128)(2,1)}, u32[]{:S(2)}, u32[]{:S(2)}) collective-permute-start(bf16[1,144,1152]{2,1,0:T(8,128)(2,1)} %constant_dynamic-slice_fusion.1), channel_id=1, source_target_pairs={{0,16},{4,20},{8,24},{12,28},{16,0},{20,4},{24,8},{28,12},{1,17},{... | collective-permute-start | bytes 995336 | tf_op jit(solution)/shard_map/ppermute | solution.py:50
  303.5 2.4 fusion.34
  308.7 10.2 %collective-permute-start.47 = (bf16[2,144,864]{2,1,0:T(8,128)(2,1)S(1)}, bf16[2,144,864]{2,1,0:T(8,128)(2,1)S(1)}, u32[]{:S(2)}, u32[]{:S(2)}) collective-permute-start(bf16[2,144,864]{2,1,0:T(8,128)(2,1)S(1)} %dynamic-slice_bitcast_fusion.5), channel_id=1, source_target_pairs={{0,8},{4,12},{8,0},{12,4},{16,24},{20,28},{24,16},{28,20},{1,9},{5... | collective-permute-start | bytes 1493000 | tf_op jit(solution)/shard_map/ppermute | solution.py:50
  320.8 1.9 add_bitcast_fusion
  322.7 15.1 %collective-permute-done.47 = bf16[2,144,864]{2,1,0:T(8,128)(2,1)S(1)} collective-permute-done((bf16[2,144,864]{2,1,0:T(8,128)(2,1)S(1)}, bf16[2,144,864]{2,1,0:T(8,128)(2,1)S(1)}, u32[]{:S(2)}, u32[]{:S(2)}) %collective-permute-start.47) | collective-permute-done | bytes 497696 | tf_op jit(solution)/shard_map/ppermute | solution.py:50
  339.0 1.9 add_bitcast_fusion.1
  340.8 11.8 %collective-permute-done.48 = bf16[1,144,864]{2,1,0:T(8,128)(2,1)S(1)} collective-permute-done((bf16[1,144,864]{2,1,0:T(8,128)(2,1)S(1)}, bf16[1,144,864]{2,1,0:T(8,128)(2,1)S(1)}, u32[]{:S(2)}, u32[]{:S(2)}) %collective-permute-start.48) | collective-permute-done | bytes 248864 | tf_op jit(solution)/shard_map/ppermute | solution.py:50
  353.5 1.6 reshape_reshape.16
  (358 shorter events, 82.0 us)
Async XLA Ops:
  0.6 113.5 %copy-start = (bf16[1152,1152]{1,0:T(8,128)(2,1)S(1)}, bf16[1152,1152]{1,0:T(8,128)(2,1)}, u32[]{:S(2)}) copy-start(bf16[1152,1152]{1,0:T(8,128)(2,1)} %param.22) | copy-start | bytes 7962628
  8.8 19.5 %collective-permute-start = (bf16[305,128]{1,0:T(8,128)(2,1)}, bf16[305,128]{1,0:T(8,128)(2,1)S(1)}, u32[]{:S(2)}, u32[]{:S(2)}) collective-permute-start(bf16[305,128]{1,0:T(8,128)(2,1)} %bitcast.216), channel_id=1, source_target_pairs={{0,4},{4,0},{8,12},{12,8},{16,20},{20,16},{24,28},{28,24},{1,5},{5... | collective-permute-start | bytes 234248 | tf_op jit(solution)/shard_map/ppermute | solution.py:50
  12.4 19.5 %collective-permute-start.1 = (bf16[305,128]{1,0:T(8,128)(2,1)}, bf16[305,128]{1,0:T(8,128)(2,1)}, u32[]{:S(2)}, u32[]{:S(2)}) collective-permute-start(bf16[305,128]{1,0:T(8,128)(2,1)} %bitcast.215), channel_id=1, source_target_pairs={{0,8},{4,12},{8,0},{12,4},{16,24},{20,28},{24,16},{28,20},{1,9},{5... | collective-permute-start | bytes 234248 | tf_op jit(solution)/shard_map/ppermute | solution.py:50
  14.6 20.3 %collective-permute-start.2 = (bf16[305,128]{1,0:T(8,128)(2,1)}, bf16[305,128]{1,0:T(8,128)(2,1)}, u32[]{:S(2)}, u32[]{:S(2)}) collective-permute-start(bf16[305,128]{1,0:T(8,128)(2,1)} %bitcast.214), channel_id=1, source_target_pairs={{0,12},{4,8},{8,4},{12,0},{16,28},{20,24},{24,20},{28,16},{1,13},{... | collective-permute-start | bytes 234248 | tf_op jit(solution)/shard_map/ppermute | solution.py:50
  15.3 21.3 %collective-permute-start.3 = (bf16[305,128]{1,0:T(8,128)(2,1)}, bf16[305,128]{1,0:T(8,128)(2,1)}, u32[]{:S(2)}, u32[]{:S(2)}) collective-permute-start(bf16[305,128]{1,0:T(8,128)(2,1)} %bitcast.213), channel_id=1, source_target_pairs={{0,16},{4,20},{8,24},{12,28},{16,0},{20,4},{24,8},{28,12},{1,17},{... | collective-permute-start | bytes 234248 | tf_op jit(solution)/shard_map/ppermute | solution.py:50
  18.9 19.4 %collective-permute-start.4 = (bf16[305,128]{1,0:T(8,128)(2,1)}, bf16[305,128]{1,0:T(8,128)(2,1)S(1)}, u32[]{:S(2)}, u32[]{:S(2)}) collective-permute-start(bf16[305,128]{1,0:T(8,128)(2,1)} %bitcast.212), channel_id=1, source_target_pairs={{0,20},{4,16},{8,28},{12,24},{16,4},{20,0},{24,12},{28,8},{1,21},{... | collective-permute-start | bytes 234248 | tf_op jit(solution)/shard_map/ppermute | solution.py:50
  28.3 10.8 %collective-permute-start.5 = (bf16[305,128]{1,0:T(8,128)(2,1)S(1)}, bf16[305,128]{1,0:T(8,128)(2,1)S(1)}, u32[]{:S(2)}, u32[]{:S(2)}) collective-permute-start(bf16[305,128]{1,0:T(8,128)(2,1)S(1)} %bitcast.251), channel_id=1, source_target_pairs={{0,24},{4,28},{8,16},{12,20},{16,8},{20,12},{24,0},{28,4},{1,25},{... | collective-permute-start | bytes 234248 | tf_op jit(solution)/shard_map/ppermute | solution.py:50
  31.9 8.0 %collective-permute-start.6 = (bf16[305,128]{1,0:T(8,128)(2,1)S(1)}, bf16[305,128]{1,0:T(8,128)(2,1)S(1)}, u32[]{:S(2)}, u32[]{:S(2)}) collective-permute-start(bf16[305,128]{1,0:T(8,128)(2,1)S(1)} %bitcast.250), channel_id=1, source_target_pairs={{0,28},{4,24},{8,20},{12,16},{16,12},{20,8},{24,4},{28,0},{1,29},{... | collective-permute-start | bytes 234248 | tf_op jit(solution)/shard_map/ppermute | solution.py:50
  34.9 12.7 %collective-permute-start.10 = (f32[4,6912]{1,0:T(4,128)S(1)}, f32[4,6912]{1,0:T(4,128)}, u32[]{:S(2)}, u32[]{:S(2)}) collective-permute-start(f32[4,6912]{1,0:T(4,128)S(1)} %fusion.172), channel_id=1, source_target_pairs={{0,1},{1,0},{2,3},{3,2},{4,5},{5,4},{6,7},{7,6},{8,9},{9,8},{10,11... | collective-permute-start | bytes 331784 | tf_op jit(solution)/shard_map/ppermute | solution.py:50
  48.6 5.5 %collective-permute-start.11 = (f32[4,6912]{1,0:T(4,128)S(1)}, f32[4,6912]{1,0:T(4,128)S(1)}, u32[]{:S(2)}, u32[]{:S(2)}) collective-permute-start(f32[4,6912]{1,0:T(4,128)S(1)} %add.474), channel_id=1, source_target_pairs={{0,2},{1,3},{2,0},{3,1},{4,6},{5,7},{6,4},{7,5},{8,10},{9,11},{10,... | collective-permute-start | bytes 331784 | tf_op jit(solution)/shard_map/ppermute | solution.py:50
  51.8 9.8 %collective-permute-start.7 = (bf16[288,512]{1,0:T(8,128)(2,1)}, bf16[288,512]{1,0:T(8,128)(2,1)S(1)}, u32[]{:S(2)}, u32[]{:S(2)}) collective-permute-start(bf16[288,512]{1,0:T(8,128)(2,1)} %get-tuple-element.170), channel_id=1, source_target_pairs={{0,1},{1,0},{2,3},{3,2},{4,5},{5,4},{6,7},{7,6},{8,9},{9,8},{10,11... | collective-permute-start | bytes 884744 | tf_op jit(solution)/shard_map/ppermute | solution.py:50
  52.1 9.5 %collective-permute-start.8 = (bf16[288,512]{1,0:T(8,128)(2,1)}, bf16[288,512]{1,0:T(8,128)(2,1)}, u32[]{:S(2)}, u32[]{:S(2)}) collective-permute-start(bf16[288,512]{1,0:T(8,128)(2,1)} %get-tuple-element.170), channel_id=1, source_target_pairs={{0,2},{1,3},{2,0},{3,1},{4,6},{5,7},{6,4},{7,5},{8,10},{9,11},{10,... | collective-permute-start | bytes 884744 | tf_op jit(solution)/shard_map/ppermute | solution.py:50
  61.6 2.5 collective-permute-start.9
  67.6 40.8 %copy-start.39 = (f32[544]{0:T(1024)}, f32[544]{0:T(1024)S(1)}, u32[]{:S(2)}) copy-start(f32[544]{0:T(1024)S(1)} %add_rsqrt_fusion) | copy-start | bytes 6532
  79.4 1.7 collective-permute-start.13
  79.9 3.3 collective-permute-start.12
  81.9 10.0 %collective-permute-start.14 = (bf16[136,1152]{1,0:T(8,128)(2,1)}, bf16[136,1152]{1,0:T(8,128)(2,1)}, u32[]{:S(2)}, u32[]{:S(2)}) collective-permute-start(bf16[136,1152]{1,0:T(8,128)(2,1)} %add_convert_fusion.5), channel_id=1, source_target_pairs={{0,2},{1,3},{2,0},{3,1},{4,6},{5,7},{6,4},{7,5},{8,10},{9,11},{10,... | collective-permute-start | bytes 940040 | tf_op jit(solution)/shard_map/ppermute | solution.py:50
  95.3 9.2 %collective-permute-start.16 = (bf16[136,1152]{1,0:T(8,128)(2,1)}, bf16[136,1152]{1,0:T(8,128)(2,1)}, u32[]{:S(2)}, u32[]{:S(2)}) collective-permute-start(bf16[136,1152]{1,0:T(8,128)(2,1)} %add_convert_fusion.4), channel_id=1, source_target_pairs={{0,2},{1,3},{2,0},{3,1},{4,6},{5,7},{6,4},{7,5},{8,10},{9,11},{10,... | collective-permute-start | bytes 940040 | tf_op jit(solution)/shard_map/ppermute | solution.py:50
  95.9 12.4 %collective-permute-start.15 = (bf16[136,1152]{1,0:T(8,128)(2,1)}, bf16[136,1152]{1,0:T(8,128)(2,1)}, u32[]{:S(2)}, u32[]{:S(2)}) collective-permute-start(bf16[136,1152]{1,0:T(8,128)(2,1)} %add_convert_fusion.4), channel_id=1, source_target_pairs={{0,1},{1,0},{2,3},{3,2},{4,5},{5,4},{6,7},{7,6},{8,9},{9,8},{10,11... | collective-permute-start | bytes 940040 | tf_op jit(solution)/shard_map/ppermute | solution.py:50
  104.4 3.9 %collective-permute-start.17 = (bf16[136,1152]{1,0:T(8,128)(2,1)}, bf16[136,1152]{1,0:T(8,128)(2,1)}, u32[]{:S(2)}, u32[]{:S(2)}) collective-permute-start(bf16[136,1152]{1,0:T(8,128)(2,1)} %collective-permute-done.16), channel_id=1, source_target_pairs={{0,1},{1,0},{2,3},{3,2},{4,5},{5,4},{6,7},{7,6},{8,9},{9,8},{10,11... | collective-permute-start | bytes 940040 | tf_op jit(solution)/shard_map/ppermute | solution.py:50
  121.0 6.5 %collective-permute-start.25 = (bf16[136,1152]{1,0:T(8,128)(2,1)S(1)}, bf16[136,1152]{1,0:T(8,128)(2,1)S(1)}, u32[]{:S(2)}, u32[]{:S(2)}) collective-permute-start(bf16[136,1152]{1,0:T(8,128)(2,1)S(1)} %get-tuple-element.133), channel_id=1, source_target_pairs={{0,1},{1,0},{2,3},{3,2},{4,5},{5,4},{6,7},{7,6},{8,9},{9,8},{10,11... | collective-permute-start | bytes 940040 | tf_op jit(solution)/shard_map/ppermute | solution.py:50
  121.6 8.2 %collective-permute-start.24 = (bf16[136,1152]{1,0:T(8,128)(2,1)S(1)}, bf16[136,1152]{1,0:T(8,128)(2,1)S(1)}, u32[]{:S(2)}, u32[]{:S(2)}) collective-permute-start(bf16[136,1152]{1,0:T(8,128)(2,1)S(1)} %get-tuple-element.132), channel_id=1, source_target_pairs={{0,1},{1,0},{2,3},{3,2},{4,5},{5,4},{6,7},{7,6},{8,9},{9,8},{10,11... | collective-permute-start | bytes 940040 | tf_op jit(solution)/shard_map/ppermute | solution.py:50
  121.7 6.6 %collective-permute-start.19 = (bf16[136,1152]{1,0:T(8,128)(2,1)S(1)}, bf16[136,1152]{1,0:T(8,128)(2,1)S(1)}, u32[]{:S(2)}, u32[]{:S(2)}) collective-permute-start(bf16[136,1152]{1,0:T(8,128)(2,1)S(1)} %get-tuple-element.135), channel_id=1, source_target_pairs={{0,1},{1,0},{2,3},{3,2},{4,5},{5,4},{6,7},{7,6},{8,9},{9,8},{10,11... | collective-permute-start | bytes 940040 | tf_op jit(solution)/shard_map/ppermute | solution.py:50
  122.2 16.1 %collective-permute-start.18 = (bf16[136,1152]{1,0:T(8,128)(2,1)S(1)}, bf16[136,1152]{1,0:T(8,128)(2,1)S(1)}, u32[]{:S(2)}, u32[]{:S(2)}) collective-permute-start(bf16[136,1152]{1,0:T(8,128)(2,1)S(1)} %get-tuple-element.134), channel_id=1, source_target_pairs={{0,1},{1,0},{2,3},{3,2},{4,5},{5,4},{6,7},{7,6},{8,9},{9,8},{10,11... | collective-permute-start | bytes 940040 | tf_op jit(solution)/shard_map/ppermute | solution.py:50
  126.2 30.2 %copy-start.25 = (bf16[1152,1152]{1,0:T(8,128)(2,1)}, bf16[1152,1152]{1,0:T(8,128)(2,1)S(1)}, u32[]{:S(2)}) copy-start(bf16[1152,1152]{1,0:T(8,128)(2,1)S(1)} %convolution_convert_fusion.1) | copy-start | bytes 7962628
  127.6 10.3 %collective-permute-start.26 = (bf16[136,1152]{1,0:T(8,128)(2,1)S(1)}, bf16[136,1152]{1,0:T(8,128)(2,1)S(1)}, u32[]{:S(2)}, u32[]{:S(2)}) collective-permute-start(bf16[136,1152]{1,0:T(8,128)(2,1)S(1)} %add_convert_fusion.1), channel_id=1, source_target_pairs={{0,2},{1,3},{2,0},{3,1},{4,6},{5,7},{6,4},{7,5},{8,10},{9,11},{10,... | collective-permute-start | bytes 940040 | tf_op jit(solution)/shard_map/ppermute | solution.py:50
  128.4 15.8 %collective-permute-start.20 = (bf16[136,1152]{1,0:T(8,128)(2,1)S(1)}, bf16[136,1152]{1,0:T(8,128)(2,1)S(1)}, u32[]{:S(2)}, u32[]{:S(2)}) collective-permute-start(bf16[136,1152]{1,0:T(8,128)(2,1)S(1)} %add_convert_fusion.3), channel_id=1, source_target_pairs={{0,2},{1,3},{2,0},{3,1},{4,6},{5,7},{6,4},{7,5},{8,10},{9,11},{10,... | collective-permute-start | bytes 940040 | tf_op jit(solution)/shard_map/ppermute | solution.py:50
  146.0 10.4 %collective-permute-start.28 = (bf16[136,1152]{1,0:T(8,128)(2,1)S(1)}, bf16[136,1152]{1,0:T(8,128)(2,1)S(1)}, u32[]{:S(2)}, u32[]{:S(2)}) collective-permute-start(bf16[136,1152]{1,0:T(8,128)(2,1)S(1)} %multiply_convert_fusion.1), channel_id=1, source_target_pairs={{0,2},{1,3},{2,0},{3,1},{4,6},{5,7},{6,4},{7,5},{8,10},{9,11},{10,... | collective-permute-start | bytes 940040 | tf_op jit(solution)/shard_map/ppermute | solution.py:50
  146.7 14.8 %collective-permute-start.27 = (bf16[136,1152]{1,0:T(8,128)(2,1)S(1)}, bf16[136,1152]{1,0:T(8,128)(2,1)S(1)}, u32[]{:S(2)}, u32[]{:S(2)}) collective-permute-start(bf16[136,1152]{1,0:T(8,128)(2,1)S(1)} %multiply_convert_fusion.1), channel_id=1, source_target_pairs={{0,1},{1,0},{2,3},{3,2},{4,5},{5,4},{6,7},{7,6},{8,9},{9,8},{10,11... | collective-permute-start | bytes 940040 | tf_op jit(solution)/shard_map/ppermute | solution.py:50
  148.2 9.5 %collective-permute-start.21 = (bf16[136,288]{1,0:T(8,128)(2,1)S(1)}, bf16[136,288]{1,0:T(8,128)(2,1)S(1)}, u32[]{:S(2)}, u32[]{:S(2)}) collective-permute-start(bf16[136,288]{1,0:T(8,128)(2,1)S(1)} %get-tuple-element.161), channel_id=1, source_target_pairs={{0,1},{1,0},{2,3},{3,2},{4,5},{5,4},{6,7},{7,6},{8,9},{9,8},{10,11... | collective-permute-start | bytes 235016 | tf_op jit(solution)/shard_map/ppermute | solution.py:50
  148.7 10.4 %collective-permute-start.22 = (bf16[136,288]{1,0:T(8,128)(2,1)S(1)}, bf16[136,288]{1,0:T(8,128)(2,1)S(1)}, u32[]{:S(2)}, u32[]{:S(2)}) collective-permute-start(bf16[136,288]{1,0:T(8,128)(2,1)S(1)} %get-tuple-element.160), channel_id=1, source_target_pairs={{0,2},{1,3},{2,0},{3,1},{4,6},{5,7},{6,4},{7,5},{8,10},{9,11},{10,... | collective-permute-start | bytes 235016 | tf_op jit(solution)/shard_map/ppermute | solution.py:50
  150.1 9.8 %collective-permute-start.23 = (bf16[136,288]{1,0:T(8,128)(2,1)S(1)}, bf16[136,288]{1,0:T(8,128)(2,1)S(1)}, u32[]{:S(2)}, u32[]{:S(2)}) collective-permute-start(bf16[136,288]{1,0:T(8,128)(2,1)S(1)} %get-tuple-element.159), channel_id=1, source_target_pairs={{0,3},{1,2},{2,1},{3,0},{4,7},{5,6},{6,5},{7,4},{8,11},{9,10},{10,... | collective-permute-start | bytes 235016 | tf_op jit(solution)/shard_map/ppermute | solution.py:50
  156.4 5.1 %collective-permute-start.29 = (bf16[136,1152]{1,0:T(8,128)(2,1)S(1)}, bf16[136,1152]{1,0:T(8,128)(2,1)S(1)}, u32[]{:S(2)}, u32[]{:S(2)}) collective-permute-start(bf16[136,1152]{1,0:T(8,128)(2,1)S(1)} %collective-permute-done.28), channel_id=1, source_target_pairs={{0,1},{1,0},{2,3},{3,2},{4,5},{5,4},{6,7},{7,6},{8,9},{9,8},{10,11... | collective-permute-start | bytes 940040 | tf_op jit(solution)/shard_map/ppermute | solution.py:50
  157.6 34.0 %collective-permute-start.55 = (bf16[4,144,1152]{2,1,0:T(8,128)(2,1)}, bf16[4,144,1152]{2,1,0:T(8,128)(2,1)}, u32[]{:S(2)}, u32[]{:S(2)}) collective-permute-start(bf16[4,144,1152]{2,1,0:T(8,128)(2,1)} %dynamic-slice_bitcast_fusion), channel_id=1, source_target_pairs={{0,4},{4,0},{8,12},{12,8},{16,20},{20,16},{24,28},{28,24},{1,5},{5... | collective-permute-start | bytes 3981320 | tf_op jit(solution)/shard_map/ppermute | solution.py:50
  159.2 59.2 %collective-permute-start.52 = (bf16[4,144,1152]{2,1,0:T(8,128)(2,1)}, bf16[4,144,1152]{2,1,0:T(8,128)(2,1)}, u32[]{:S(2)}, u32[]{:S(2)}) collective-permute-start(bf16[4,144,1152]{2,1,0:T(8,128)(2,1)} %dynamic-slice_bitcast_fusion.1), channel_id=1, source_target_pairs={{0,4},{4,0},{8,12},{12,8},{16,20},{20,16},{24,28},{28,24},{1,5},{5... | collective-permute-start | bytes 3981320 | tf_op jit(solution)/shard_map/ppermute | solution.py:50
  168.3 59.5 %collective-permute-start.49 = (bf16[4,144,288]{2,1,0:T(8,128)(2,1)}, bf16[4,144,288]{2,1,0:T(8,128)(2,1)}, u32[]{:S(2)}, u32[]{:S(2)}) collective-permute-start(bf16[4,144,288]{2,1,0:T(8,128)(2,1)} %dynamic-slice_bitcast_fusion.6), channel_id=1, source_target_pairs={{0,4},{4,0},{8,12},{12,8},{16,20},{20,16},{24,28},{28,24},{1,5},{5... | collective-permute-start | bytes 995336 | tf_op jit(solution)/shard_map/ppermute | solution.py:50
  190.8 116.5 %collective-permute-start.46 = (bf16[4,144,864]{2,1,0:T(8,128)(2,1)}, bf16[4,144,864]{2,1,0:T(8,128)(2,1)}, u32[]{:S(2)}, u32[]{:S(2)}) collective-permute-start(bf16[4,144,864]{2,1,0:T(8,128)(2,1)} %dynamic-slice_bitcast_fusion.2), channel_id=1, source_target_pairs={{0,4},{4,0},{8,12},{12,8},{16,20},{20,16},{24,28},{28,24},{1,5},{5... | collective-permute-start | bytes 2985992 | tf_op jit(solution)/shard_map/ppermute | solution.py:50
  191.6 37.4 %collective-permute-start.31 = (bf16[136,1152]{1,0:T(8,128)(2,1)S(1)}, bf16[136,1152]{1,0:T(8,128)(2,1)S(1)}, u32[]{:S(2)}, u32[]{:S(2)}) collective-permute-start(bf16[136,1152]{1,0:T(8,128)(2,1)S(1)} %get-tuple-element.131), channel_id=1, source_target_pairs={{0,1},{1,0},{2,3},{3,2},{4,5},{5,4},{6,7},{7,6},{8,9},{9,8},{10,11... | collective-permute-start | bytes 940040 | tf_op jit(solution)/shard_map/ppermute | solution.py:50
  191.7 55.2 %collective-permute-start.30 = (bf16[136,1152]{1,0:T(8,128)(2,1)S(1)}, bf16[136,1152]{1,0:T(8,128)(2,1)S(1)}, u32[]{:S(2)}, u32[]{:S(2)}) collective-permute-start(bf16[136,1152]{1,0:T(8,128)(2,1)S(1)} %get-tuple-element.130), channel_id=1, source_target_pairs={{0,1},{1,0},{2,3},{3,2},{4,5},{5,4},{6,7},{7,6},{8,9},{9,8},{10,11... | collective-permute-start | bytes 940040 | tf_op jit(solution)/shard_map/ppermute | solution.py:50
  194.1 33.7 %copy-start.22 = (bf16[1152,288]{1,0:T(8,128)(2,1)S(1)}, bf16[1152,288]{1,0:T(8,128)(2,1)}, u32[]{:S(2)}) copy-start(bf16[1152,288]{1,0:T(8,128)(2,1)} %copy.194) | copy-start | bytes 1990660
  218.3 50.3 %collective-permute-start.56 = (bf16[2,144,1152]{2,1,0:T(8,128)(2,1)S(1)}, bf16[2,144,1152]{2,1,0:T(8,128)(2,1)}, u32[]{:S(2)}, u32[]{:S(2)}) collective-permute-start(bf16[2,144,1152]{2,1,0:T(8,128)(2,1)S(1)} %dynamic-slice_bitcast_fusion.3), channel_id=1, source_target_pairs={{0,8},{4,12},{8,0},{12,4},{16,24},{20,28},{24,16},{28,20},{1,9},{5... | collective-permute-start | bytes 1990664 | tf_op jit(solution)/shard_map/ppermute | solution.py:50
  220.0 26.9 %copy-start.19 = (f32[544,1152]{1,0:T(8,128)S(1)}, f32[544,1152]{1,0:T(8,128)}, u32[]{:S(2)}) copy-start(f32[544,1152]{1,0:T(8,128)} %get-tuple-element.128) | copy-start | bytes 7520260
  229.0 10.2 %collective-permute-start.50 = (bf16[2,144,288]{2,1,0:T(8,128)(2,1)S(1)}, bf16[2,144,288]{2,1,0:T(8,128)(2,1)S(1)}, u32[]{:S(2)}, u32[]{:S(2)}) collective-permute-start(bf16[2,144,288]{2,1,0:T(8,128)(2,1)S(1)} %dynamic-slice_bitcast_fusion.7), channel_id=1, source_target_pairs={{0,8},{4,12},{8,0},{12,4},{16,24},{20,28},{24,16},{28,20},{1,9},{5... | collective-permute-start | bytes 497672 | tf_op jit(solution)/shard_map/ppermute | solution.py:50
  229.2 17.7 %collective-permute-start.32 = (bf16[136,1152]{1,0:T(8,128)(2,1)S(1)}, bf16[136,1152]{1,0:T(8,128)(2,1)S(1)}, u32[]{:S(2)}, u32[]{:S(2)}) collective-permute-start(bf16[136,1152]{1,0:T(8,128)(2,1)S(1)} %add_convert_fusion), channel_id=1, source_target_pairs={{0,2},{1,3},{2,0},{3,1},{4,6},{5,7},{6,4},{7,5},{8,10},{9,11},{10,... | collective-permute-start | bytes 940040 | tf_op jit(solution)/shard_map/ppermute | solution.py:50
  239.3 6.9 %collective-permute-start.51 = (bf16[1,144,288]{2,1,0:T(8,128)(2,1)S(1)}, bf16[1,144,288]{2,1,0:T(8,128)(2,1)S(1)}, u32[]{:S(2)}, u32[]{:S(2)}) collective-permute-start(bf16[1,144,288]{2,1,0:T(8,128)(2,1)S(1)} %constant_dynamic-slice_fusion.2), channel_id=1, source_target_pairs={{0,16},{4,20},{8,24},{12,28},{16,0},{20,4},{24,8},{28,12},{1,17},{... | collective-permute-start | bytes 248840 | tf_op jit(solution)/shard_map/ppermute | solution.py:50
  249.9 3.8 %collective-permute-start.37 = (bf16[72,128]{1,0:T(8,128)(2,1)S(1)}, bf16[72,128]{1,0:T(8,128)(2,1)S(1)}, u32[]{:S(2)}, u32[]{:S(2)}) collective-permute-start(bf16[72,128]{1,0:T(8,128)(2,1)S(1)} %bitcast.254), channel_id=1, source_target_pairs={{0,2},{1,3},{2,0},{3,1},{4,6},{5,7},{6,4},{7,5},{8,10},{9,11},{10,... | collective-permute-start | bytes 55304 | tf_op jit(solution)/shard_map/ppermute | solution.py:50
  251.7 2.8 collective-permute-start.36
  253.8 1.5 collective-permute-start.38
  254.0 8.4 %collective-permute-start.33 = (bf16[136,288]{1,0:T(8,128)(2,1)S(1)}, bf16[136,288]{1,0:T(8,128)(2,1)S(1)}, u32[]{:S(2)}, u32[]{:S(2)}) collective-permute-start(bf16[136,288]{1,0:T(8,128)(2,1)S(1)} %get-tuple-element.157), channel_id=1, source_target_pairs={{0,1},{1,0},{2,3},{3,2},{4,5},{5,4},{6,7},{7,6},{8,9},{9,8},{10,11... | collective-permute-start | bytes 235016 | tf_op jit(solution)/shard_map/ppermute | solution.py:50
  254.6 8.5 %collective-permute-start.34 = (bf16[136,288]{1,0:T(8,128)(2,1)S(1)}, bf16[136,288]{1,0:T(8,128)(2,1)S(1)}, u32[]{:S(2)}, u32[]{:S(2)}) collective-permute-start(bf16[136,288]{1,0:T(8,128)(2,1)S(1)} %get-tuple-element.156), channel_id=1, source_target_pairs={{0,2},{1,3},{2,0},{3,1},{4,6},{5,7},{6,4},{7,5},{8,10},{9,11},{10,... | collective-permute-start | bytes 235016 | tf_op jit(solution)/shard_map/ppermute | solution.py:50
  255.3 7.8 %collective-permute-start.35 = (bf16[136,288]{1,0:T(8,128)(2,1)S(1)}, bf16[136,288]{1,0:T(8,128)(2,1)S(1)}, u32[]{:S(2)}, u32[]{:S(2)}) collective-permute-start(bf16[136,288]{1,0:T(8,128)(2,1)S(1)} %get-tuple-element.155), channel_id=1, source_target_pairs={{0,3},{1,2},{2,1},{3,0},{4,7},{5,6},{6,5},{7,4},{8,11},{9,10},{10,... | collective-permute-start | bytes 235016 | tf_op jit(solution)/shard_map/ppermute | solution.py:50
  262.4 18.1 %collective-permute-start.53 = (bf16[2,144,1152]{2,1,0:T(8,128)(2,1)}, bf16[2,144,1152]{2,1,0:T(8,128)(2,1)S(1)}, u32[]{:S(2)}, u32[]{:S(2)}) collective-permute-start(bf16[2,144,1152]{2,1,0:T(8,128)(2,1)} %dynamic-slice_bitcast_fusion.4), channel_id=1, source_target_pairs={{0,8},{4,12},{8,0},{12,4},{16,24},{20,28},{24,16},{28,20},{1,9},{5... | collective-permute-start | bytes 1990664 | tf_op jit(solution)/shard_map/ppermute | solution.py:50
  265.7 17.6 %collective-permute-start.39 = (bf16[318,128]{1,0:T(8,128)(2,1)S(1)}, bf16[318,128]{1,0:T(8,128)(2,1)S(1)}, u32[]{:S(2)}, u32[]{:S(2)}) collective-permute-start(bf16[318,128]{1,0:T(8,128)(2,1)S(1)} %get-tuple-element.140), channel_id=1, source_target_pairs={{0,4},{4,0},{8,12},{12,8},{16,20},{20,16},{24,28},{28,24},{1,5},{5... | collective-permute-start | bytes 244232 | tf_op jit(solution)/shard_map/ppermute | solution.py:50
  267.3 18.0 %collective-permute-start.40 = (bf16[318,128]{1,0:T(8,128)(2,1)S(1)}, bf16[318,128]{1,0:T(8,128)(2,1)S(1)}, u32[]{:S(2)}, u32[]{:S(2)}) collective-permute-start(bf16[318,128]{1,0:T(8,128)(2,1)S(1)} %get-tuple-element.141), channel_id=1, source_target_pairs={{0,8},{4,12},{8,0},{12,4},{16,24},{20,28},{24,16},{28,20},{1,9},{5... | collective-permute-start | bytes 244232 | tf_op jit(solution)/shard_map/ppermute | solution.py:50
  268.7 20.2 %collective-permute-start.41 = (bf16[318,128]{1,0:T(8,128)(2,1)S(1)}, bf16[318,128]{1,0:T(8,128)(2,1)S(1)}, u32[]{:S(2)}, u32[]{:S(2)}) collective-permute-start(bf16[318,128]{1,0:T(8,128)(2,1)S(1)} %get-tuple-element.142), channel_id=1, source_target_pairs={{0,12},{4,8},{8,4},{12,0},{16,28},{20,24},{24,20},{28,16},{1,13},{... | collective-permute-start | bytes 244232 | tf_op jit(solution)/shard_map/ppermute | solution.py:50
  270.6 32.9 %copy-start.50 = (s32[512]{0:T(512)S(1)}, s32[512]{0:T(512)}, u32[]{:S(2)}) copy-start(s32[512]{0:T(512)} %copy-done.49) | copy-start | bytes 6148
  280.4 8.8 %collective-permute-start.42 = (bf16[318,128]{1,0:T(8,128)(2,1)S(1)}, bf16[318,128]{1,0:T(8,128)(2,1)S(1)}, u32[]{:S(2)}, u32[]{:S(2)}) collective-permute-start(bf16[318,128]{1,0:T(8,128)(2,1)S(1)} %get-tuple-element.143), channel_id=1, source_target_pairs={{0,16},{4,20},{8,24},{12,28},{16,0},{20,4},{24,8},{28,12},{1,17},{... | collective-permute-start | bytes 244232 | tf_op jit(solution)/shard_map/ppermute | solution.py:50
  283.3 11.5 %collective-permute-start.43 = (bf16[318,128]{1,0:T(8,128)(2,1)S(1)}, bf16[318,128]{1,0:T(8,128)(2,1)S(1)}, u32[]{:S(2)}, u32[]{:S(2)}) collective-permute-start(bf16[318,128]{1,0:T(8,128)(2,1)S(1)} %get-tuple-element.144), channel_id=1, source_target_pairs={{0,20},{4,16},{8,28},{12,24},{16,4},{20,0},{24,12},{28,8},{1,21},{... | collective-permute-start | bytes 244232 | tf_op jit(solution)/shard_map/ppermute | solution.py:50
  285.3 17.1 %collective-permute-start.44 = (bf16[318,128]{1,0:T(8,128)(2,1)S(1)}, bf16[318,128]{1,0:T(8,128)(2,1)S(1)}, u32[]{:S(2)}, u32[]{:S(2)}) collective-permute-start(bf16[318,128]{1,0:T(8,128)(2,1)S(1)} %get-tuple-element.145), channel_id=1, source_target_pairs={{0,24},{4,28},{8,16},{12,20},{16,8},{20,12},{24,0},{28,4},{1,25},{... | collective-permute-start | bytes 244232 | tf_op jit(solution)/shard_map/ppermute | solution.py:50
  288.9 13.6 %collective-permute-start.45 = (bf16[318,128]{1,0:T(8,128)(2,1)S(1)}, bf16[318,128]{1,0:T(8,128)(2,1)S(1)}, u32[]{:S(2)}, u32[]{:S(2)}) collective-permute-start(bf16[318,128]{1,0:T(8,128)(2,1)S(1)} %get-tuple-element.138), channel_id=1, source_target_pairs={{0,28},{4,24},{8,20},{12,16},{16,12},{20,8},{24,4},{28,0},{1,29},{... | collective-permute-start | bytes 244232 | tf_op jit(solution)/shard_map/ppermute | solution.py:50
  289.2 31.6 %collective-permute-start.57 = (bf16[1,144,1152]{2,1,0:T(8,128)(2,1)}, bf16[1,144,1152]{2,1,0:T(8,128)(2,1)}, u32[]{:S(2)}, u32[]{:S(2)}) collective-permute-start(bf16[1,144,1152]{2,1,0:T(8,128)(2,1)} %constant_dynamic-slice_fusion), channel_id=1, source_target_pairs={{0,16},{4,20},{8,24},{12,28},{16,0},{20,4},{24,8},{28,12},{1,17},{... | collective-permute-start | bytes 995336 | tf_op jit(solution)/shard_map/ppermute | solution.py:50
  294.8 44.1 %collective-permute-start.54 = (bf16[1,144,1152]{2,1,0:T(8,128)(2,1)}, bf16[1,144,1152]{2,1,0:T(8,128)(2,1)}, u32[]{:S(2)}, u32[]{:S(2)}) collective-permute-start(bf16[1,144,1152]{2,1,0:T(8,128)(2,1)} %constant_dynamic-slice_fusion.1), channel_id=1, source_target_pairs={{0,16},{4,20},{8,24},{12,28},{16,0},{20,4},{24,8},{28,12},{1,17},{... | collective-permute-start | bytes 995336 | tf_op jit(solution)/shard_map/ppermute | solution.py:50
  308.7 29.1 %collective-permute-start.47 = (bf16[2,144,864]{2,1,0:T(8,128)(2,1)S(1)}, bf16[2,144,864]{2,1,0:T(8,128)(2,1)S(1)}, u32[]{:S(2)}, u32[]{:S(2)}) collective-permute-start(bf16[2,144,864]{2,1,0:T(8,128)(2,1)S(1)} %dynamic-slice_bitcast_fusion.5), channel_id=1, source_target_pairs={{0,8},{4,12},{8,0},{12,4},{16,24},{20,28},{24,16},{28,20},{1,9},{5... | collective-permute-start | bytes 1493000 | tf_op jit(solution)/shard_map/ppermute | solution.py:50
  338.0 14.7 %collective-permute-start.48 = (bf16[1,144,864]{2,1,0:T(8,128)(2,1)S(1)}, bf16[1,144,864]{2,1,0:T(8,128)(2,1)S(1)}, u32[]{:S(2)}, u32[]{:S(2)}) collective-permute-start(bf16[1,144,864]{2,1,0:T(8,128)(2,1)S(1)} %constant_dynamic-slice_fusion.3), channel_id=1, source_target_pairs={{0,16},{4,20},{8,24},{12,28},{16,0},{20,4},{24,8},{28,12},{1,17},{... | collective-permute-start | bytes 746504 | tf_op jit(solution)/shard_map/ppermute | solution.py:50
  (52 other events, 460.7 us)

commit v2 on v1

v2 whole, which is shorter than its diff:
```python
from functools import partial

import jax
import jax.numpy as jnp
from jax import lax
from jax.experimental import pallas as pl
from jax.experimental.pallas import tpu as pltpu
from jax.sharding import PartitionSpec as P

HEAD = 72
QUARTERS = 4
SPARE = 8
scale = HEAD ** (-0.5)
epsilon = 1e-06
gelu_coeff = 0.7978845608028654
low = jnp.bfloat16
full = jnp.float32
VMEM_ASK = 32 * 1024 * 1024
RIDERS = 48
SWAP_OWNERS = 8


def dot(a, b, dims=((1,), (0,))):
    return lax.dot_general(a, b, (dims, ((), ())), preferred_element_type=full)


def normalize(rows):
    centered = rows - jnp.mean(rows, axis=-1, keepdims=True)
    inverse = lax.rsqrt(jnp.mean(centered * centered, axis=-1, keepdims=True) + epsilon)
    return (centered * inverse, inverse)


def normalize_back(unit, inverse, grad):
    return inverse * (
        grad
        - jnp.mean(grad, axis=-1, keepdims=True)
        - unit * jnp.mean(grad * unit, axis=-1, keepdims=True)
    )


def gelu_both(value):
    square = value * value
    curve = jnp.tanh(gelu_coeff * (value + 0.044715 * square * value))
    slope = 0.5 * (1.0 + curve) + 0.5 * value * (1.0 - curve * curve) * gelu_coeff * (
        1.0 + 3.0 * 0.044715 * square
    )
    return (0.5 * value * (1.0 + curve), slope)


def swap(value, axis, bit):
    size = lax.axis_size(axis)
    return lax.ppermute(value, axis, [(index, index ^ bit) for index in range(size)])


def gather_blocks(own):
    near = swap(own, "tensor", 1)
    across = swap(own, "tensor", 2)
    return [own, near, across, swap(across, "tensor", 1)]


def sum_far(part_2, part_3):
    got = swap(part_3, "tensor", 1)
    far = (part_2.astype(full) + got.astype(full)).astype(low)
    return far, swap(far, "tensor", 2)


class OwnerSum:
    def __init__(self, partial_sum, order):
        owners = lax.axis_size("dp")
        self.bits = owners.bit_length() - 1
        rows, columns = partial_sum.shape
        self.held = partial_sum.reshape((2,) * self.bits + (rows // owners, columns))
        self.left = list(range(self.bits - 1, -1, -1))
        self.order = list(order) + [bit for bit in range(self.bits) if bit not in order]
        self.send()

    def send(self):
        bit = self.order.pop(0)
        axis = self.left.index(bit)
        self.left.remove(bit)
        mine = (lax.axis_index("dp") >> bit) % 2
        given = lax.dynamic_index_in_dim(self.held, 1 - mine, axis, keepdims=False)
        self.kept = lax.dynamic_index_in_dim(self.held, mine, axis, keepdims=False)
        self.got = swap(given, "dp", 1 << bit)

    def step(self, *events):
        got = after(self.got, *events)
        total = self.kept.astype(full) + got.astype(full)
        if not self.order:
            self.held = total
            return total
        self.held = total.astype(low)
        self.send()
        return self.held

    def finish(self, *events):
        while True:
            last = not self.order
            total = self.step(*events)
            if last:
                return total


def exchange_owners(slabs):
    if len(slabs) > 1:
        return [slabs[0]] + [swap(slab, "dp", index) for index, slab in enumerate(slabs) if index]
    return [lax.all_to_all(slabs[0], "dp", split_axis=0, concat_axis=0, tiled=True)]


def attend(projected_ref, bias_ref, output_ref, attended_ref, chunk, half, width_part):
    span = slice(chunk * half, (chunk + 1) * half)
    pieces = []
    for head in range(width_part // HEAD):
        at = head * HEAD
        queries = projected_ref[span, at : at + HEAD]
        keys = projected_ref[:, width_part + at : width_part + at + HEAD]
        values = projected_ref[:, 2 * width_part + at : 2 * width_part + at + HEAD]
        scores = dot(queries, keys, ((1,), (1,))) * scale + bias_ref[span, :]
        spread = jnp.exp(scores - jnp.max(scores, axis=1, keepdims=True))
        probs = spread * (1.0 / jnp.sum(spread, axis=1, keepdims=True))
        pieces.append(dot(probs.astype(low), values))
    attended = jnp.concatenate(pieces, axis=1).astype(low)
    attended_ref[...] = attended
    return dot(attended, output_ref[...])


def entry_kernel(
    lane_ref,
    piece_0,
    piece_1,
    piece_2,
    piece_3,
    mask_ref,
    chosen_ref,
    entry_ref,
    bias_ref,
    output_ref,
    spatial_ref,
    normed_ref,
    projected_ref,
    attended_ref,
    part_0,
    part_1,
    gathered,
):
    lane = lane_ref[0]
    width_part = piece_0.shape[0]
    block, width = spatial_ref.shape
    group = block - SPARE
    half = 2 * block
    for index, piece in enumerate((piece_0, piece_1, piece_2, piece_3)):
        at = pl.multiple_of((lane ^ index) * width_part, 16)
        gathered[pl.ds(at, width_part), :] = piece[...]
    row_id = lax.broadcasted_iota(jnp.int32, (group, group), 0)
    column_id = lax.broadcasted_iota(jnp.int32, (group, group), 1)
    eye = (row_id == column_id).astype(full).astype(low)
    spare_id = lax.broadcasted_iota(jnp.int32, (SPARE, width), 0)
    spare = jnp.where(spare_id == 0, mask_ref[...].astype(full), 0.0)
    for chunk in (1, 0):
        span = slice(chunk * half, (chunk + 1) * half)
        normed = []
        for index in (2 * chunk, 2 * chunk + 1):
            at = pl.multiple_of((lane ^ index) * group, 128)
            kept = dot(eye, gathered[:, pl.ds(at, group)], ((1,), (1,)))
            rows = jnp.concatenate([kept, spare], axis=0)
            if index == 0:
                spatial_ref[...] = rows.astype(low)
            unit, inverse = normalize(rows)
            shift = chosen_ref[index : index + 1, :width]
            gain = chosen_ref[index : index + 1, width : 2 * width]
            normed.append(unit * (1.0 + gain) + shift)
        normed = jnp.concatenate(normed, axis=0).astype(low)
        normed_ref[span, :] = normed
        projected_ref[span, :] = dot(normed, entry_ref[...], ((1,), (1,))).astype(low)
    part = attend(projected_ref, bias_ref, output_ref, attended_ref, 1, half, width_part)
    part_0[...] = part[:block].astype(low)
    part_1[...] = part[block:].astype(low)


def attend_kernel(projected_ref, bias_ref, output_ref, attended_ref, part_0, part_1):
    block = part_0.shape[0]
    part = attend(
        projected_ref, bias_ref, output_ref, attended_ref, 0, 2 * block, output_ref.shape[0]
    )
    part_0[...] = part[:block].astype(low)
    part_1[...] = part[block:].astype(low)


def middle_kernel(
    part_0, part_1, part_2, spatial_ref, chosen_ref, branch_ref, middle_ref, normed_ref
):
    width = spatial_ref.shape[1]
    branch = part_0[...].astype(full) + part_1[...].astype(full) + part_2[...].astype(full)
    branch_ref[...] = branch
    middle = spatial_ref[...].astype(full) + chosen_ref[0:1, 2 * width : 3 * width] * branch
    middle_ref[...] = middle
    unit, inverse = normalize(middle)
    shift = chosen_ref[0:1, 3 * width : 4 * width]
    gain = chosen_ref[0:1, 4 * width : 5 * width]
    normed_ref[...] = (unit * (1.0 + gain) + shift).astype(low)


def feed_kernel(
    piece_0,
    piece_1,
    back_ref,
    expand_ref,
    normed_ref,
    activated_ref,
    hidden_grad_ref,
    part_0,
    part_1,
):
    block = piece_0.shape[0]
    normed = jnp.concatenate([piece_0[...].astype(full), piece_1[...].astype(full)], axis=0)
    normed = normed.astype(low)
    normed_ref[...] = normed
    hidden = dot(normed, expand_ref[...])
    activated, slope = gelu_both(hidden)
    activated_ref[...] = activated.astype(low)
    hidden_grad = (back_ref[...] * slope).astype(low)
    hidden_grad_ref[...] = hidden_grad
    part = dot(hidden_grad, expand_ref[...], ((1,), (1,)))
    part_0[...] = part[:block].astype(low)
    part_1[...] = part[block:].astype(low)


def middle_back_kernel(
    part_0,
    part_1,
    part_2,
    middle_ref,
    branch_ref,
    upstream_ref,
    chosen_ref,
    middle_grad_ref,
    branch_grad_ref,
    sums_ref,
):
    width = middle_ref.shape[1]
    normed_grad = part_0[...].astype(full) + part_1[...].astype(full) + part_2[...].astype(full)
    unit, inverse = normalize(middle_ref[...])
    gain = chosen_ref[0:1, 4 * width : 5 * width]
    middle_grad = upstream_ref[...] + normalize_back(unit, inverse, normed_grad * (1.0 + gain))
    middle_grad_ref[...] = middle_grad
    branch_grad_ref[...] = (chosen_ref[0:1, 2 * width : 3 * width] * middle_grad).astype(low)
    sums_ref[0:1, :] = jnp.sum(middle_grad * branch_ref[...], axis=0, keepdims=True)
    sums_ref[1:2, :] = jnp.sum(normed_grad, axis=0, keepdims=True)
    sums_ref[2:3, :] = jnp.sum(normed_grad * unit, axis=0, keepdims=True)


def attend_back_kernel(
    projected_ref,
    bias_ref,
    output_ref,
    entry_ref,
    piece_0,
    piece_1,
    piece_2,
    piece_3,
    branch_grad_ref,
    grad_ref,
    part_0,
    part_1,
):
    rows, width_all = projected_ref.shape
    width_part = width_all // 3
    block = piece_0.shape[0]
    half = 2 * block
    for chunk, pair in enumerate(((piece_0, piece_1), (piece_2, piece_3))):
        branch_grad_ref[chunk * half : (chunk + 1) * half, :] = jnp.concatenate(
            [piece[...].astype(full) for piece in pair], axis=0
        ).astype(low)
    attended_grad = dot(branch_grad_ref[...], output_ref[...], ((1,), (1,))).astype(low)
    pieces = [[], [], []]
    for head in range(width_part // HEAD):
        at = head * HEAD
        queries = projected_ref[:, at : at + HEAD]
        keys = projected_ref[:, width_part + at : width_part + at + HEAD]
        values = projected_ref[:, 2 * width_part + at : 2 * width_part + at + HEAD]
        grad = attended_grad[:, at : at + HEAD]
        scores = dot(keys, queries, ((1,), (1,))) * scale + bias_ref[...]
        spread = jnp.exp(scores - jnp.max(scores, axis=0, keepdims=True))
        probs = spread * (1.0 / jnp.sum(spread, axis=0, keepdims=True))
        pieces[2].append(dot(probs.astype(low), grad))
        prob_grad = dot(values, grad, ((1,), (1,)))
        delta = jnp.sum(probs * prob_grad, axis=0, keepdims=True)
        score_grad = (probs * (prob_grad - delta)).astype(low)
        pieces[1].append(dot(score_grad, queries) * scale)
        pieces[0].append(dot(score_grad, keys, ((0,), (0,))) * scale)
    grad_ref[...] = jnp.concatenate(pieces[0] + pieces[1] + pieces[2], axis=1).astype(low)
    part = dot(grad_ref[half:, :], entry_ref[...])
    part_0[...] = part[:block].astype(low)
    part_1[...] = part[block:].astype(low)


def entry_back_kernel(grad_ref, entry_ref, part_0, part_1):
    block = part_0.shape[0]
    part = dot(grad_ref[: 2 * block, :], entry_ref[...])
    part_0[...] = part[:block].astype(low)
    part_1[...] = part[block:].astype(low)


def pack_kernel(owners, me_ref, kept_ref, owner_ref, position_ref, riders_ref, *out_refs):
    slot_ref = out_refs[-1]
    extra, capacity = riders_ref.shape
    kept_count = kept_ref.shape[1]
    owner_local = owner_ref[...] ^ me_ref[0]
    owner_id = lax.broadcasted_iota(jnp.int32, (owners, kept_count), 0)
    hot = (owner_id == owner_local).astype(full)
    row_id = lax.broadcasted_iota(jnp.int32, (kept_count, kept_count), 0)
    column_id = lax.broadcasted_iota(jnp.int32, (kept_count, kept_count), 1)
    before = dot(hot.astype(low), (row_id < column_id).astype(full).astype(low))
    rank = jnp.sum(hot * before, axis=0, keepdims=True).astype(jnp.int32)
    slot = owner_local * capacity + rank
    slot_ref[...] = slot
    coded = position_ref[...] + 1
    tag_id = lax.broadcasted_iota(jnp.int32, (extra, kept_count), 0)
    tags = jnp.where(tag_id == 0, coded >> 5, jnp.where(tag_id == 1, coded & 31, 0))
    rows = jnp.concatenate([kept_ref[...], tags.astype(full).astype(low)], axis=0)
    slot_id = lax.broadcasted_iota(jnp.int32, (capacity, kept_count), 0)
    for index in range(owners):
        matrix = (slot_id + index * capacity == slot).astype(full).astype(low)
        slab = dot(rows, matrix, ((1,), (1,)))
        split = kept_ref.shape[0]
        slab = jnp.concatenate([slab[:split], slab[split:] + riders_ref[...].astype(full)], axis=0)
        if len(out_refs) == 2:
            out_refs[0][me_ref[0] ^ index] = slab.astype(low)
        else:
            out_refs[index][...] = slab.astype(low)


def unpack_kernel(owners, me_ref, *refs):
    slab_refs, (compact_ref, slot_rank_ref, token_rank_ref, arrived) = refs[:-4], refs[-4:]
    width_part, arrived_count = compact_ref.shape
    slots_all = arrived.shape[1]
    own_tokens = token_rank_ref.shape[1]
    capacity = slots_all // owners
    for index in range(owners):
        slab = slab_refs[0][me_ref[0] ^ index] if len(slab_refs) == 1 else slab_refs[index][...]
        arrived[:, index * capacity : (index + 1) * capacity] = slab
    tags = arrived[width_part : width_part + 16, :].astype(full)
    place = tags[0:1] * 32.0 + tags[1:2] - 1.0
    turned = jnp.transpose(jnp.broadcast_to(place, (8, slots_all)))[:, 0:1]
    turned = jnp.where(turned < 0.0, 1e9, turned)
    slot_rank = jnp.sum(jnp.where(turned < place, 1.0, 0.0), axis=0, keepdims=True)
    slot_rank = jnp.where(place < 0.0, -1.0, slot_rank).astype(jnp.int32)
    slot_rank_ref[...] = slot_rank
    spot = lax.broadcasted_iota(jnp.int32, (1, own_tokens), 1).astype(full)
    token_rank = jnp.sum(jnp.where(turned < spot, 1.0, 0.0), axis=0, keepdims=True)
    filled = jnp.sum(jnp.where(turned == spot, 1.0, 0.0), axis=0, keepdims=True)
    token_rank_ref[...] = jnp.where(filled > 0.0, token_rank, -1.0).astype(jnp.int32)
    rank_id = lax.broadcasted_iota(jnp.int32, (arrived_count, slots_all), 0)
    matrix = (rank_id == slot_rank).astype(full).astype(low)
    compact_ref[...] = dot(arrived[:width_part, :], matrix, ((1,), (1,))).astype(low)


def back_kernel(
    lane_ref,
    part_0,
    part_1,
    part_2,
    spatial_ref,
    middle_grad_ref,
    chosen_ref,
    sums_ref,
    feed_sum_ref,
    piece_0,
    piece_1,
    piece_2,
    piece_3,
    turned,
    riders,
):
    lane = lane_ref[0]
    block, width = spatial_ref.shape
    group = block - SPARE
    width_part = width // QUARTERS
    normed_grad = part_0[...].astype(full) + part_1[...].astype(full) + part_2[...].astype(full)
    unit, inverse = normalize(spatial_ref[...].astype(full))
    gain = chosen_ref[0:1, width : 2 * width]
    grad = middle_grad_ref[...] + normalize_back(unit, inverse, normed_grad * (1.0 + gain))
    turned[...] = jnp.transpose(grad[:group]).astype(low)
    mask_sum = grad[group : group + 1]
    mask_high = mask_sum.astype(low).astype(full)
    fields = [
        jnp.sum(normed_grad, axis=0, keepdims=True),
        jnp.sum(normed_grad * unit, axis=0, keepdims=True),
        sums_ref[0:1, :],
        sums_ref[1:2, :],
        sums_ref[2:3, :],
        feed_sum_ref[...],
        mask_high,
        mask_sum - mask_high,
    ]
    chunks = width // 128
    riders[...] = jnp.zeros_like(riders)
    for number, field in enumerate(fields):
        for chunk in range(chunks):
            at = number * chunks + chunk
            riders[at : at + 1, :] = field[:, chunk * 128 : (chunk + 1) * 128]
    rider_rows = riders[...].astype(low)
    for index, piece in enumerate((piece_0, piece_1, piece_2, piece_3)):
        at = pl.multiple_of((lane ^ index) * width_part, 16)
        piece[:width_part, :] = turned[pl.ds(at, width_part), :]
        piece[width_part:, :] = rider_rows


def slots_kernel(
    owners, lane_ref, me_ref, big_ref, rank_ref, piece_0, piece_1, piece_2, piece_3, *refs
):
    slab_refs, (table_ref, table, mask_total) = refs[:-3], refs[-3:]
    lane = lane_ref[0]
    me = me_ref[0]
    group = piece_0.shape[1]
    slots_all = rank_ref.shape[1]
    capacity = slots_all // owners
    chunks = table_ref.shape[1]
    width_part = slab_refs[0].shape[0] - RIDERS
    pieces = [piece_0, piece_1, piece_2, piece_3]
    rows = jnp.concatenate([piece[:width_part, :] for piece in pieces], axis=1)
    row_id = lax.broadcasted_iota(jnp.int32, (group, slots_all), 0)
    matrix = jnp.concatenate(
        [
            (row_id + (lane ^ index) * group == rank_ref[...]).astype(full).astype(low)
            for index in range(QUARTERS)
        ],
        axis=0,
    )
    slots = dot(rows, matrix)
    table[...] = jnp.zeros_like(table)
    summed = jnp.zeros((chunks, 128), full)
    mask_sum = jnp.zeros((16, 128), full)
    mask_rows = chunks // 6
    for index, piece in enumerate(pieces):
        field = piece[width_part : width_part + chunks, :].astype(full)
        summed = summed + field
        rest = piece[width_part + chunks - chunks % 16 :, :].astype(full)
        table[lane ^ index, :chunks, :] = field
        at = chunks % 16
        mask_sum = mask_sum + jnp.concatenate(
            [
                rest[at : at + mask_rows] + rest[at + mask_rows : at + 2 * mask_rows],
                jnp.zeros((16 - mask_rows, 128), full),
            ],
            axis=0,
        )
    mask_total[...] = mask_sum

    @pl.when(big_ref[0] == 1)
    def _():
        table[...] = jnp.zeros_like(table)
        table[0, :chunks, :] = summed

    table_ref[...] = table[:, :chunks, :].astype(low)
    for index in range(owners):
        owner = me ^ index
        start = (owner * chunks) // owners
        fields = [table[row, pl.ds(start, 8), :] for row in range(QUARTERS)]
        mask_start = (owner * mask_rows) // owners
        mask_part = mask_total[pl.ds(mask_start, 2), :]
        mask_high = mask_part.astype(low).astype(full)
        fields += [mask_high, mask_part - mask_high, jnp.zeros((RIDERS - 36, 128), full)]
        slab = jnp.concatenate([slots[:, index * capacity : (index + 1) * capacity]] + fields, axis=0)
        slab_refs[index][...] = slab.astype(low)


def kept_kernel(owners, me_ref, slot_ref, lifted_ref, *refs):
    slab_refs = refs[:owners]
    kept_ref, modulate_ref, mask_ref, table = refs[owners:]
    width_part, kept_count = kept_ref.shape
    capacity = slab_refs[0].shape[1]
    table_part = modulate_ref.shape[1]
    mask_part = mask_ref.shape[1]
    me = me_ref[0]
    rows = jnp.concatenate([slab[:width_part, :] for slab in slab_refs], axis=1)
    slot_id = lax.broadcasted_iota(jnp.int32, (owners * capacity, kept_count), 0)
    matrix = (slot_id == slot_ref[...]).astype(full).astype(low)
    kept_ref[...] = dot(rows, matrix).astype(low)
    mask_sum = jnp.zeros((1, 256), full)
    for index, slab in enumerate(slab_refs):
        rider = slab[width_part:, :].astype(full)
        for row in range(QUARTERS):
            at = index * QUARTERS + row
            for chunk in range(8):
                from_row = row * 8 + chunk
                table[at : at + 1, chunk * 128 : (chunk + 1) * 128] = rider[
                    from_row : from_row + 1
                ]
        high, rest = rider[32:34], rider[34:36]
        both = high + rest
        mask_sum = mask_sum + jnp.concatenate([both[0:1], both[1:2]], axis=1)
    shift = (me * table_part) % 128
    field = pltpu.roll(table[...], (1024 - shift) % 1024, 1)[:, :table_part]
    modulate_ref[...] = dot(lifted_ref[...], field.astype(low), ((0,), (0,)))
    shift = (me * mask_part) % 128
    mask_sum = jnp.broadcast_to(mask_sum, (8, 256))
    mask_ref[...] = pltpu.roll(mask_sum, (256 - shift) % 256, 1)[0:1, :mask_part]


def out_kernel(
    lane_ref,
    part_0,
    part_1,
    part_2,
    middle_ref,
    upstream_ref,
    chosen_ref,
    feed_sum_ref,
    piece_0,
    piece_1,
    piece_2,
    piece_3,
    turned,
    riders,
):
    lane = lane_ref[0]
    block, width = middle_ref.shape
    group = block - SPARE
    width_part = width // QUARTERS
    feed = part_0[...].astype(full) + part_1[...].astype(full) + part_2[...].astype(full)
    feed_sum_ref[...] = jnp.sum(feed * upstream_ref[...], axis=0, keepdims=True)
    out = middle_ref[...] + chosen_ref[0:1, 5 * width : 6 * width] * feed
    turned[...] = jnp.transpose(out[:group]).astype(low)
    riders[...] = jnp.zeros_like(riders)
    for chunk in range(width // 128):
        riders[chunk : chunk + 1, :] = out[group : group + 1, chunk * 128 : (chunk + 1) * 128]
    rider_rows = riders[...].astype(low)
    for index, piece in enumerate((piece_0, piece_1, piece_2, piece_3)):
        at = pl.multiple_of((lane ^ index) * width_part, 16)
        piece[:width_part, :] = turned[pl.ds(at, width_part), :]
        piece[width_part:, :] = rider_rows


def layer_kernel(
    lane_ref, rank_ref, piece_0, piece_1, piece_2, piece_3, out_ref, spare, turned
):
    lane = lane_ref[0]
    width_part, own_tokens = out_ref.shape
    group = piece_0.shape[1]
    quarter = own_tokens // QUARTERS
    pieces = (piece_0, piece_1, piece_2, piece_3)
    rows = jnp.concatenate([piece[:width_part, :] for piece in pieces], axis=1)
    row_id = lax.broadcasted_iota(jnp.int32, (group, own_tokens), 0)
    matrix = jnp.concatenate(
        [
            (row_id + (lane ^ index) * group == rank_ref[...]).astype(full).astype(low)
            for index in range(QUARTERS)
        ],
        axis=0,
    )
    spare[...] = jnp.zeros_like(spare)
    for index, piece in enumerate(pieces):
        rider = piece[width_part:, :].astype(full)
        for chunk in range(spare.shape[1] // 128):
            spare[index : index + 1, chunk * 128 : (chunk + 1) * 128] = rider[chunk : chunk + 1]
    turned[...] = jnp.transpose(spare[...])
    columns = turned[pl.ds(pl.multiple_of(lane * width_part, 16), width_part), :].astype(low)
    spare_id = lax.broadcasted_iota(jnp.int32, (8, own_tokens), 0)
    spot = lax.broadcasted_iota(jnp.int32, (8, own_tokens), 1) // quarter
    empty = rank_ref[...] < 0
    spots = jnp.where(((spare_id ^ lane) == spot) & (spare_id < QUARTERS) & empty, 1.0, 0.0)
    out_ref[...] = (dot(rows, matrix) + dot(columns, spots.astype(low))).astype(low)


def call(kernel, outs, *operands, **options):
    return pl.pallas_call(
        kernel,
        out_shape=tuple(jax.ShapeDtypeStruct(shape, kind) for shape, kind in outs),
        compiler_params=pltpu.CompilerParams(vmem_limit_bytes=VMEM_ASK),
        **options,
    )(*operands)


def after(value, *others):
    return lax.optimization_barrier((value,) + others)[0]


def body(
    kept_rows,
    owner_index,
    kept_position,
    resolution,
    mask_token,
    condition,
    modulate_weight,
    entry_weight,
    output_weight,
    expand_weight,
    shrink_weight,
    cotangent,
):
    owners = lax.axis_size("dp")
    me = lax.axis_index("dp")
    lane = lax.axis_index("tensor")
    kept_count, width_part = kept_rows.shape
    width = mask_token.shape[0]
    own_tokens = cotangent.shape[0]
    quarter = own_tokens // QUARTERS
    group = quarter // 2
    arrived_count = own_tokens // 2
    block = group + SPARE
    rows = QUARTERS * block
    capacity = 2 * kept_count // owners
    slots_all = owners * capacity
    big = resolution[0] == 1

    direct = owners <= SWAP_OWNERS
    small = pl.BlockSpec(memory_space=pltpu.SMEM)
    plain = pl.BlockSpec(memory_space=pltpu.VMEM)
    lane_word = lane.reshape(1).astype(jnp.int32)
    me_word = me.reshape(1).astype(jnp.int32)
    context_part = lax.dynamic_slice_in_dim(
        condition.astype(full), lane * width_part, width_part, 1
    )
    lifted = jax.nn.silu(context_part).astype(low)
    riders = lifted.reshape(-1, capacity)
    rider_count = riders.shape[0]
    extra = -(-(rider_count + 2) // 16) * 16
    riders = jnp.pad(riders, ((2, extra - 2 - rider_count), (0, 0)))
    slab_rows = width_part + extra
    if direct:
        slab_shapes = (((slab_rows, capacity), low),) * owners
    else:
        slab_shapes = (((owners, slab_rows, capacity), low),)
    *slabs, slot_index = call(
        partial(pack_kernel, owners),
        slab_shapes + (((1, kept_count), jnp.int32),),
        me_word,
        kept_rows.T,
        owner_index[None, :],
        kept_position[None, :],
        riders,
        in_specs=[small] + [plain] * 4,
    )
    slabs = exchange_owners(slabs)
    if direct:
        lifted_all = jnp.stack([slab[width_part + 2 : width_part + 2 + rider_count] for slab in slabs])
    else:
        owner_order = jnp.arange(owners, dtype=jnp.int32) ^ me
        lifted_all = slabs[0][:, width_part + 2 : width_part + 2 + rider_count]
    lifted_all = lifted_all.reshape(owners * QUARTERS, width_part)
    compact, slot_rank, token_rank = call(
        partial(unpack_kernel, owners),
        (
            ((width_part, arrived_count), low),
            ((1, slots_all), jnp.int32),
            ((1, own_tokens), jnp.int32),
        ),
        me_word,
        *slabs,
        in_specs=[small] + [plain] * len(slabs),
        scratch_shapes=[pltpu.VMEM((slab_rows, slots_all), low)],
    )
    spatial_pieces = gather_blocks(compact)
    token_flat = token_rank[0]
    spare_row = ((jnp.arange(own_tokens, dtype=jnp.int32) // quarter) ^ lane) * block + group
    token_row = jnp.where(
        token_flat >= 0,
        ((token_flat // group) ^ lane) * block + token_flat % group,
        spare_row,
    )
    row_ids = jnp.arange(rows, dtype=jnp.int32)
    row_inner = row_ids % block
    is_spare = row_inner == group
    spread_matrix = (row_ids[:, None] == token_row[None, :]).astype(low)

    table = dot(lifted, modulate_weight)
    table = table + swap(table, "tensor", 1)
    table = table + swap(table, "tensor", 2)
    local_rows = jnp.arange(QUARTERS, dtype=jnp.int32) ^ lane
    chosen = jnp.where(big, table[0:1], jnp.take(table, local_rows, axis=0))

    def per_row(index):
        piece = chosen[:, index * width : (index + 1) * width]
        return jnp.broadcast_to(piece[:, None, :], (QUARTERS, block, width)).reshape(rows, width)

    def own_row(index):
        return chosen[0:1, index * width : (index + 1) * width]

    upstream = dot(spread_matrix, cotangent)
    feed_grad = (per_row(5) * upstream).astype(low)
    upstream_own = upstream[:block]

    key_block = row_ids // block
    same = key_block[:, None] == key_block[None, :]
    kept_key = (row_inner < group)[None, :]
    spare_key = is_spare[None, :]
    allowed_small = same & (kept_key | spare_key)
    allowed_big = kept_key | (spare_key & (key_block == 0)[None, :])
    allowed = jnp.where(big, allowed_big, allowed_small)
    weight_log = jnp.where(
        spare_key, jnp.log(jnp.where(big, float(arrived_count), float(group))), 0.0
    )
    bias = jnp.where(allowed, weight_log, -1e30)
    bias_turned = bias.T

    entry_flat = jnp.transpose(entry_weight, (1, 2, 0)).reshape(3 * width_part, width)
    token_shape = ((block, width), low)
    half = 2 * block
    spatial_own, normed_one, projected, attended_far, part_2, part_3 = call(
        entry_kernel,
        (
            token_shape,
            ((rows, width), low),
            ((rows, 3 * width_part), low),
            ((half, width_part), low),
            token_shape,
            token_shape,
        ),
        lane_word,
        *spatial_pieces,
        mask_token[None, :],
        chosen[:, : 2 * width],
        entry_flat,
        bias,
        output_weight,
        in_specs=[small] + [plain] * 9,
        scratch_shapes=[pltpu.VMEM((width, arrived_count), low)],
    )
    far, across = sum_far(part_2, part_3)
    attended_near, part_0, part_1 = call(
        attend_kernel,
        (((half, width_part), low), token_shape, token_shape),
        after(projected, far),
        bias,
        output_weight,
    )
    got = swap(part_1, "tensor", 1)
    hidden_back = dot(after(feed_grad, part_0), shrink_weight, ((1,), (1,)))
    branch, middle, normed_two_own = call(
        middle_kernel,
        (((block, width), full), ((block, width), full), token_shape),
        part_0,
        got,
        after(across, hidden_back),
        spatial_own,
        chosen,
    )

    def feed_call(piece_0, piece_1, back):
        return call(
            feed_kernel,
            (((half, width), low), ((half, width), low), ((half, width), low))
            + (token_shape, token_shape),
            piece_0,
            piece_1,
            back,
            expand_weight,
        )

    near_piece = swap(normed_two_own, "tensor", 1)
    across = swap(normed_two_own, "tensor", 2)
    normed_near, activated_near, hidden_near, part_0, part_1 = feed_call(
        normed_two_own, near_piece, hidden_back[:half]
    )
    last_piece = swap(after(across, part_0), "tensor", 1)
    normed_far, activated_far, hidden_far, part_2, part_3 = feed_call(
        across, last_piece, hidden_back[half:]
    )
    far, across = sum_far(part_2, part_3)
    got = swap(part_1, "tensor", 1)
    activated = jnp.concatenate([after(activated_near, far), activated_far])
    shrink_partial = dot(feed_grad, activated, ((0,), (0,))).astype(low)
    shrink_sum = OwnerSum(shrink_partial, (0, 1, 2))
    normed_two = jnp.concatenate([after(normed_near, shrink_partial), normed_far])
    hidden_grad = jnp.concatenate([hidden_near, hidden_far])
    expand_partial = dot(normed_two, hidden_grad, ((0,), (0,))).astype(low)
    expand_sum = OwnerSum(expand_partial, (1, 0, 2))
    middle_grad, branch_grad_own, sums = call(
        middle_back_kernel,
        (((block, width), full), token_shape, ((SPARE, width), full)),
        part_0,
        got,
        after(across, expand_partial),
        middle,
        branch,
        upstream_own,
        chosen,
    )
    branch_pieces = gather_blocks(branch_grad_own)
    feed_parts = dot(after(activated, branch_grad_own), shrink_weight).astype(low)
    feed_parts = feed_parts.reshape(QUARTERS, block, width)
    feed_far = swap(feed_parts[3], "tensor", 1)
    feed_got = swap(feed_parts[1], "tensor", 1)
    feed_far = (feed_parts[2].astype(full) + feed_far.astype(full)).astype(low)
    branch_grad, projected_grad, part_2, part_3 = call(
        attend_back_kernel,
        (((rows, width), low), ((rows, 3 * width_part), low), token_shape, token_shape),
        projected,
        bias_turned,
        output_weight,
        entry_flat,
        *branch_pieces[:3],
        after(branch_pieces[3], feed_far),
    )
    feed_across = swap(after(feed_far, branch_pieces[3]), "tensor", 2)
    far, across = sum_far(part_2, after(part_3, feed_across))
    part_0, part_1 = call(
        entry_back_kernel, (token_shape, token_shape), after(projected_grad, far), entry_flat
    )
    got = swap(part_1, "tensor", 1)
    entry_partial = dot(
        after(normed_one, part_1), projected_grad, ((0,), (0,))
    ).astype(low)
    entry_sum = OwnerSum(entry_partial, (0, 1, 2))
    shrink_sum.step(entry_partial)
    expand_sum.step(entry_partial)
    piece_shape = ((width_part + 80, group), low)
    out_shape = ((width_part + 16, group), low)
    feed_sum, *out_pieces = call(
        out_kernel,
        (((1, width), full),) + (out_shape,) * QUARTERS,
        lane_word,
        feed_parts[0],
        feed_got,
        after(feed_across, entry_partial),
        middle,
        upstream_own,
        chosen,
        in_specs=[small] + [plain] * 6,
        scratch_shapes=[pltpu.VMEM((width, group), low), pltpu.VMEM((16, 128), full)],
    )
    back_pieces = call(
        back_kernel,
        (piece_shape,) * QUARTERS,
        lane_word,
        part_0,
        got,
        across,
        spatial_own,
        middle_grad,
        chosen,
        sums,
        feed_sum,
        in_specs=[small] + [plain] * 8,
        scratch_shapes=[pltpu.VMEM((width, group), low), pltpu.VMEM((80, 128), full)],
    )
    back_pieces = [back_pieces[0]] + [
        swap(back_pieces[index], "tensor", index) for index in range(1, QUARTERS)
    ]
    output_partial = dot(
        after(branch_grad, entry_partial),
        jnp.concatenate([attended_near, attended_far]),
        ((0,), (0,)),
    ).astype(low)
    output_sum = OwnerSum(output_partial, (0, 1, 2))
    chunks = 6 * width // 128
    big_word = resolution[:1]
    logistic = jax.nn.sigmoid(context_part)
    logistic = logistic * (1.0 + context_part * (1.0 - logistic))
    if direct:
        *slabs, table_grad = call(
            partial(slots_kernel, owners),
            (((width_part + RIDERS, capacity), low),) * owners
            + (((QUARTERS, chunks, 128), low),),
            lane_word,
            me_word,
            big_word,
            slot_rank,
            *back_pieces,
            in_specs=[small] * 3 + [plain] * 5,
            scratch_shapes=[
                pltpu.VMEM((QUARTERS, chunks + 2, 128), full),
                pltpu.VMEM((16, 128), full),
            ],
        )
        slabs = exchange_owners(slabs)
        table_grad = table_grad.reshape(QUARTERS, 6 * width)
        kept_grad, modulate_grad, mask_grad = call(
            partial(kept_kernel, owners),
            (
                ((width_part, kept_count), low),
                ((width_part, 6 * width // owners), full),
                ((1, width // owners), full),
            ),
            me_word,
            slot_index,
            lifted_all,
            *slabs,
            in_specs=[small] + [plain] * (2 + owners),
            scratch_shapes=[pltpu.VMEM((owners * QUARTERS, 1024), full)],
        )
        mask_grad = mask_grad[0]
    else:
        rows_back = jnp.concatenate([piece[:width_part] for piece in back_pieces], axis=1)
        rank_ids = jnp.arange(arrived_count, dtype=jnp.int32)
        rank_ids = ((rank_ids // group) ^ lane) * group + rank_ids % group
        matrix = (rank_ids[:, None] == slot_rank).astype(low)
        slabs = dot(rows_back, matrix).astype(low).reshape(width_part, owners, capacity)
        slabs = jnp.take(jnp.transpose(slabs, (1, 0, 2)), owner_order, axis=0)
        slabs = jnp.take(exchange_owners([slabs])[0], owner_order, axis=0)
        slabs = jnp.transpose(slabs, (1, 0, 2)).reshape(width_part, slots_all)
        slot_ids = jnp.arange(slots_all, dtype=jnp.int32)[:, None]
        kept_grad = dot(slabs, (slot_ids == slot_index).astype(low)).astype(low)
        riders = jnp.stack([piece[width_part : width_part + 8 * width // 128] for piece in back_pieces])
        riders = riders.reshape(QUARTERS, 8, width).astype(full)
        mask_total = jnp.sum(riders[:, 6] + riders[:, 7], axis=0)
        table_local = riders[:, :6].reshape(QUARTERS, 6 * width)
        table_small = jnp.take(table_local, jnp.arange(QUARTERS, dtype=jnp.int32) ^ lane, axis=0)
        first = jnp.arange(QUARTERS, dtype=jnp.int32)[:, None] == 0
        table_big = jnp.where(first, jnp.sum(table_local, axis=0, keepdims=True), 0.0)
        table_grad = jnp.where(big, table_big, table_small).astype(low)
        sent = jnp.transpose(table_grad.reshape(QUARTERS, owners, -1), (1, 0, 2))
        table_all = exchange_owners([sent])[0].reshape(owners * QUARTERS, -1)
        modulate_grad = dot(lifted_all, table_all, ((0,), (0,)))
        mask_grad = lax.psum_scatter(mask_total, "dp", scatter_dimension=0, tiled=True)
    condition_grad = dot(table_grad, modulate_weight, ((1,), (1,))) * logistic
    out_pieces = [out_pieces[0]] + [
        swap(after(out_pieces[index], *slabs[:1]), "tensor", index) for index in range(1, QUARTERS)
    ]
    layer_out = call(
        layer_kernel,
        (((width_part, own_tokens), low),),
        lane_word,
        token_rank,
        *out_pieces,
        in_specs=[small] + [plain] * 5,
        scratch_shapes=[pltpu.VMEM((8, width), full), pltpu.VMEM((width, 8), full)],
    )[0]
    shrink_grad = shrink_sum.finish()
    expand_grad = expand_sum.finish()
    entry_grad = entry_sum.finish()
    output_grad = output_sum.finish()

    return (
        layer_out.T,
        kept_grad.T,
        mask_grad,
        condition_grad,
        modulate_grad,
        entry_grad.reshape(entry_grad.shape[0], 3, width_part),
        output_grad.T,
        expand_grad,
        shrink_grad.T,
    )


def solution(mesh):
    return jax.shard_map(
        body,
        mesh=mesh,
        in_specs=(
            P("dp", "tensor"),
            P("dp"),
            P("dp"),
            P("dp"),
            P(),
            P("dp", None),
            P("tensor", None),
            P(None, None, "tensor"),
            P("tensor", None),
            P(None, "tensor"),
            P("tensor", None),
            P("dp", None),
        ),
        out_specs=(
            P("dp", "tensor"),
            P("dp", "tensor"),
            P("dp"),
            P("dp", "tensor"),
            P("tensor", "dp"),
            P("dp", None, "tensor"),
            P("tensor", "dp"),
            P("dp", "tensor"),
            P("tensor", "dp"),
        ),
        check_vma=False,
    )
```

time: 363 us -> 285 us (0.79)
  waiting for transfers between devices: 136 us -> 98.9 us
  matrix products: 51.5 us -> 24.4 us
  Pallas kernels: 13.5 us -> 39.4 us
  other arithmetic: 39.4 us -> 17.8 us
  starting transfers between devices: 64.8 us -> 52.6 us
  local copies, waits for them, and re-layouts: 48.3 us -> 44 us
    ppermute x58 -> x55, waiting for transfers between devices: 136 us -> 98.9 us  [swap(): lax.ppermute(value, axis, [(index, index ^ bit) for index in range(size)])]
    dot_general x23 -> x9, matrix products: 51.5 us -> 24.4 us  [dot(): return lax.dot_general(a, b, (dims, ((), ())), preferred_element_type=full)]
    pallas_call x2 -> x15, Pallas kernels: 13.5 us -> 39.4 us  [call(): pl.pallas_call(kernel, out_shape=tuple((jax.ShapeDtypeStruct(shape, kind)...]
    another operation x13 -> x1, local copies, waits for them, and re-layouts: 13.5 us -> 1.27 us  [body(): jnp.stack([slab[width_part + 2:width_part + 2 + rider_count] for slab in...]
    ppermute x58 -> x55, starting transfers between devices: 64.8 us -> 52.6 us  [swap(): lax.ppermute(value, axis, [(index, index ^ bit) for index in range(size)])]
    reduce_sum x10 -> x0, other arithmetic: 8.89 us -> none  [the longest x1 3.21 us: body(): jnp.sum((there & (place_column < place[None, :])).astype(jnp.int32), axis=0)]
    dynamic_slice x0 -> x4, local copies, waits for them, and re-layouts: none -> 7.07 us  [the longest x2 4.72 us: send(): self.kept = lax.dynamic_index_in_dim(self.held, mine, axis, keepdims=False)]
    unnamed x139 -> x111, local copies, waits for them, and re-layouts: 12.2 us -> 18.9 us
  transfers between devices with their start and end apart: 58 -> 55, of which waited for: 18 -> 22; matrix products, arithmetic and copies ran while one was open for 27% -> 25% of each run, Pallas kernels for 2% -> 10%
where the time goes in v2:
time: 285 us; the launch traced here: 280 us
  waiting for transfers between devices  98.9 us (35%)
  starting transfers between devices  52.6 us (18%)
  local copies, waits for them, and re-layouts  44 us (15%)
  Pallas kernels  39.4 us (14%)
  matrix products  24.4 us (9%)
  other arithmetic  17.8 us (6%)
    ppermute x55, waiting for transfers between devices, swap(): lax.ppermute(value, axis, [(index, index ^ bit) for index in range(size)])  98.9 us
    ppermute x55, starting transfers between devices, swap(): lax.ppermute(value, axis, [(index, index ^ bit) for index in range(size)])  52.6 us
    pallas_call x15, Pallas kernels, call(): pl.pallas_call(kernel, out_shape=tuple((jax.ShapeDtypeStruct(shape, kind)...  39.4 us
    dot_general x9, matrix products, dot(): return lax.dot_general(a, b, (dims, ((), ())), preferred_element_type=full)  24.4 us
    unnamed x111, local copies, waits for them, and re-layouts  18.9 us
    convert_element_type x8, other arithmetic, step(): self.held = total.astype(low)  6.87 us
  transfers between devices with their start and end apart: 55, of which 22 were waited for; matrix products, arithmetic and copies ran while one was open for 25% of the time, Pallas kernels for 10%

profile of v2, /device:TPU:0, one launch (start us, length us, event | category | flops | bytes accessed | tf_op | source)
XLA Modules:
  0.0 279.7 jit_solution(3177690399212566779)
XLA Ops:
  4.0 1.7 shard_map.187
  5.7 3.0 %collective-permute-start = (bf16[304,128]{1,0:T(8,128)(2,1)S(1)}, bf16[304,128]{1,0:T(8,128)(2,1)S(1)}, u32[]{:S(2)}, u32[]{:S(2)}) collective-permute-start(bf16[304,128]{1,0:T(8,128)(2,1)S(1)} %get-tuple-element.94), channel_id=1, source_target_pairs={{0,4},{4,0},{8,12},{12,8},{16,20},{20,16},{24,28},{28,24},{1,5},{5... | collective-permute-start | bytes 233480 | tf_op jit(solution)/shard_map/ppermute | solution.py:52
  8.7 1.6 collective-permute-start.1
  10.3 3.0 %collective-permute-start.3 = (bf16[304,128]{1,0:T(8,128)(2,1)}, bf16[304,128]{1,0:T(8,128)(2,1)S(1)}, u32[]{:S(2)}, u32[]{:S(2)}) collective-permute-start(bf16[304,128]{1,0:T(8,128)(2,1)} %get-tuple-element.97), channel_id=1, source_target_pairs={{0,16},{4,20},{8,24},{12,28},{16,0},{20,4},{24,8},{28,12},{1,17},{... | collective-permute-start | bytes 233480 | tf_op jit(solution)/shard_map/ppermute | solution.py:52
  15.3 3.4 %fusion.49 = f32[4,6912]{1,0:T(4,128)} fusion(bf16[4,288]{1,0:T(4,128)(2,1)S(1)} %fusion.33, bf16[288,6912]{1,0:T(8,128)(2,1)} %param.18), kind=kOutput, calls=%fused_computation.137 | convolution fusion | flops 15925248 | bytes 4094208 | tf_op jit(solution)/shard_map/dot_general | solution.py:24
  18.7 1.9 select_select_fusion
  21.9 3.6 %collective-permute-start.5 = (bf16[304,128]{1,0:T(8,128)(2,1)}, bf16[304,128]{1,0:T(8,128)(2,1)S(1)}, u32[]{:S(2)}, u32[]{:S(2)}) collective-permute-start(bf16[304,128]{1,0:T(8,128)(2,1)} %get-tuple-element.99), channel_id=1, source_target_pairs={{0,24},{4,28},{8,16},{12,20},{16,8},{20,12},{24,0},{28,4},{1,25},{... | collective-permute-start | bytes 233480 | tf_op jit(solution)/shard_map/ppermute | solution.py:52
  26.3 2.1 collective-permute-done.5.refs_6_
  28.4 5.0 %collective-permute-done.6.refs_7_ = bf16[304,128]{1,0:T(8,128)(2,1)S(1)} collective-permute-done((bf16[304,128]{1,0:T(8,128)(2,1)}, bf16[304,128]{1,0:T(8,128)(2,1)S(1)}, u32[]{:S(2)}, u32[]{:S(2)}) %collective-permute-start.6) | collective-permute-done | bytes 77856 | tf_op jit(solution)/shard_map/ppermute | solution.py:52
  36.1 3.7 %shard_map.188 = (bf16[288,512]{1,0:T(8,128)(2,1)}, s32[1,1024]{1,0:T(1,128)S(1)}, s32[1,1024]{1,0:T(1,128)S(1)}) custom-call(s32[1]{0:T(128)} %bitcast.1.me_ref, bf16[304,128]{1,0:T(8,128)(2,1)S(1)} %copy-done.28, bf16[304,128]{1,0:T(8,128)(2,1)S(1)} %copy-done.26, bf16[304,128]{1,0:T(8,128)(2,1)S(1)} %copy-done.22, ...), custom_call_target="tpu_custom_call" | custom-call | tf_op jit(solution)/shard_map/pallas_call | solution.py:567
  39.8 1.5 collective-permute-start.8
  42.8 5.5 %collective-permute-done.11 = f32[4,6912]{1,0:T(4,128)S(1)} collective-permute-done((f32[4,6912]{1,0:T(4,128)S(1)}, f32[4,6912]{1,0:T(4,128)S(1)}, u32[]{:S(2)}, u32[]{:S(2)}) %collective-permute-start.11) | collective-permute-done | bytes 110624 | tf_op jit(solution)/shard_map/ppermute | solution.py:52
  49.0 3.3 %gather_fusion = f32[4,6912]{1,0:T(4,128)} fusion(f32[4,6912]{1,0:T(4,128)} %add.221, s32[1024]{0:T(1024)S(1)} %pad_clamp_fusion), kind=kCustom, calls=%fused_computation | custom fusion | bytes 221200 | tf_op jit(solution)/shard_map/jit(_take)/gather | solution.py:672
  55.2 1.6 copy-done.2
  56.8 1.3 copy-done.4
  58.1 6.4 %shard_map.189 = (bf16[136,1152]{1,0:T(8,128)(2,1)S(1)}, bf16[544,1152]{1,0:T(8,128)(2,1)S(1)}, bf16[544,864]{1,0:T(8,128)(2,1)S(1)}, bf16[272,288]{1,0:T(8,128)...) custom-call(s32[1]{0:T(128)} %bitcast.lane_ref, bf16[288,512]{1,0:T(8,128)(2,1)} %get-tuple-element.102.piece_0, ...), custom_call_target="tpu_custom_call" | custom-call | tf_op jit(solution)/shard_map/pallas_call | solution.py:567
  66.1 1.7 fusion.2
  67.9 1.6 collective-permute-start.14
  69.5 3.2 %shard_map.190 = (bf16[272,288]{1,0:T(8,128)(2,1)S(1)}, bf16[136,1152]{1,0:T(8,128)(2,1)S(1)}, bf16[136,1152]{1,0:T(8,128)(2,1)S(1)}) custom-call(bf16[544,864]{1,0:T(8,128)(2,1)S(1)} %get-tuple-element.106.projected_ref, f32[544,544]{1,0:T(8,128)S(1)} %copy-done.5, bf16[288,1152]{1,0:T(8,128)(2,1)S(1)} %copy-done.7), custom_call_target="tpu_custom_call" | custom-call | tf_op jit(solution)/shard_map/pallas_call | solution.py:567
  73.5 2.0 fusion.50
  75.5 2.2 collective-permute-done.14.part_2
  78.1 1.6 collective-permute-start.16
  79.8 1.4 collective-permute-done.15.piece_1
  81.3 2.6 shard_map.192
  83.9 3.2 %collective-permute-done.16.piece_0 = bf16[136,1152]{1,0:T(8,128)(2,1)S(1)} collective-permute-done((bf16[136,1152]{1,0:T(8,128)(2,1)S(1)}, bf16[136,1152]{1,0:T(8,128)(2,1)S(1)}, u32[]{:S(2)}, u32[]{:S(2)}) %collective-permute-start.16) | collective-permute-done | bytes 313376 | tf_op jit(solution)/shard_map/ppermute | solution.py:52
  89.6 2.4 shard_map.193
  94.7 1.6 collective-permute-start.20
  96.3 4.0 %convolution_convert_fusion.1 = bf16[1152,1152]{1,0:T(8,128)(2,1)} fusion(bf16[544,1152]{1,0:T(8,128)(2,1)S(1)} %get-tuple-element.109, bf16[544,1152]{1,0:T(8,128)(2,1)S(1)} %constant_dynamic-update-slice_fusion), kind=kOutput, calls=%fused_computation.2 | convolution fusion | flops 1445216256 | bytes 5160960 | tf_op jit(solution)/shard_map/dot_general | solution.py:24
  100.4 4.0 %convolution_convert_fusion = bf16[1152,1152]{1,0:T(8,128)(2,1)} fusion(bf16[272,1152]{1,0:T(8,128)(2,1)S(1)} %get-tuple-element.123, bf16[272,1152]{1,0:T(8,128)(2,1)S(1)} %get-tuple-element.122, bf16[272,1152]{1,0:T(8,128)(2,1)S(1)} %get-tuple-element.125, bf16[272,1152]{1,0:T(8,128)(2,1)S(1)} %get-tuple-element.124), kind=kOutput, calls=%fused_computation.1 | convolution fusion | flops 1450229760 | bytes 5160960 | tf_op jit(solution)/shard_map/dot_general | solution.py:24
  104.5 1.4 shard_map.194
  105.9 1.5 collective-permute-start.23
  107.4 2.0 convolution_convert_fusion.3
  110.3 1.3 constant_dynamic-update-slice_fusion.3
  114.3 1.3 collective-permute-done.23.piece_2
  118.6 3.3 %constant_dynamic-slice_fusion.1 = (bf16[2,2,1,144,1152]{4,3,2,1,0:T(8,128)(2,1)}, bf16[2,2,1,144,1152]{4,3,2,1,0:T(8,128)(2,1)S(1)}) fusion(bf16[2,2,2,144,1152]{4,3,2,1,0:T(8,128)(2,1)} %bitcast.152, s32[]{:T(128)S(6)} %select_n.233, s32[]{:T(128)S(6)} %select_n.234), kind=kLoop, calls=%fused_computation.98 | loop fusion | bytes 5308424 | tf_op jit(solution)/shard_map/jit(dynamic_index_in_dim)/dynamic_slice | solution.py:83
  124.0 8.8 %shard_map.195 = (bf16[544,1152]{1,0:T(8,128)(2,1)S(1)}, bf16[544,864]{1,0:T(8,128)(2,1)S(1)}, bf16[136,1152]{1,0:T(8,128)(2,1)S(1)}, bf16[136,1152]{1,0:T(8,128)(2,1)S(1)}) custom-call(bf16[544,864]{1,0:T(8,128)(2,1)S(1)} %copy-done.12, f32[544,544]{1,0:T(8,128)S(1)} %copy-done.10, bf16[288,1152]{1,0:T(8,128)(2,1)S(1)} %copy-done.7, ...), custom_call_target="tpu_custom_call" | custom-call | tf_op jit(solution)/shard_map/pallas_call | solution.py:567
  132.9 1.4 constant_dynamic-slice_fusion.3
  137.6 1.6 shard_map.196
  139.3 3.1 %convolution_convert_fusion.2 = bf16[1152,864]{0,1:T(8,128)(2,1)} fusion(bf16[544,1152]{1,0:T(8,128)(2,1)S(1)} %copy-done.32, bf16[544,864]{1,0:T(8,128)(2,1)S(1)} %get-tuple-element.138.grad_ref), kind=kOutput, calls=%fused_computation.3 | convolution fusion | flops 1083912192 | bytes 4184064 | tf_op jit(solution)/shard_map/dot_general | solution.py:24
  142.4 1.6 convolution_convert_fusion.4
  144.0 1.5 copy.28
  145.6 8.7 %collective-permute-done.52 = bf16[2,2,144,1152]{3,2,0,1:T(8,128)(2,1)} collective-permute-done((bf16[2,2,144,1152]{3,2,0,1:T(8,128)(2,1)}, bf16[2,2,144,1152]{3,2,0,1:T(8,128)(2,1)}, u32[]{:S(2)}, u32[]{:S(2)}) %collective-permute-start.52) | collective-permute-done | bytes 1327136 | tf_op jit(solution)/shard_map/ppermute | solution.py:52
  154.7 2.3 fusion
  157.9 9.4 %collective-permute-done.49 = bf16[2,2,144,1152]{3,2,0,1:T(8,128)(2,1)} collective-permute-done((bf16[2,2,144,1152]{3,2,0,1:T(8,128)(2,1)}, bf16[2,2,144,1152]{3,2,0,1:T(8,128)(2,1)}, u32[]{:S(2)}, u32[]{:S(2)}) %collective-permute-start.49) | collective-permute-done | bytes 1327136 | tf_op jit(solution)/shard_map/ppermute | solution.py:52
  167.6 1.6 fusion.1
  170.3 1.7 collective-permute-start.47
  172.9 4.2 %copy.27 = bf16[1152,864]{1,0:T(8,128)(2,1)} copy(bf16[1152,864]{0,1:T(8,128)(2,1)} %convolution_convert_fusion.2) | data formatting | bytes 3981312 | tf_op jit(solution)/shard_map/convert_element_type | solution.py:805
  177.1 1.4 shard_map.197
  178.6 1.9 shard_map.198
  182.6 3.6 %collective-permute-done.31.piece_2 = bf16[368,128]{1,0:T(8,128)(2,1)S(1)} collective-permute-done((bf16[368,128]{1,0:T(8,128)(2,1)S(1)}, bf16[368,128]{1,0:T(8,128)(2,1)S(1)}, u32[]{:S(2)}, u32[]{:S(2)}) %collective-permute-start.31) | collective-permute-done | bytes 94240 | tf_op jit(solution)/shard_map/ppermute | solution.py:52
  195.3 3.0 %collective-permute-start.40 = (bf16[336,128]{1,0:T(8,128)(2,1)S(1)}, bf16[336,128]{1,0:T(8,128)(2,1)S(1)}, u32[]{:S(2)}, u32[]{:S(2)}) collective-permute-start(bf16[336,128]{1,0:T(8,128)(2,1)S(1)} %get-tuple-element.164), channel_id=1, source_target_pairs={{0,20},{4,16},{8,28},{12,24},{16,4},{20,0},{24,12},{28,8},{1,21},{... | collective-permute-start | bytes 258056 | tf_op jit(solution)/shard_map/ppermute | solution.py:52
  199.7 2.7 collective-permute-start.42
  202.4 6.8 %collective-permute-done.39.refs_4_ = bf16[336,128]{1,0:T(8,128)(2,1)S(1)} collective-permute-done((bf16[336,128]{1,0:T(8,128)(2,1)S(1)}, bf16[336,128]{1,0:T(8,128)(2,1)S(1)}, u32[]{:S(2)}, u32[]{:S(2)}) %collective-permute-start.39) | collective-permute-done | bytes 86048 | tf_op jit(solution)/shard_map/ppermute | solution.py:52
  209.2 2.5 convolution_multiply_fusion
  211.7 1.6 shard_map.200
  215.3 1.7 shard_map.201
  219.1 2.3 collective-permute-start.54
  221.4 9.7 %collective-permute-done.50 = bf16[2,144,1152]{2,1,0:T(8,128)(2,1)S(1)} collective-permute-done((bf16[2,144,1152]{2,1,0:T(8,128)(2,1)S(1)}, bf16[2,144,1152]{2,1,0:T(8,128)(2,1)S(1)}, u32[]{:S(2)}, u32[]{:S(2)}) %collective-permute-start.50) | collective-permute-done | bytes 663584 | tf_op jit(solution)/shard_map/ppermute | solution.py:52
  231.4 3.0 %collective-permute-start.51 = (bf16[144,1152]{1,0:T(8,128)(2,1)S(1)}, bf16[144,1152]{1,0:T(8,128)(2,1)S(1)}, u32[]{:S(2)}, u32[]{:S(2)}) collective-permute-start(bf16[144,1152]{1,0:T(8,128)(2,1)S(1)} %dynamic-slice_bitcast_fusion.6), channel_id=1, source_target_pairs={{0,16},{4,20},{8,24},{12,28},{16,0},{20,4},{24,8},{28,12},{1,17},{... | collective-permute-start | bytes 995336 | tf_op jit(solution)/shard_map/ppermute | solution.py:52
  234.3 17.0 %collective-permute-done.43 = bf16[2,2,144,864]{3,2,1,0:T(8,128)(2,1)S(1)} collective-permute-done((bf16[2,2,144,864]{3,2,1,0:T(8,128)(2,1)S(1)}, bf16[2,2,144,864]{3,2,1,0:T(8,128)(2,1)S(1)}, u32[]{:S(2)}, u32[]{:S(2)}) %collective-permute-start.43) | collective-permute-done | bytes 995360 | tf_op jit(solution)/shard_map/ppermute | solution.py:52
  253.4 10.2 %collective-permute-done.44 = bf16[2,144,864]{2,1,0:T(8,128)(2,1)S(1)} collective-permute-done((bf16[2,144,864]{2,1,0:T(8,128)(2,1)S(1)}, bf16[2,144,864]{2,1,0:T(8,128)(2,1)S(1)}, u32[]{:S(2)}, u32[]{:S(2)}) %collective-permute-start.44) | collective-permute-done | bytes 497696 | tf_op jit(solution)/shard_map/ppermute | solution.py:52
  263.8 3.1 %collective-permute-start.45 = (bf16[144,864]{1,0:T(8,128)(2,1)S(1)}, bf16[144,864]{1,0:T(8,128)(2,1)S(1)}, u32[]{:S(2)}, u32[]{:S(2)}) collective-permute-start(bf16[144,864]{1,0:T(8,128)(2,1)S(1)} %dynamic-slice_bitcast_fusion.7), channel_id=1, source_target_pairs={{0,16},{4,20},{8,24},{12,28},{16,0},{20,4},{24,8},{28,12},{1,17},{... | collective-permute-start | bytes 746504 | tf_op jit(solution)/shard_map/ppermute | solution.py:52
  267.8 7.9 %collective-permute-done.45 = bf16[144,864]{1,0:T(8,128)(2,1)S(1)} collective-permute-done((bf16[144,864]{1,0:T(8,128)(2,1)S(1)}, bf16[144,864]{1,0:T(8,128)(2,1)S(1)}, u32[]{:S(2)}, u32[]{:S(2)}) %collective-permute-start.45) | collective-permute-done | bytes 248864 | tf_op jit(solution)/shard_map/ppermute | solution.py:52
  276.6 1.8 reshape.209
  (239 shorter events, 60.1 us)
Async XLA Ops:
  0.6 72.9 %copy-start = (bf16[1152,1152]{1,0:T(8,128)(2,1)S(1)}, bf16[1152,1152]{1,0:T(8,128)(2,1)}, u32[]{:S(2)}) copy-start(bf16[1152,1152]{1,0:T(8,128)(2,1)} %param.22) | copy-start | bytes 7962628
  5.7 14.9 %copy-start.27 = (bf16[304,128]{1,0:T(8,128)(2,1)}, bf16[304,128]{1,0:T(8,128)(2,1)S(1)}, u32[]{:S(2)}) copy-start(bf16[304,128]{1,0:T(8,128)(2,1)S(1)} %get-tuple-element.93.refs_0_) | copy-start | bytes 233476
  5.7 15.5 %collective-permute-start = (bf16[304,128]{1,0:T(8,128)(2,1)S(1)}, bf16[304,128]{1,0:T(8,128)(2,1)S(1)}, u32[]{:S(2)}, u32[]{:S(2)}) collective-permute-start(bf16[304,128]{1,0:T(8,128)(2,1)S(1)} %get-tuple-element.94), channel_id=1, source_target_pairs={{0,4},{4,0},{8,12},{12,8},{16,20},{20,16},{24,28},{28,24},{1,5},{5... | collective-permute-start | bytes 233480 | tf_op jit(solution)/shard_map/ppermute | solution.py:52
  8.7 16.8 %collective-permute-start.1 = (bf16[304,128]{1,0:T(8,128)(2,1)S(1)}, bf16[304,128]{1,0:T(8,128)(2,1)S(1)}, u32[]{:S(2)}, u32[]{:S(2)}) collective-permute-start(bf16[304,128]{1,0:T(8,128)(2,1)S(1)} %get-tuple-element.95), channel_id=1, source_target_pairs={{0,8},{4,12},{8,0},{12,4},{16,24},{20,28},{24,16},{28,20},{1,9},{5... | collective-permute-start | bytes 233480 | tf_op jit(solution)/shard_map/ppermute | solution.py:52
  10.3 15.9 %collective-permute-start.2 = (bf16[304,128]{1,0:T(8,128)(2,1)}, bf16[304,128]{1,0:T(8,128)(2,1)}, u32[]{:S(2)}, u32[]{:S(2)}) collective-permute-start(bf16[304,128]{1,0:T(8,128)(2,1)} %get-tuple-element.96), channel_id=1, source_target_pairs={{0,12},{4,8},{8,4},{12,0},{16,28},{20,24},{24,20},{28,16},{1,13},{... | collective-permute-start | bytes 233480 | tf_op jit(solution)/shard_map/ppermute | solution.py:52
  10.3 15.9 %collective-permute-start.3 = (bf16[304,128]{1,0:T(8,128)(2,1)}, bf16[304,128]{1,0:T(8,128)(2,1)S(1)}, u32[]{:S(2)}, u32[]{:S(2)}) collective-permute-start(bf16[304,128]{1,0:T(8,128)(2,1)} %get-tuple-element.97), channel_id=1, source_target_pairs={{0,16},{4,20},{8,24},{12,28},{16,0},{20,4},{24,8},{28,12},{1,17},{... | collective-permute-start | bytes 233480 | tf_op jit(solution)/shard_map/ppermute | solution.py:52
  13.3 13.0 %collective-permute-start.4 = (bf16[304,128]{1,0:T(8,128)(2,1)}, bf16[304,128]{1,0:T(8,128)(2,1)S(1)}, u32[]{:S(2)}, u32[]{:S(2)}) collective-permute-start(bf16[304,128]{1,0:T(8,128)(2,1)} %get-tuple-element.98), channel_id=1, source_target_pairs={{0,20},{4,16},{8,28},{12,24},{16,4},{20,0},{24,12},{28,8},{1,21},{... | collective-permute-start | bytes 233480 | tf_op jit(solution)/shard_map/ppermute | solution.py:52
  21.9 6.5 %collective-permute-start.5 = (bf16[304,128]{1,0:T(8,128)(2,1)}, bf16[304,128]{1,0:T(8,128)(2,1)S(1)}, u32[]{:S(2)}, u32[]{:S(2)}) collective-permute-start(bf16[304,128]{1,0:T(8,128)(2,1)} %get-tuple-element.99), channel_id=1, source_target_pairs={{0,24},{4,28},{8,16},{12,20},{16,8},{20,12},{24,0},{28,4},{1,25},{... | collective-permute-start | bytes 233480 | tf_op jit(solution)/shard_map/ppermute | solution.py:52
  26.1 7.3 %collective-permute-start.6 = (bf16[304,128]{1,0:T(8,128)(2,1)}, bf16[304,128]{1,0:T(8,128)(2,1)S(1)}, u32[]{:S(2)}, u32[]{:S(2)}) collective-permute-start(bf16[304,128]{1,0:T(8,128)(2,1)} %get-tuple-element.100), channel_id=1, source_target_pairs={{0,28},{4,24},{8,20},{12,16},{16,12},{20,8},{24,4},{28,0},{1,29},{... | collective-permute-start | bytes 233480 | tf_op jit(solution)/shard_map/ppermute | solution.py:52
  26.1 29.1 %copy-start.7 = (bf16[288,1152]{1,0:T(8,128)(2,1)S(1)}, bf16[288,1152]{1,0:T(8,128)(2,1)}, u32[]{:S(2)}) copy-start(bf16[288,1152]{1,0:T(8,128)(2,1)} %output_ref.5) | copy-start | bytes 1990660
  26.1 15.1 %collective-permute-start.10 = (f32[4,6912]{1,0:T(4,128)}, f32[4,6912]{1,0:T(4,128)S(1)}, u32[]{:S(2)}, u32[]{:S(2)}) collective-permute-start(f32[4,6912]{1,0:T(4,128)} %fusion.49), channel_id=1, source_target_pairs={{0,1},{1,0},{2,3},{3,2},{4,5},{5,4},{6,7},{7,6},{8,9},{9,8},{10,11... | collective-permute-start | bytes 331784 | tf_op jit(solution)/shard_map/ppermute | solution.py:52
  26.2 27.1 %copy-start.20 = (bf16[304,128]{1,0:T(8,128)(2,1)}, bf16[304,128]{1,0:T(8,128)(2,1)S(1)}, u32[]{:S(2)}) copy-start(bf16[304,128]{1,0:T(8,128)(2,1)S(1)} %collective-permute-done.4.refs_5_) | copy-start | bytes 233476
  39.8 13.5 %collective-permute-start.8 = (bf16[288,512]{1,0:T(8,128)(2,1)}, bf16[288,512]{1,0:T(8,128)(2,1)}, u32[]{:S(2)}, u32[]{:S(2)}) collective-permute-start(bf16[288,512]{1,0:T(8,128)(2,1)} %get-tuple-element.102.piece_0), channel_id=1, source_target_pairs={{0,2},{1,3},{2,0},{3,1},{4,6},{5,7},{6,4},{7,5},{8,10},{9,11},{10,... | collective-permute-start | bytes 884744 | tf_op jit(solution)/shard_map/ppermute | solution.py:52
  42.2 6.2 %collective-permute-start.11 = (f32[4,6912]{1,0:T(4,128)S(1)}, f32[4,6912]{1,0:T(4,128)S(1)}, u32[]{:S(2)}, u32[]{:S(2)}) collective-permute-start(f32[4,6912]{1,0:T(4,128)S(1)} %add.220), channel_id=1, source_target_pairs={{0,2},{1,3},{2,0},{3,1},{4,6},{5,7},{6,4},{7,5},{8,10},{9,11},{10,... | collective-permute-start | bytes 331784 | tf_op jit(solution)/shard_map/ppermute | solution.py:52
  42.8 11.6 %collective-permute-start.7 = (bf16[288,512]{1,0:T(8,128)(2,1)}, bf16[288,512]{1,0:T(8,128)(2,1)}, u32[]{:S(2)}, u32[]{:S(2)}) collective-permute-start(bf16[288,512]{1,0:T(8,128)(2,1)} %get-tuple-element.102.piece_0), channel_id=1, source_target_pairs={{0,1},{1,0},{2,3},{3,2},{4,5},{5,4},{6,7},{7,6},{8,9},{9,8},{10,11... | collective-permute-start | bytes 884744 | tf_op jit(solution)/shard_map/ppermute | solution.py:52
  53.3 1.9 collective-permute-start.9
  64.6 13.1 %copy-start.15 = (bf16[136,1152]{1,0:T(8,128)(2,1)}, bf16[136,1152]{1,0:T(8,128)(2,1)S(1)}, u32[]{:S(2)}) copy-start(bf16[136,1152]{1,0:T(8,128)(2,1)S(1)} %get-tuple-element.111.spatial_ref) | copy-start | bytes 940036
  64.6 3.3 %collective-permute-start.12 = (bf16[136,1152]{1,0:T(8,128)(2,1)S(1)}, bf16[136,1152]{1,0:T(8,128)(2,1)S(1)}, u32[]{:S(2)}, u32[]{:S(2)}) collective-permute-start(bf16[136,1152]{1,0:T(8,128)(2,1)S(1)} %get-tuple-element.105), channel_id=1, source_target_pairs={{0,1},{1,0},{2,3},{3,2},{4,5},{5,4},{6,7},{7,6},{8,9},{9,8},{10,11... | collective-permute-start | bytes 940040 | tf_op jit(solution)/shard_map/ppermute | solution.py:52
  67.9 9.8 %collective-permute-start.14 = (bf16[136,1152]{1,0:T(8,128)(2,1)S(1)}, bf16[136,1152]{1,0:T(8,128)(2,1)S(1)}, u32[]{:S(2)}, u32[]{:S(2)}) collective-permute-start(bf16[136,1152]{1,0:T(8,128)(2,1)S(1)} %add_convert_fusion.3), channel_id=1, source_target_pairs={{0,2},{1,3},{2,0},{3,1},{4,6},{5,7},{6,4},{7,5},{8,10},{9,11},{10,... | collective-permute-start | bytes 940040 | tf_op jit(solution)/shard_map/ppermute | solution.py:52
  73.4 4.3 %collective-permute-start.13 = (bf16[136,1152]{1,0:T(8,128)(2,1)S(1)}, bf16[136,1152]{1,0:T(8,128)(2,1)S(1)}, u32[]{:S(2)}, u32[]{:S(2)}) collective-permute-start(bf16[136,1152]{1,0:T(8,128)(2,1)S(1)} %get-tuple-element.108), channel_id=1, source_target_pairs={{0,1},{1,0},{2,3},{3,2},{4,5},{5,4},{6,7},{7,6},{8,9},{9,8},{10,11... | collective-permute-start | bytes 940040 | tf_op jit(solution)/shard_map/ppermute | solution.py:52
  78.1 26.4 %copy-start.13 = (f32[136,1152]{1,0:T(8,128)}, f32[136,1152]{1,0:T(8,128)S(1)}, u32[]{:S(2)}) copy-start(f32[136,1152]{1,0:T(8,128)S(1)} %get-tuple-element.127.middle_ref) | copy-start | bytes 1880068
  78.1 8.9 %collective-permute-start.16 = (bf16[136,1152]{1,0:T(8,128)(2,1)S(1)}, bf16[136,1152]{1,0:T(8,128)(2,1)S(1)}, u32[]{:S(2)}, u32[]{:S(2)}) collective-permute-start(bf16[136,1152]{1,0:T(8,128)(2,1)S(1)} %get-tuple-element.112.piece_0), channel_id=1, source_target_pairs={{0,2},{1,3},{2,0},{3,1},{4,6},{5,7},{6,4},{7,5},{8,10},{9,11},{10,... | collective-permute-start | bytes 940040 | tf_op jit(solution)/shard_map/ppermute | solution.py:52
  79.7 1.6 collective-permute-start.15
  87.0 2.5 collective-permute-start.17
  92.0 2.6 collective-permute-start.18
  94.5 10.0 %collective-permute-start.19 = (bf16[136,1152]{1,0:T(8,128)(2,1)S(1)}, bf16[136,1152]{1,0:T(8,128)(2,1)S(1)}, u32[]{:S(2)}, u32[]{:S(2)}) collective-permute-start(bf16[136,1152]{1,0:T(8,128)(2,1)S(1)} %get-tuple-element.120), channel_id=1, source_target_pairs={{0,1},{1,0},{2,3},{3,2},{4,5},{5,4},{6,7},{7,6},{8,9},{9,8},{10,11... | collective-permute-start | bytes 940040 | tf_op jit(solution)/shard_map/ppermute | solution.py:52
  94.7 9.9 %collective-permute-start.20 = (bf16[136,1152]{1,0:T(8,128)(2,1)S(1)}, bf16[136,1152]{1,0:T(8,128)(2,1)S(1)}, u32[]{:S(2)}, u32[]{:S(2)}) collective-permute-start(bf16[136,1152]{1,0:T(8,128)(2,1)S(1)} %add_convert_fusion.2), channel_id=1, source_target_pairs={{0,2},{1,3},{2,0},{3,1},{4,6},{5,7},{6,4},{7,5},{8,10},{9,11},{10,... | collective-permute-start | bytes 940040 | tf_op jit(solution)/shard_map/ppermute | solution.py:52
  105.9 9.7 %collective-permute-start.23 = (bf16[136,1152]{1,0:T(8,128)(2,1)}, bf16[136,1152]{1,0:T(8,128)(2,1)}, u32[]{:S(2)}, u32[]{:S(2)}) collective-permute-start(bf16[136,1152]{1,0:T(8,128)(2,1)} %get-tuple-element.129.piece_0), channel_id=1, source_target_pairs={{0,2},{1,3},{2,0},{3,1},{4,6},{5,7},{6,4},{7,5},{8,10},{9,11},{10,... | collective-permute-start | bytes 940040 | tf_op jit(solution)/shard_map/ppermute | solution.py:52
  110.3 5.3 %collective-permute-start.22 = (bf16[136,1152]{1,0:T(8,128)(2,1)S(1)}, bf16[136,1152]{1,0:T(8,128)(2,1)S(1)}, u32[]{:S(2)}, u32[]{:S(2)}) collective-permute-start(bf16[136,1152]{1,0:T(8,128)(2,1)S(1)} %get-tuple-element.192), channel_id=1, source_target_pairs={{0,1},{1,0},{2,3},{3,2},{4,5},{5,4},{6,7},{7,6},{8,9},{9,8},{10,11... | collective-permute-start | bytes 940040 | tf_op jit(solution)/shard_map/ppermute | solution.py:52
  113.7 9.8 %collective-permute-start.26 = (bf16[136,1152]{1,0:T(8,128)(2,1)}, bf16[136,1152]{1,0:T(8,128)(2,1)S(1)}, u32[]{:S(2)}, u32[]{:S(2)}) collective-permute-start(bf16[136,1152]{1,0:T(8,128)(2,1)} %get-tuple-element.129.piece_0), channel_id=1, source_target_pairs={{0,1},{1,0},{2,3},{3,2},{4,5},{5,4},{6,7},{7,6},{8,9},{9,8},{10,11... | collective-permute-start | bytes 940040 | tf_op jit(solution)/shard_map/ppermute | solution.py:52
  115.6 1.8 collective-permute-start.24
  117.4 15.4 %collective-permute-start.25 = (bf16[136,1152]{1,0:T(8,128)(2,1)S(1)}, bf16[136,1152]{1,0:T(8,128)(2,1)S(1)}, u32[]{:S(2)}, u32[]{:S(2)}) collective-permute-start(bf16[136,1152]{1,0:T(8,128)(2,1)S(1)} %add_convert_fusion.1), channel_id=1, source_target_pairs={{0,2},{1,3},{2,0},{3,1},{4,6},{5,7},{6,4},{7,5},{8,10},{9,11},{10,... | collective-permute-start | bytes 940040 | tf_op jit(solution)/shard_map/ppermute | solution.py:52
  123.1 31.2 %collective-permute-start.52 = (bf16[2,2,144,1152]{3,2,0,1:T(8,128)(2,1)}, bf16[2,2,144,1152]{3,2,0,1:T(8,128)(2,1)}, u32[]{:S(2)}, u32[]{:S(2)}) collective-permute-start(bf16[2,2,144,1152]{3,2,0,1:T(8,128)(2,1)} %bitcast.138), channel_id=1, source_target_pairs={{0,4},{4,0},{8,12},{12,8},{16,20},{20,16},{24,28},{28,24},{1,5},{5... | collective-permute-start | bytes 3981320 | tf_op jit(solution)/shard_map/ppermute | solution.py:52
  132.8 3.1 %collective-permute-start.27 = (bf16[136,1152]{1,0:T(8,128)(2,1)S(1)}, bf16[136,1152]{1,0:T(8,128)(2,1)S(1)}, u32[]{:S(2)}, u32[]{:S(2)}) collective-permute-start(bf16[136,1152]{1,0:T(8,128)(2,1)S(1)} %get-tuple-element.137), channel_id=1, source_target_pairs={{0,1},{1,0},{2,3},{3,2},{4,5},{5,4},{6,7},{7,6},{8,9},{9,8},{10,11... | collective-permute-start | bytes 940040 | tf_op jit(solution)/shard_map/ppermute | solution.py:52
  135.5 31.8 %collective-permute-start.49 = (bf16[2,2,144,1152]{3,2,0,1:T(8,128)(2,1)}, bf16[2,2,144,1152]{3,2,0,1:T(8,128)(2,1)}, u32[]{:S(2)}, u32[]{:S(2)}) collective-permute-start(bf16[2,2,144,1152]{3,2,0,1:T(8,128)(2,1)} %bitcast.139), channel_id=1, source_target_pairs={{0,8},{4,12},{8,0},{12,4},{16,24},{20,28},{24,16},{28,20},{1,9},{5... | collective-permute-start | bytes 3981320 | tf_op jit(solution)/shard_map/ppermute | solution.py:52
  135.5 41.6 %collective-permute-start.21 = (bf16[136,1152]{1,0:T(8,128)(2,1)}, bf16[136,1152]{1,0:T(8,128)(2,1)}, u32[]{:S(2)}, u32[]{:S(2)}) collective-permute-start(bf16[136,1152]{1,0:T(8,128)(2,1)} %get-tuple-element.193), channel_id=1, source_target_pairs={{0,1},{1,0},{2,3},{3,2},{4,5},{5,4},{6,7},{7,6},{8,9},{9,8},{10,11... | collective-permute-start | bytes 940040 | tf_op jit(solution)/shard_map/ppermute | solution.py:52
  136.8 41.8 %collective-permute-start.29 = (bf16[136,1152]{1,0:T(8,128)(2,1)}, bf16[136,1152]{1,0:T(8,128)(2,1)S(1)}, u32[]{:S(2)}, u32[]{:S(2)}) collective-permute-start(bf16[136,1152]{1,0:T(8,128)(2,1)} %add_convert_fusion), channel_id=1, source_target_pairs={{0,2},{1,3},{2,0},{3,1},{4,6},{5,7},{6,4},{7,5},{8,10},{9,11},{10,... | collective-permute-start | bytes 940040 | tf_op jit(solution)/shard_map/ppermute | solution.py:52
  139.3 39.3 %collective-permute-start.28 = (bf16[136,1152]{1,0:T(8,128)(2,1)}, bf16[136,1152]{1,0:T(8,128)(2,1)}, u32[]{:S(2)}, u32[]{:S(2)}) collective-permute-start(bf16[136,1152]{1,0:T(8,128)(2,1)} %get-tuple-element.139), channel_id=1, source_target_pairs={{0,1},{1,0},{2,3},{3,2},{4,5},{5,4},{6,7},{7,6},{8,9},{9,8},{10,11... | collective-permute-start | bytes 940040 | tf_op jit(solution)/shard_map/ppermute | solution.py:52
  154.3 14.9 %collective-permute-start.46 = (bf16[2,2,144,288]{3,2,1,0:T(8,128)(2,1)S(1)}, bf16[2,2,144,288]{3,2,1,0:T(8,128)(2,1)S(1)}, u32[]{:S(2)}, u32[]{:S(2)}) collective-permute-start(bf16[2,2,144,288]{3,2,1,0:T(8,128)(2,1)S(1)} %dynamic-slice_bitcast_fusion.4), channel_id=1, source_target_pairs={{0,4},{4,0},{8,12},{12,8},{16,20},{20,16},{24,28},{28,24},{1,5},{5... | collective-permute-start | bytes 995336 | tf_op jit(solution)/shard_map/ppermute | solution.py:52
  167.3 50.5 %collective-permute-start.53 = (bf16[2,144,1152]{2,1,0:T(8,128)(2,1)}, bf16[2,144,1152]{2,1,0:T(8,128)(2,1)}, u32[]{:S(2)}, u32[]{:S(2)}) collective-permute-start(bf16[2,144,1152]{2,1,0:T(8,128)(2,1)} %dynamic-slice_bitcast_fusion.1), channel_id=1, source_target_pairs={{0,8},{4,12},{8,0},{12,4},{16,24},{20,28},{24,16},{28,20},{1,9},{5... | collective-permute-start | bytes 1990664 | tf_op jit(solution)/shard_map/ppermute | solution.py:52
  170.3 19.8 %collective-permute-start.47 = (bf16[2,144,288]{2,1,0:T(8,128)(2,1)}, bf16[2,144,288]{2,1,0:T(8,128)(2,1)}, u32[]{:S(2)}, u32[]{:S(2)}) collective-permute-start(bf16[2,144,288]{2,1,0:T(8,128)(2,1)} %dynamic-slice_bitcast_fusion.8), channel_id=1, source_target_pairs={{0,8},{4,12},{8,0},{12,4},{16,24},{20,28},{24,16},{28,20},{1,9},{5... | collective-permute-start | bytes 497672 | tf_op jit(solution)/shard_map/ppermute | solution.py:52
  178.6 12.7 %copy-start.47 = (bf16[2,2,144,288]{3,2,1,0:T(8,128)(2,1)S(1)}, bf16[2,2,144,288]{3,2,1,0:T(8,128)(2,1)}, u32[]{:S(2)}) copy-start(bf16[2,2,144,288]{3,2,1,0:T(8,128)(2,1)} %copy-done.46) | copy-start | bytes 995332
  178.6 30.6 %copy-start.37 = (bf16[288,6912]{1,0:T(8,128)(2,1)S(1)}, bf16[288,6912]{1,0:T(8,128)(2,1)}, u32[]{:S(2)}) copy-start(bf16[288,6912]{1,0:T(8,128)(2,1)} %param.18) | copy-start | bytes 11943940
  180.5 2.0 collective-permute-start.30
  180.6 5.6 %collective-permute-start.31 = (bf16[368,128]{1,0:T(8,128)(2,1)S(1)}, bf16[368,128]{1,0:T(8,128)(2,1)S(1)}, u32[]{:S(2)}, u32[]{:S(2)}) collective-permute-start(bf16[368,128]{1,0:T(8,128)(2,1)S(1)} %get-tuple-element.151), channel_id=1, source_target_pairs={{0,2},{1,3},{2,0},{3,1},{4,6},{5,7},{6,4},{7,5},{8,10},{9,11},{10,... | collective-permute-start | bytes 282632 | tf_op jit(solution)/shard_map/ppermute | solution.py:52
  181.5 5.7 %collective-permute-start.32 = (bf16[368,128]{1,0:T(8,128)(2,1)S(1)}, bf16[368,128]{1,0:T(8,128)(2,1)S(1)}, u32[]{:S(2)}, u32[]{:S(2)}) collective-permute-start(bf16[368,128]{1,0:T(8,128)(2,1)S(1)} %get-tuple-element.152), channel_id=1, source_target_pairs={{0,3},{1,2},{2,1},{3,0},{4,7},{5,6},{6,5},{7,4},{8,11},{9,10},{10,... | collective-permute-start | bytes 282632 | tf_op jit(solution)/shard_map/ppermute | solution.py:52
  187.9 4.4 %collective-permute-start.33 = (bf16[304,128]{1,0:T(8,128)(2,1)S(1)}, bf16[304,128]{1,0:T(8,128)(2,1)S(1)}, u32[]{:S(2)}, u32[]{:S(2)}) collective-permute-start(bf16[304,128]{1,0:T(8,128)(2,1)S(1)} %get-tuple-element.154), channel_id=1, source_target_pairs={{0,1},{1,0},{2,3},{3,2},{4,5},{5,4},{6,7},{7,6},{8,9},{9,8},{10,11... | collective-permute-start | bytes 233480 | tf_op jit(solution)/shard_map/ppermute | solution.py:52
  188.6 4.9 %collective-permute-start.34 = (bf16[304,128]{1,0:T(8,128)(2,1)S(1)}, bf16[304,128]{1,0:T(8,128)(2,1)S(1)}, u32[]{:S(2)}, u32[]{:S(2)}) collective-permute-start(bf16[304,128]{1,0:T(8,128)(2,1)S(1)} %get-tuple-element.156), channel_id=1, source_target_pairs={{0,2},{1,3},{2,0},{3,1},{4,6},{5,7},{6,4},{7,5},{8,10},{9,11},{10,... | collective-permute-start | bytes 233480 | tf_op jit(solution)/shard_map/ppermute | solution.py:52
  189.5 5.1 %collective-permute-start.35 = (bf16[304,128]{1,0:T(8,128)(2,1)S(1)}, bf16[304,128]{1,0:T(8,128)(2,1)S(1)}, u32[]{:S(2)}, u32[]{:S(2)}) collective-permute-start(bf16[304,128]{1,0:T(8,128)(2,1)S(1)} %get-tuple-element.158), channel_id=1, source_target_pairs={{0,3},{1,2},{2,1},{3,0},{4,7},{5,6},{6,5},{7,4},{8,11},{9,10},{10,... | collective-permute-start | bytes 233480 | tf_op jit(solution)/shard_map/ppermute | solution.py:52
  190.1 5.2 %collective-permute-start.36 = (bf16[336,128]{1,0:T(8,128)(2,1)S(1)}, bf16[336,128]{1,0:T(8,128)(2,1)S(1)}, u32[]{:S(2)}, u32[]{:S(2)}) collective-permute-start(bf16[336,128]{1,0:T(8,128)(2,1)S(1)} %get-tuple-element.160), channel_id=1, source_target_pairs={{0,4},{4,0},{8,12},{12,8},{16,20},{20,16},{24,28},{28,24},{1,5},{5... | collective-permute-start | bytes 258056 | tf_op jit(solution)/shard_map/ppermute | solution.py:52
  192.3 6.0 %collective-permute-start.37 = (bf16[336,128]{1,0:T(8,128)(2,1)S(1)}, bf16[336,128]{1,0:T(8,128)(2,1)S(1)}, u32[]{:S(2)}, u32[]{:S(2)}) collective-permute-start(bf16[336,128]{1,0:T(8,128)(2,1)S(1)} %get-tuple-element.161), channel_id=1, source_target_pairs={{0,8},{4,12},{8,0},{12,4},{16,24},{20,28},{24,16},{28,20},{1,9},{5... | collective-permute-start | bytes 258056 | tf_op jit(solution)/shard_map/ppermute | solution.py:52
  193.5 6.2 %collective-permute-start.38 = (bf16[336,128]{1,0:T(8,128)(2,1)S(1)}, bf16[336,128]{1,0:T(8,128)(2,1)S(1)}, u32[]{:S(2)}, u32[]{:S(2)}) collective-permute-start(bf16[336,128]{1,0:T(8,128)(2,1)S(1)} %get-tuple-element.162), channel_id=1, source_target_pairs={{0,12},{4,8},{8,4},{12,0},{16,28},{20,24},{24,20},{28,16},{1,13},{... | collective-permute-start | bytes 258056 | tf_op jit(solution)/shard_map/ppermute | solution.py:52
  194.6 14.5 %collective-permute-start.39 = (bf16[336,128]{1,0:T(8,128)(2,1)S(1)}, bf16[336,128]{1,0:T(8,128)(2,1)S(1)}, u32[]{:S(2)}, u32[]{:S(2)}) collective-permute-start(bf16[336,128]{1,0:T(8,128)(2,1)S(1)} %get-tuple-element.163), channel_id=1, source_target_pairs={{0,16},{4,20},{8,24},{12,28},{16,0},{20,4},{24,8},{28,12},{1,17},{... | collective-permute-start | bytes 258056 | tf_op jit(solution)/shard_map/ppermute | solution.py:52
  195.3 18.0 %collective-permute-start.40 = (bf16[336,128]{1,0:T(8,128)(2,1)S(1)}, bf16[336,128]{1,0:T(8,128)(2,1)S(1)}, u32[]{:S(2)}, u32[]{:S(2)}) collective-permute-start(bf16[336,128]{1,0:T(8,128)(2,1)S(1)} %get-tuple-element.164), channel_id=1, source_target_pairs={{0,20},{4,16},{8,28},{12,24},{16,4},{20,0},{24,12},{28,8},{1,21},{... | collective-permute-start | bytes 258056 | tf_op jit(solution)/shard_map/ppermute | solution.py:52
  198.3 16.0 %collective-permute-start.41 = (bf16[336,128]{1,0:T(8,128)(2,1)S(1)}, bf16[336,128]{1,0:T(8,128)(2,1)S(1)}, u32[]{:S(2)}, u32[]{:S(2)}) collective-permute-start(bf16[336,128]{1,0:T(8,128)(2,1)S(1)} %get-tuple-element.165), channel_id=1, source_target_pairs={{0,24},{4,28},{8,16},{12,20},{16,8},{20,12},{24,0},{28,4},{1,25},{... | collective-permute-start | bytes 258056 | tf_op jit(solution)/shard_map/ppermute | solution.py:52
  199.7 15.6 %collective-permute-start.42 = (bf16[336,128]{1,0:T(8,128)(2,1)S(1)}, bf16[336,128]{1,0:T(8,128)(2,1)S(1)}, u32[]{:S(2)}, u32[]{:S(2)}) collective-permute-start(bf16[336,128]{1,0:T(8,128)(2,1)S(1)} %get-tuple-element.166), channel_id=1, source_target_pairs={{0,28},{4,24},{8,20},{12,16},{16,12},{20,8},{24,4},{28,0},{1,29},{... | collective-permute-start | bytes 258056 | tf_op jit(solution)/shard_map/ppermute | solution.py:52
  209.2 8.6 %collective-permute-start.48 = (bf16[144,288]{1,0:T(8,128)(2,1)S(1)}, bf16[144,288]{1,0:T(8,128)(2,1)S(1)}, u32[]{:S(2)}, u32[]{:S(2)}) collective-permute-start(bf16[144,288]{1,0:T(8,128)(2,1)S(1)} %dynamic-slice_bitcast_fusion.9), channel_id=1, source_target_pairs={{0,16},{4,20},{8,24},{12,28},{16,0},{20,4},{24,8},{28,12},{1,17},{... | collective-permute-start | bytes 248840 | tf_op jit(solution)/shard_map/ppermute | solution.py:52
  213.3 17.9 %collective-permute-start.50 = (bf16[2,144,1152]{2,1,0:T(8,128)(2,1)S(1)}, bf16[2,144,1152]{2,1,0:T(8,128)(2,1)S(1)}, u32[]{:S(2)}, u32[]{:S(2)}) collective-permute-start(bf16[2,144,1152]{2,1,0:T(8,128)(2,1)S(1)} %copy-done.49), channel_id=1, source_target_pairs={{0,4},{4,0},{8,12},{12,8},{16,20},{20,16},{24,28},{28,24},{1,5},{5... | collective-permute-start | bytes 1990664 | tf_op jit(solution)/shard_map/ppermute | solution.py:52
  214.3 37.1 %collective-permute-start.43 = (bf16[2,2,144,864]{3,2,1,0:T(8,128)(2,1)S(1)}, bf16[2,2,144,864]{3,2,1,0:T(8,128)(2,1)S(1)}, u32[]{:S(2)}, u32[]{:S(2)}) collective-permute-start(bf16[2,2,144,864]{3,2,1,0:T(8,128)(2,1)S(1)} %dynamic-slice_bitcast_fusion), channel_id=1, source_target_pairs={{0,4},{4,0},{8,12},{12,8},{16,20},{20,16},{24,28},{28,24},{1,5},{5... | collective-permute-start | bytes 2985992 | tf_op jit(solution)/shard_map/ppermute | solution.py:52
  217.0 14.1 %copy-start.42 = (bf16[2,2,144,1152]{3,2,0,1:T(8,128)(2,1)S(1)}, bf16[2,2,144,1152]{3,2,0,1:T(8,128)(2,1)}, u32[]{:S(2)}) copy-start(bf16[2,2,144,1152]{3,2,0,1:T(8,128)(2,1)} %copy-done.41) | copy-start | bytes 3981316
  219.1 33.4 %collective-permute-start.54 = (bf16[144,1152]{1,0:T(8,128)(2,1)S(1)}, bf16[144,1152]{1,0:T(8,128)(2,1)S(1)}, u32[]{:S(2)}, u32[]{:S(2)}) collective-permute-start(bf16[144,1152]{1,0:T(8,128)(2,1)S(1)} %dynamic-slice_bitcast_fusion.5), channel_id=1, source_target_pairs={{0,16},{4,20},{8,24},{12,28},{16,0},{20,4},{24,8},{28,12},{1,17},{... | collective-permute-start | bytes 995336 | tf_op jit(solution)/shard_map/ppermute | solution.py:52
  231.4 21.1 %collective-permute-start.51 = (bf16[144,1152]{1,0:T(8,128)(2,1)S(1)}, bf16[144,1152]{1,0:T(8,128)(2,1)S(1)}, u32[]{:S(2)}, u32[]{:S(2)}) collective-permute-start(bf16[144,1152]{1,0:T(8,128)(2,1)S(1)} %dynamic-slice_bitcast_fusion.6), channel_id=1, source_target_pairs={{0,16},{4,20},{8,24},{12,28},{16,0},{20,4},{24,8},{28,12},{1,17},{... | collective-permute-start | bytes 995336 | tf_op jit(solution)/shard_map/ppermute | solution.py:52
  251.7 11.9 %collective-permute-start.44 = (bf16[2,144,864]{2,1,0:T(8,128)(2,1)S(1)}, bf16[2,144,864]{2,1,0:T(8,128)(2,1)S(1)}, u32[]{:S(2)}, u32[]{:S(2)}) collective-permute-start(bf16[2,144,864]{2,1,0:T(8,128)(2,1)S(1)} %dynamic-slice_bitcast_fusion.3), channel_id=1, source_target_pairs={{0,8},{4,12},{8,0},{12,4},{16,24},{20,28},{24,16},{28,20},{1,9},{5... | collective-permute-start | bytes 1493000 | tf_op jit(solution)/shard_map/ppermute | solution.py:52
  263.8 11.9 %collective-permute-start.45 = (bf16[144,864]{1,0:T(8,128)(2,1)S(1)}, bf16[144,864]{1,0:T(8,128)(2,1)S(1)}, u32[]{:S(2)}, u32[]{:S(2)}) collective-permute-start(bf16[144,864]{1,0:T(8,128)(2,1)S(1)} %dynamic-slice_bitcast_fusion.7), channel_id=1, source_target_pairs={{0,16},{4,20},{8,24},{12,28},{16,0},{20,4},{24,8},{28,12},{1,17},{... | collective-permute-start | bytes 746504 | tf_op jit(solution)/shard_map/ppermute | solution.py:52
  (42 other events, 157.5 us)
